TPU v7x, 512 devices: a whole 4x4x16 slice. The times are simulated.
512 devices in a mesh: lev: 8 (over x, core), tile: 64 (over z, y).
Axes of the slice: x: 4, y: 4, z: 16, core: 2. Of those that a mesh axis runs over, the one named last changes fastest.
Arguments:
- lam_in: float32 [4, 48, 1024, 1024], P(None, 'lev', 'tile'), may hold values from -6 to 6
- courant_x: float32 [48, 1024, 1024], P('lev', 'tile'), may hold values from -0.15 to 0.15
- courant_y: float32 [48, 1024, 1024], P('lev', 'tile'), may hold values from -0.15 to 0.15
- kz_face: float32 [48, 1024, 1024], P('lev', 'tile'), may hold values from 0.02 to 0.15
- loss_rate: float32 [4, 48], P(None, 'lev'), may hold values from 0.05 to 1
- profile: float32 [4, 48], P(None, 'lev'), may hold values from 0.1 to 1
- kernel: float32 [48], P('lev'), may hold values from 0.3 to 1.5
- obs_values: bfloat16 [524288, 128], P(('lev', 'tile')), may hold values from -0.75 to 0.75
- obs_tile: int32 [524288, 1], P(('lev', 'tile')), may hold values from 0 to 63, as said below
- obs_block: int32 [524288], P(('lev', 'tile')), may hold values from 0 to 127
Outputs:
- lam_out: float32 [4, 48, 1024, 1024], P(None, 'lev', 'tile')
- emis_grad: float32 [4, 1024, 1024], P(None, 'tile', 'lev')
Inputs may be any that keep to these rules, and one draw needn't show every extreme that they name: `obs_tile`: of the 1024 rows of one device (aligned blocks of 1024 rows), at most 64 name any one tile, and one tile is named exactly 64 times in every block.
All inputs are finite; a program needn't handle non-finite values.
Results may differ from a plain program's by a relative error of at most 0.0015.
Values may be sent and summed in bfloat16 or wider, within the bound.
No kernel may reach another device: no remote copies, remote signals or barrier semaphores. Data moves between devices by JAX's collectives and lax.ppermute only.
A program may use at most 64 MiB of HBM per device.

v0:
```python
import jax
import jax.numpy as jnp
from jax import lax
from jax.sharding import PartitionSpec as P

STEPS = 2


def shifted(value, axis, steps):
    count = lax.axis_size(axis)
    leading, last = (max(0, -steps), min(count, count - steps))
    return lax.ppermute(value, axis, [(source, source + steps) for source in range(leading, last)])


def shortened(x):

    def short(part):
        return part.astype(jnp.bfloat16) if part.dtype == jnp.float32 else part

    return jax.tree.map(short, x)


def padded(block, sides, width):
    for axis, dim in sides:
        count = lax.axis_size(axis)
        forward = [(i, i + 1) for i in range(count - 1)]
        backward = [(target, source) for source, target in forward]
        low = lax.ppermute(
            lax.slice_in_dim(block, block.shape[dim] - width, None, axis=dim), axis, forward
        )
        high = lax.ppermute(lax.slice_in_dim(block, 0, width, axis=dim), axis, backward)
        block = jnp.concatenate([low, block, high], axis=dim)
    return block


def on_device(
    lam_in,
    courant_x,
    courant_y,
    kz_face,
    loss_rate,
    profile,
    kernel,
    obs_values,
    obs_tile,
    obs_block,
):
    tile_count = lax.axis_size("tile")
    level_count = lax.axis_size("lev")
    tile_index = lax.axis_index("tile")
    level_index = lax.axis_index("lev")
    tracers, levels, tile_rows, tile_cols = lam_in.shape
    pixels = obs_values.shape[1]
    blocks = tile_rows * tile_cols // pixels
    east_edge = (tile_index == tile_count - 1) & (jnp.arange(tile_rows) == tile_rows - 1)
    courant_east = jnp.where(east_edge[None, :, None], 0.0, courant_x)
    north_edge = jnp.arange(tile_cols) == tile_cols - 1
    courant_north = jnp.where(north_edge[None, None, :], 0.0, courant_y)
    top_level = (level_index == level_count - 1) & (jnp.arange(levels) == levels - 1)
    kz_masked = jnp.where(top_level[:, None, None], 0.0, kz_face)
    flat_index = obs_tile[:, 0] * blocks + obs_block
    selector = (jnp.arange(blocks * lax.axis_size("tile"))[:, None] == flat_index[None, :]).astype(
        obs_values.dtype
    )
    partial_map = lax.psum_scatter(
        jnp.dot(selector, obs_values, preferred_element_type=jnp.float32),
        "tile",
        scatter_dimension=0,
        tiled=True,
    )
    pixel_map = lax.psum(partial_map, "lev")
    field_map = pixel_map.reshape(tile_rows, tile_cols)
    adjoint = lam_in + kernel[None, :, None, None] * field_map[None, None]
    weights = profile[:, :, None, None]
    surface = jnp.zeros((tracers, tile_rows, tile_cols), jnp.float32)
    courant_rim = shifted(courant_east[:, tile_rows - 1 :, :], "tile", 1)
    courant_west = jnp.concatenate([courant_rim, courant_east[:, :-1]], axis=1)
    courant_south = jnp.pad(courant_north[:, :, :-1], ((0, 0), (0, 0), (1, 0)))
    kz_rim = shifted(kz_masked[levels - 1 :].astype(jnp.bfloat16), "lev", 1).astype(jnp.float32)
    kz_below = jnp.concatenate([kz_rim, kz_masked[:-1]], axis=0)
    decay_factor = jnp.exp(-loss_rate)[:, :, None, None]
    east_gain = jnp.maximum(courant_east, 0.0)
    west_gain = jnp.minimum(courant_west, 0.0)
    north_gain = jnp.maximum(courant_north, 0.0)
    south_gain = jnp.minimum(courant_south, 0.0)
    for step_index in range(STEPS):
        surface = surface + jnp.sum(weights * adjoint, axis=1)
        scaled = decay_factor * adjoint
        level_ext = padded(shortened(scaled), (("lev", 1),), 1).astype(scaled.dtype)
        mixed = (
            scaled
            + kz_masked * (level_ext[:, 2:] - scaled)
            - kz_below * (scaled - level_ext[:, :-2])
        )
        row_ext = padded(shortened(mixed), (("tile", 2),), 1).astype(mixed.dtype)
        col_pad = jnp.pad(mixed, ((0, 0), (0, 0), (0, 0), (1, 1)))
        result = mixed + east_gain * (row_ext[:, :, 2:] - mixed)
        result = result + west_gain * (mixed - row_ext[:, :, :-2])
        result = result + north_gain * (col_pad[:, :, :, 2:] - mixed)
        result = result + south_gain * (mixed - col_pad[:, :, :, :-2])
        adjoint = result
    gradient = lax.psum_scatter(surface, "lev", scatter_dimension=2, tiled=True)
    return (adjoint, gradient)


def solution(mesh):
    in_specs = (
        P(None, "lev", "tile", None),
        P("lev", "tile", None),
        P("lev", "tile", None),
        P("lev", "tile", None),
        P(None, "lev"),
        P(None, "lev"),
        P("lev"),
        P(("lev", "tile"), None),
        P(("lev", "tile"), None),
        P(("lev", "tile")),
    )
    out_specs = (P(None, "lev", "tile", None), P(None, "tile", "lev"))
    return jax.shard_map(
        on_device, mesh=mesh, in_specs=in_specs, out_specs=out_specs, check_vma=False
    )
```

profile of v0, /device:TPU:24, one launch (start us, length us, event | category | flops | bytes accessed | tf_op | source)
XLA Modules:
  0.0 880.0 jit_solution(14432524898852602617)
XLA Ops:
  8.6 7.1 fusion
  15.8 0.9 copy-done.11
  16.9 1.9 collective-permute-start.2
  19.0 3.5 collective-permute-start.5
  22.5 2.0 broadcast_maximum_fusion
  24.4 695.0 %reduce-scatter.3.cloned.1.call-done = f32[128,128]{1,0:T(8,128)} async-done(((f32[8192,128]{1,0:T(8,128)}), f32[128,128]{1,0:T(8,128)}) %reduce-scatter.3.cloned.1.call-update) | async-done | bytes 65552 | tf_op jit(solution)/shard_map/reduce_scatter | solution.py:65
  719.5 1.5 mul.146
  721.0 73.1 %all-reduce.5.cloned.1.call-done = f32[16,1024]{1,0:T(8,128)} async-done(((f32[16,1024]{1,0:T(8,128)}), f32[16,1024]{1,0:T(8,128)}) %all-reduce.5.cloned.1.call-update) | async-done | bytes 65552 | tf_op jit(solution)/shard_map/psum | solution.py:71
  794.1 0.9 broadcast_multiply_fusion
  795.3 1.3 collective-permute-start
  796.7 1.3 collective-permute-start.1
  798.2 1.7 collective-permute-done.1
  800.9 3.4 collective-permute-start.3
  804.3 2.4 collective-permute-start.4
  807.4 5.5 collective-permute-done.4
  813.4 1.6 multiply_reduce_fusion
  815.2 3.6 collective-permute-start.6
  818.8 1.3 collective-permute-start.7
  820.2 2.7 collective-permute-done.7
  824.0 1.9 collective-permute-start.8
  825.9 3.9 collective-permute-start.9
  830.6 3.9 collective-permute-done.9
  835.1 2.5 fusion.11
  837.5 35.9 %reduce-scatter.5.cloned.1.call-done = f32[4,16,128]{2,1,0:T(8,128)} async-done(((f32[4,16,1024]{2,1,0:T(8,128)}), f32[4,16,128]{2,1,0:T(8,128)}) %reduce-scatter.5.cloned.1.call-update) | async-done | bytes 32784 | tf_op jit(solution)/shard_map/reduce_scatter | solution.py:102
  (71 shorter events, 7.0 us)
Async XLA Ops:
  7.2 712.3 %reduce-scatter.3.cloned.1.call-start = ((), (), s32[]{:S(2)}) async-start(), calls=%async_computation.2 | async-start | bytes 4259840 | tf_op jit(solution)/shard_map/reduce_scatter | solution.py:65
  15.8 778.3 %all-reduce.5.cloned.1.call-start = ((), (), s32[]{:S(2)}) async-start(), calls=%async_computation.3 | async-start | bytes 131072 | tf_op jit(solution)/shard_map/psum | solution.py:71
  16.7 704.3 %copy-start.13 = (f32[4,6]{1,0:T(4,128)S(1)}, f32[4,6]{1,0:T(4,128)}, u32[]{:S(2)}) copy-start(f32[4,6]{1,0:T(4,128)} %param.14) | copy-start | bytes 292
  16.7 777.4 %copy-start.15 = (f32[6]{0:T(128)S(1)}, f32[6]{0:T(128)}, u32[]{:S(2)}) copy-start(f32[6]{0:T(128)} %param.16) | copy-start | bytes 76
  16.8 778.2 %copy-start.1 = (f32[4,6,16,1024]{3,2,1,0:T(8,128)S(1)}, f32[4,6,16,1024]{3,2,1,0:T(8,128)}, u32[]{:S(2)}) copy-start(f32[4,6,16,1024]{3,2,1,0:T(8,128)} %param.10) | copy-start | bytes 4718596
  16.9 781.3 %collective-permute-start.2 = (bf16[1,16,1024]{2,1,0:T(8,128)(2,1)S(1)}, bf16[1,16,1024]{2,1,0:T(8,128)(2,1)S(1)}, u32[]{:S(2)}, u32[]{:S(2)}) collective-permute-start(bf16[1,16,1024]{2,1,0:T(8,128)(2,1)S(1)} %slice.207), channel_id=1, source_target_pairs={{0,64},{64,128},{128,192},{192,256},{256,320},{320,384},{384,448},... | collective-permute-start | bytes 98312 | tf_op jit(solution)/shard_map/ppermute | solution.py:12
  18.9 776.4 %copy-start.8 = (f32[6,16,1024]{2,1,0:T(8,128)}, f32[6,16,1024]{2,1,0:T(8,128)S(1)}, u32[]{:S(2)}) copy-start(f32[6,16,1024]{2,1,0:T(8,128)S(1)} %get-tuple-element.8) | copy-start | bytes 1179652
  18.9 794.5 %copy-start.4 = (f32[6,16,1024]{2,1,0:T(8,128)}, f32[6,16,1024]{2,1,0:T(8,128)S(1)}, u32[]{:S(2)}) copy-start(f32[6,16,1024]{2,1,0:T(8,128)S(1)} %get-tuple-element.7) | copy-start | bytes 1179652
  19.0 787.8 %collective-permute-start.5 = (f32[6,1,1024]{2,1,0:T(1,128)S(1)}, f32[6,1,1024]{2,1,0:T(1,128)S(1)}, u32[]{:S(2)}, u32[]{:S(2)}) collective-permute-start(f32[6,1,1024]{2,1,0:T(1,128)S(1)} %slice.110), channel_id=1, source_target_pairs={{0,1},{1,2},{2,3},{3,4},{4,5},{5,6},{6,7},{7,8},{8,9},{9,10},{10,1... | collective-permute-start | bytes 73736 | tf_op jit(solution)/shard_map/ppermute | solution.py:12
  720.9 152.5 %reduce-scatter.5.cloned.1.call-start = ((), (), s32[]{:S(2)}) async-start(), calls=%async_computation.4 | async-start | bytes 294912 | tf_op jit(solution)/shard_map/reduce_scatter | solution.py:102
  795.3 2.9 collective-permute-start
  796.7 3.2 collective-permute-start.1
  800.1 6.7 copy-start.9
  800.9 6.5 collective-permute-start.3
  804.3 8.6 collective-permute-start.4
  806.8 6.6 copy-start.2
  806.8 6.6 copy-start.6
  806.9 6.6 copy-start.14
  815.2 4.9 collective-permute-start.6
  818.8 4.0 collective-permute-start.7
  824.0 6.7 collective-permute-start.8
  825.9 8.6 collective-permute-start.9
  830.6 4.4 copy-start.3
  830.6 4.4 copy-start.5
  (5 other events, 12.8 us)
Sparse Core Ops, SparseCore 0:
  15.9 703.5 reduce-scatter.2
  721.9 72.1 all-reduce.4
  830.7 42.6 reduce-scatter.4
where the time goes:
time: 881 us; the launch traced here: 880 us
  waiting for transfers between devices  818 us (93%)
  starting transfers between devices  24.6 us (3%)
  between operations  14.3 us (2%)
  other arithmetic  12.7 us (1%)
    reduce_scatter x1, waiting for transfers between devices, on_device(): lax.psum_scatter(jnp.dot(selector, obs_values, preferred_element_type=jnp...  695 us
    psum x1, waiting for transfers between devices, on_device(): pixel_map = lax.psum(partial_map, 'lev')  73.1 us
    reduce_scatter x1, waiting for transfers between devices, on_device(): gradient = lax.psum_scatter(surface, 'lev', scatter_dimension=2, tiled=True)  35.9 us
  transfers between devices with their start and end apart: 13, of which 8 were waited for; matrix products, arithmetic and copies ran while one was open for 1% of the time, Pallas kernels for 0%

commit v1 on v0

v1 whole, which is shorter than its diff:
```python
import functools

import jax
import jax.numpy as jnp
import numpy as np
from jax import lax
from jax.experimental import pallas as pl
from jax.experimental.pallas import tpu as pltpu
from jax.sharding import Mesh
from jax.sharding import PartitionSpec as P

SPLIT = (4, 2, 16, 4)
SHIFTS = ((0, 8), (4, 12), (1, 9), (7, 15), (2, 10), (6, 14), (3, 11), (5, 13))
CAP = 64
LEV = ("x", "core")
TILE = ("z", "y")
ROWS = 24
VMEM = 48 * 1024 * 1024


def chain(axes, count, steps):
    first, last = max(0, -steps), min(count, count - steps)
    return functools.partial(
        lax.ppermute, axis_name=axes, perm=[(i, i + steps) for i in range(first, last)]
    )


def pack_kernel(tile_ref, block_ref, base_ref, obs_ref, out_ref):
    tiles = base_ref.shape[0]
    members, depth, _ = out_ref.shape
    count = obs_ref.shape[0]
    pair = 2 * CAP
    tile = tile_ref[...]
    block = block_ref[...]
    hot = lax.broadcasted_iota(jnp.int32, (tiles, count), 0) == tile
    before = lax.broadcasted_iota(jnp.int32, (count, count), 0) < lax.broadcasted_iota(
        jnp.int32, (count, count), 1
    )
    rank = jnp.dot(
        hot.astype(jnp.bfloat16), before.astype(jnp.bfloat16), preferred_element_type=jnp.float32
    )
    place = jnp.sum(jnp.where(hot, rank + base_ref[...], 0.0), axis=0, keepdims=True)
    place = place.astype(jnp.int32)
    member = place // pair
    slot = place - member * pair
    code = (block + 1 + jnp.where(slot >= CAP, 128, 0)).astype(jnp.float32)
    owns = lax.broadcasted_iota(jnp.int32, (members, count), 0) == member
    at = lax.broadcasted_iota(jnp.int32, (pair, count), 0) == slot
    codes = lax.dot_general(
        owns.astype(jnp.bfloat16),
        jnp.where(at, code, 0.0).astype(jnp.bfloat16),
        (((1,), (1,)), ((), ())),
        preferred_element_type=jnp.float32,
    ).astype(jnp.bfloat16)
    out_ref[:, pair:, :] = jnp.broadcast_to(codes[:, None, :], (members, depth - pair, 128))
    group = min(4, members)

    def body(g, _):
        rows = lax.broadcasted_iota(jnp.int32, (group * pair, count), 0)
        pick = rows == place - g * (group * pair)
        got = jnp.dot(
            pick.astype(jnp.bfloat16), obs_ref[...], preferred_element_type=jnp.float32
        ).astype(jnp.bfloat16)
        out_ref[pl.ds(g * group, group), :pair, :] = got.reshape(group, pair, 128)
        return 0

    lax.fori_loop(0, members // group, body, 0)


def sum_kernel(got_ref, out_ref):
    sources = got_ref.shape[0]
    pair = 2 * CAP
    total = jnp.zeros((256, 128), jnp.float32)
    for s in range(0, sources, 2):
        code = jnp.concatenate(
            [got_ref[s + i, pair : pair + 16, :].astype(jnp.float32)[:1] for i in range(2)], axis=1
        )
        pick = lax.broadcasted_iota(jnp.int32, (256, 2 * pair), 0) + 1 == code.astype(jnp.int32)
        rows = jnp.concatenate([got_ref[s + i, :pair, :] for i in range(2)], axis=0)
        total += jnp.dot(pick.astype(jnp.bfloat16), rows, preferred_element_type=jnp.float32)
    out_ref[...] = total.reshape(2, 128, 128)


def roll(x, shift, axis):
    return pltpu.roll(x, shift % x.shape[axis], axis)


def step_kernel(
    decay_ref,
    gain_ref,
    profile_ref,
    lam_ref,
    kz_ref,
    cx_ref,
    cy_ref,
    low_ref,
    high_ref,
    rim_ref,
    map_ref,
    out_ref,
    surface_ref,
    kzs,
    cxs,
    cys,
    blocks,
    field,
    scaled,
    later,
    mixed,
    moved,
):
    f32 = jnp.float32
    cols = lam_ref.shape[3]
    groups, parts = cols // 128, map_ref.shape[0]

    total = map_ref[0]
    for k in range(1, parts):
        total = total + map_ref[k]
    blocks[0:144, :] = total[0:144]
    blocks[144:176, :] = jnp.zeros((32, 128), f32)
    blocks[176:192, :] = total[144:160]
    for q in range(groups):
        field[:, q * 128 : (q + 1) * 128] = blocks[pl.ds(q, ROWS, stride=groups), :]

    def put(ref, at, body, plane):
        ref[at, 0:16, :] = body.astype(f32)
        ref[at, 16:24, :] = rim_ref[plane].astype(f32)

    for l in range(9):
        body = low_ref[8 + l] if l < 2 else (kz_ref[l - 2] if l < 8 else high_ref[8])
        put(kzs, l, body, 40 + l)
    for l in range(8):
        put(cxs, l, low_ref[10] if l < 1 else (cx_ref[l - 1] if l < 7 else high_ref[9]), 49 + l)
        put(cys, l, low_ref[11] if l < 1 else (cy_ref[l - 1] if l < 7 else high_ref[10]), 57 + l)

    def mix(ref, at, kz_at):
        here = ref[at]
        return here + kzs[kz_at] * (ref[at + 1] - here) - kzs[kz_at - 1] * (here - ref[at - 1])

    def advect(m, at):
        cx = cxs[at]
        gx = roll(m, -1, 0) - m
        value = m + jnp.maximum(cx, 0.0) * gx + roll(jnp.minimum(cx, 0.0) * gx, 1, 0)
        cy = cys[at]
        gy = roll(m, -1, 1) - m
        return value + jnp.maximum(cy, 0.0) * gy + roll(jnp.minimum(cy, 0.0) * gy, 1, 1)

    def tracer(c, _):
        total = jnp.zeros((16, cols), f32)
        for l in range(10):
            if l < 2:
                body = low_ref[c * 2 + l].astype(f32)
            elif l < 8:
                body = lam_ref[c, l - 2]
            else:
                body = high_ref[c * 2 + l - 8].astype(f32)
            own = body + gain_ref[l] * field[0:16, :]
            if 2 <= l < 8:
                total = total + profile_ref[c * 6 + l - 2] * own
            rim = rim_ref[c * 10 + l].astype(f32) + gain_ref[l] * field[16:24, :]
            scaled[l, 0:16, :] = decay_ref[c * 10 + l] * own
            scaled[l, 16:24, :] = decay_ref[c * 10 + l] * rim
        for l in range(1, 9):
            value = advect(mix(scaled, l, l), l - 1)
            if 2 <= l < 8:
                total = total + profile_ref[c * 6 + l - 2] * value[0:16]
            later[l - 1] = decay_ref[c * 10 + l] * value
        for q in range(groups):
            surface_ref[q, pl.ds(c * 16, 16), :] = total[:, q * 128 : (q + 1) * 128]
        for l in range(2, 8):
            out_ref[c, l - 2] = advect(mix(later, l - 1, l), l - 1)[0:16]
        return 0

    lax.fori_loop(0, lam_ref.shape[0], tracer, 0)


def on_device(
    lam_in,
    courant_x,
    courant_y,
    kz_face,
    loss_rate,
    profile,
    kernel,
    obs_values,
    obs_tile,
    obs_block,
):
    f32, bf16 = jnp.float32, jnp.bfloat16
    size_x, size_core, size_z, size_y = SPLIT
    lev_count, tile_count = size_x * size_core, size_z * size_y
    members = lev_count * size_y
    lev_index, tile_index = lax.axis_index(LEV), lax.axis_index(TILE)
    z_index = lax.axis_index("z")
    tracers, levels, rows, cols = lam_in.shape
    blocks = rows * cols // 128
    vmem = pl.BlockSpec(memory_space=pltpu.VMEM)
    smem = pl.BlockSpec(memory_space=pltpu.SMEM)
    params = pltpu.CompilerParams(vmem_limit_bytes=VMEM)

    last_row = (tile_index == tile_count - 1) & (jnp.arange(rows) == rows - 1)
    cx = jnp.where(last_row[None, :, None], 0.0, courant_x)
    cy = jnp.where((jnp.arange(cols) == cols - 1)[None, None, :], 0.0, courant_y)
    top = (lev_index == lev_count - 1) & (jnp.arange(levels) == levels - 1)
    kz = jnp.where(top[:, None, None], 0.0, kz_face)
    decay = jnp.exp(-loss_rate)

    def coded(first):
        row = jnp.concatenate([decay[:, first : first + 2].reshape(-1), kernel[first : first + 2]])
        row = jnp.pad(row, (0, cols - row.shape[0]))
        head = lax.reduce_precision(row, 8, 7)
        both = jnp.stack([head, row - head])
        return jnp.pad(both, ((0, rows - 2), (0, 0)))[None]

    def planes(first):
        return lam_in[:, first : first + 2].reshape(2 * tracers, rows, cols)

    up = jnp.concatenate([planes(levels - 2), kz[-2:], cx[-1:], cy[-1:], coded(levels - 2)])
    down = jnp.concatenate([planes(0), kz[:1], cx[:1], cy[:1], coded(0)])
    low = chain(LEV, lev_count, 1)(up.astype(bf16))
    high = chain(LEV, lev_count, -1)(down.astype(bf16))

    place = {d: (k, j) for k, pair in enumerate(SHIFTS) for j, d in enumerate(pair)}
    order = jnp.array([2 * size_y * place[d][0] + place[d][1] for d in range(size_z)], jnp.int32)
    tile = jnp.arange(tile_count)
    distance = (tile // size_y - z_index + size_z) % size_z
    base = (CAP * (order[distance] + 2 * (tile % size_y))).astype(f32)[:, None]
    packed = pl.pallas_call(
        pack_kernel,
        out_shape=jax.ShapeDtypeStruct((members, 2 * CAP + 16, 128), bf16),
        in_specs=[vmem] * 4,
        out_specs=vmem,
        compiler_params=params,
    )(obs_tile.reshape(1, -1), obs_block.reshape(1, -1), base, obs_values)
    got = lax.all_to_all(packed, LEV + ("y",), 0, 0, tiled=True)
    sums = pl.pallas_call(
        sum_kernel,
        out_shape=jax.ShapeDtypeStruct((2, blocks, 128), f32),
        in_specs=[vmem],
        out_specs=vmem,
        compiler_params=params,
    )(got)

    def along_z(value, j):
        perm = [
            (k * size_z + z, k * size_z + (z + SHIFTS[k][j]) % size_z)
            for k in range(lev_count)
            for z in range(size_z)
        ]
        return lax.ppermute(value, LEV + ("z",), perm)

    part = along_z(sums[0], 0) + along_z(sums[1], 1)
    edge = 2 * cols // 128
    after = chain(TILE, tile_count, -1)(part[:edge])
    prior = chain(TILE, tile_count, 1)(part[-edge:])
    part = jnp.concatenate([part, after, prior])
    parts = lax.all_gather(part, LEV, axis=0)

    def extended(own, below, above):
        return jnp.concatenate([below.astype(f32), own, above.astype(f32)], axis=-3)

    low_lam = low[: 2 * tracers].reshape(tracers, 2, rows, cols)
    high_lam = high[: 2 * tracers].reshape(tracers, 2, rows, cols)
    edge_of = lambda a, first, n: lax.slice_in_dim(a, first, first + n, axis=a.ndim - 2)

    def rim(first, n):
        cut = lambda a: edge_of(a, first, n)
        lam_rim = extended(cut(lam_in), cut(low_lam), cut(high_lam))
        kz_rim = extended(cut(kz), cut(low[8:10]), cut(high[8:9]))
        cx_rim = extended(cut(cx), cut(low[10:11]), cut(high[9:10]))
        cy_rim = extended(cut(cy), cut(low[11:12]), cut(high[10:11]))
        lam_rim = lam_rim.reshape((-1,) + lam_rim.shape[2:])
        return jnp.concatenate([lam_rim, kz_rim, cx_rim, cy_rim]).astype(bf16)

    from_after = chain(TILE, tile_count, -1)(rim(0, 2))
    from_prior = chain(TILE, tile_count, 1)(rim(rows - 2, 2))
    gap = jnp.zeros((from_after.shape[0], 4, cols), bf16)
    rims = jnp.concatenate([from_after, gap, from_prior], axis=1)

    def decoded(row):
        both = row[:2, : 2 * tracers + 2].astype(f32)
        both = both[0] + both[1]
        return both[: 2 * tracers].reshape(tracers, 2), both[2 * tracers :]

    low_decay, low_gain = decoded(low[12])
    high_decay, high_gain = decoded(high[11])
    decays = jnp.concatenate([low_decay, decay, high_decay], axis=1).reshape(-1)
    gains = jnp.concatenate([low_gain, kernel, high_gain])

    lam_out, surface = pl.pallas_call(
        step_kernel,
        out_shape=(
            jax.ShapeDtypeStruct(lam_in.shape, f32),
            jax.ShapeDtypeStruct((lev_count, tracers * rows, cols // lev_count), f32),
        ),
        in_specs=[smem] * 3 + [vmem] * 8,
        out_specs=(vmem, vmem),
        scratch_shapes=[
            pltpu.VMEM((9, ROWS, cols), f32),
            pltpu.VMEM((8, ROWS, cols), f32),
            pltpu.VMEM((8, ROWS, cols), f32),
            pltpu.VMEM((ROWS * cols // 128, 128), f32),
            pltpu.VMEM((ROWS, cols), f32),
            pltpu.VMEM((10, ROWS, cols), f32),
            pltpu.VMEM((8, ROWS, cols), f32),
            pltpu.VMEM((ROWS, cols), f32),
            pltpu.VMEM((ROWS, cols), f32),
        ],
        compiler_params=params,
    )(
        decays,
        gains,
        profile.reshape(-1),
        lam_in,
        kz,
        cx,
        cy,
        low,
        high,
        rims,
        parts,
    )
    shares = lax.all_to_all(surface, LEV, 0, 0, tiled=True)
    gradient = jnp.sum(shares, axis=0).reshape(tracers, rows, cols // lev_count)
    return lam_out, gradient


def solution(mesh):
    grid = Mesh(np.asarray(mesh.devices).reshape(SPLIT), ("x", "core", "z", "y"))
    in_specs = (
        P(None, LEV, TILE, None),
        P(LEV, TILE, None),
        P(LEV, TILE, None),
        P(LEV, TILE, None),
        P(None, LEV),
        P(None, LEV),
        P(LEV),
        P(LEV + TILE, None),
        P(LEV + TILE, None),
        P(LEV + TILE),
    )
    out_specs = (P(None, LEV, TILE, None), P(None, TILE, LEV))
    return jax.shard_map(
        on_device, mesh=grid, in_specs=in_specs, out_specs=out_specs, check_vma=False
    )
```

time: 881 us -> 126 us (0.14)
  the two profiles are of different devices: /device:TPU:24 before, /device:TPU:32 now
where the time goes in v1:
time: 126 us; the launch traced here: 125 us
  starting transfers between devices  41 us (33%)
  blocking collectives  30 us (24%)
  local copies, waits for them, and re-layouts  23.7 us (19%)
  Pallas kernels  13.7 us (11%)
  waiting for transfers between devices  9.47 us (8%)
  other arithmetic  6.18 us (5%)
    all_gather x1, blocking collectives, on_device(): parts = lax.all_gather(part, LEV, axis=0)  18.6 us
    unnamed x59, local copies, waits for them, and re-layouts  15.5 us
    ppermute x2, starting transfers between devices, along_z(): return lax.ppermute(value, LEV + ('z',), perm)  15.3 us
    all_to_all x1, blocking collectives, on_device(): shares = lax.all_to_all(surface, LEV, 0, 0, tiled=True)  11.4 us
    all_to_all x1, starting transfers between devices, on_device(): got = lax.all_to_all(packed, LEV + ('y',), 0, 0, tiled=True)  7.97 us
    pallas_call x1, Pallas kernels, on_device(): pl.pallas_call(step_kernel, out_shape=(jax.ShapeDtypeStruct(lam_in.shape,...  7.7 us
    ppermute x2, waiting for transfers between devices, along_z(): return lax.ppermute(value, LEV + ('z',), perm)  5.81 us
    ppermute x1, starting transfers between devices, on_device(): from_after = chain(TILE, tile_count, -1)(rim(0, 2))  5.69 us
  transfers between devices with their start and end apart: 9, of which 2 were waited for; matrix products, arithmetic and copies ran while one was open for 16% of the time, Pallas kernels for 5%

profile of v1, /device:TPU:32, one launch (start us, length us, event | category | flops | bytes accessed | tf_op | source)
XLA Modules:
  0.0 125.2 jit_solution(2868622887311657504)
XLA Ops:
  0.7 0.8 fusion.34
  2.4 2.3 %copy.30 = bf16[4,6,16,1024]{3,1,2,0:T(8,128)(2,1)S(1)} copy(f32[4,6,16,1024]{3,2,1,0:T(8,128)} %lam_ref.1) | data formatting | bytes 2359296 | tf_op args[0]
  10.2 1.3 %collective-permute-start.1 = (bf16[12,16,1024]{2,1,0:T(8,128)(2,1)}, bf16[12,16,1024]{2,1,0:T(8,128)(2,1)S(1)}, u32[]{:S(2)}, u32[]{:S(2)}) collective-permute-start(bf16[12,16,1024]{2,1,0:T(8,128)(2,1)} %constant_dynamic-update-slice_fusion.4), channel_id=1, source_target_pairs={{64,0},{128,64},{192,128},{256,192},{320,256},{384,320},{448,384},... | collective-permute-start | bytes 1179656 | tf_op jit(solution)/shard_map/ppermute | solution.py:221
  12.3 3.0 %collective-permute-start = (bf16[13,16,1024]{2,1,0:T(8,128)(2,1)}, bf16[13,16,1024]{2,1,0:T(8,128)(2,1)S(1)}, u32[]{:S(2)}, u32[]{:S(2)}) collective-permute-start(bf16[13,16,1024]{2,1,0:T(8,128)(2,1)} %constant_dynamic-update-slice_fusion), channel_id=1, source_target_pairs={{0,64},{64,128},{128,192},{192,256},{256,320},{320,384},{384,448},... | collective-permute-start | bytes 1277960 | tf_op jit(solution)/shard_map/ppermute | solution.py:220
  15.5 0.8 gather_fusion
  16.5 5.3 %shard_map.122 = bf16[32,144,128]{2,1,0:T(8,128)(2,1)} custom-call(s32[1,1024]{1,0:T(1,128)S(1)} %bitcast.32, s32[1,1024]{1,0:T(1,128)S(1)} %bitcast.33, f32[64,1]{1,0:T(8,128)S(1)} %fusion.16.base_ref, bf16[1024,128]{1,0:T(8,128)(2,1)S(1)} %copy-done.3), custom_call_target="tpu_custom_call" | custom-call | tf_op jit(solution)/shard_map/pallas_call | solution.py:228
  21.8 8.0 %all-to-all-start = ((bf16[32,144,128]{2,1,0:T(8,128)(2,1)}), bf16[32,144,128]{2,1,0:T(8,128)(2,1)S(1)}, u32[]{:S(2)}, u32[]{:S(2)}) async-start(bf16[32,144,128]{2,1,0:T(8,128)(2,1)} %shard_map.122), calls=%async_computation | async-start | bytes 2359296 | tf_op jit(solution)/shard_map/all_to_all | solution.py:235
  30.5 1.6 %fusion.28 = (bf16[4,6,2,1024]{3,1,2,0:T(8,128)(2,1)S(1)}, bf16[4,6,2,1024]{3,1,2,0:T(8,128)(2,1)}) fusion(bf16[4,6,16,1024]{3,1,2,0:T(8,128)(2,1)} %copy-done.7), kind=kLoop, calls=%fused_computation.102 | loop fusion | bytes 393216 | tf_op jit(solution)/shard_map/slice | solution.py:264
  35.2 1.2 pad_maximum_fusion.1
  36.6 0.8 constant_dynamic-update-slice_fusion.18
  37.6 0.8 constant_dynamic-update-slice_fusion.28
  40.8 1.6 %constant_dynamic-update-slice_fusion.13 = (bf16[65,2,1024]{2,1,0:T(2,128)(2,1)}, bf16[65,2,1024]{2,1,0:T(2,128)(2,1)}) fusion(bf16[65,2,1024]{2,1,0:T(2,128)(2,1)} %get-tuple-element.18, bf16[6,16,1024]{2,1,0:T(8,128)(2,1)} %copy-done.8, bf16[65,2,1024]{2,1,0:T(2,128)(2,1)} %get-tuple-element.19), kind=kLoop, calls=%fused_computation.38 | loop fusion | bytes 98304
  43.6 1.6 %constant_dynamic-update-slice_fusion.10 = (bf16[65,2,1024]{2,1,0:T(2,128)(2,1)}, bf16[65,2,1024]{2,1,0:T(2,128)(2,1)}) fusion(bf16[65,2,1024]{2,1,0:T(2,128)(2,1)} %get-tuple-element.16, bf16[6,16,1024]{2,1,0:T(8,128)(2,1)} %copy-done.9, bf16[65,2,1024]{2,1,0:T(2,128)(2,1)} %get-tuple-element.17), kind=kLoop, calls=%fused_computation.35 | loop fusion | bytes 98304
  45.8 5.7 %collective-permute-start.2 = (bf16[65,2,1024]{2,1,0:T(2,128)(2,1)}, bf16[65,2,1024]{2,1,0:T(2,128)(2,1)}, u32[]{:S(2)}, u32[]{:S(2)}) collective-permute-start(bf16[65,2,1024]{2,1,0:T(2,128)(2,1)} %get-tuple-element.22), channel_id=1, source_target_pairs={{1,0},{2,1},{3,2},{4,3},{5,4},{6,5},{7,6},{8,7},{9,8},{10,9},{11,1... | collective-permute-start | bytes 798728 | tf_op jit(solution)/shard_map/ppermute | solution.py:275
  51.5 1.9 %collective-permute-start.3 = (bf16[65,2,1024]{2,1,0:T(2,128)(2,1)}, bf16[65,2,1024]{2,1,0:T(2,128)(2,1)}, u32[]{:S(2)}, u32[]{:S(2)}) collective-permute-start(bf16[65,2,1024]{2,1,0:T(2,128)(2,1)} %get-tuple-element.23), channel_id=1, source_target_pairs={{0,1},{1,2},{2,3},{3,4},{4,5},{5,6},{6,7},{7,8},{8,9},{9,10},{10,1... | collective-permute-start | bytes 798728 | tf_op jit(solution)/shard_map/ppermute | solution.py:276
  54.3 14.6 %collective-permute-start.5 = (f32[128,128]{1,0:T(8,128)S(1)}, f32[128,128]{1,0:T(8,128)S(1)}, u32[]{:S(2)}, u32[]{:S(2)}) collective-permute-start(f32[128,128]{1,0:T(8,128)S(1)} %get-tuple-element.42), channel_id=1, source_target_pairs={{0,32},{4,36},{8,40},{12,44},{16,48},{20,52},{24,56},{28,60},{32,0... | collective-permute-start | bytes 196616 | tf_op jit(solution)/shard_map/ppermute | solution.py:250
  69.8 5.8 %collective-permute-done.5 = f32[128,128]{1,0:T(8,128)S(1)} collective-permute-done((f32[128,128]{1,0:T(8,128)S(1)}, f32[128,128]{1,0:T(8,128)S(1)}, u32[]{:S(2)}, u32[]{:S(2)}) %collective-permute-start.5) | collective-permute-done | bytes 65568 | tf_op jit(solution)/shard_map/ppermute | solution.py:250
  75.7 3.5 %collective-permute-start.6 = (f32[16,128]{1,0:T(8,128)S(1)}, f32[16,128]{1,0:T(8,128)S(1)}, u32[]{:S(2)}, u32[]{:S(2)}) collective-permute-start(f32[16,128]{1,0:T(8,128)S(1)} %get-tuple-element.44), channel_id=1, source_target_pairs={{1,0},{2,1},{3,2},{4,3},{5,4},{6,5},{7,6},{8,7},{9,8},{10,9},{11,1... | collective-permute-start | bytes 24584 | tf_op jit(solution)/shard_map/ppermute | solution.py:254
  79.2 2.3 %collective-permute-start.7 = (f32[16,128]{1,0:T(8,128)S(1)}, f32[16,128]{1,0:T(8,128)S(1)}, u32[]{:S(2)}, u32[]{:S(2)}) collective-permute-start(f32[16,128]{1,0:T(8,128)S(1)} %get-tuple-element.45), channel_id=1, source_target_pairs={{0,1},{1,2},{2,3},{3,4},{4,5},{5,6},{6,7},{7,8},{8,9},{9,10},{10,1... | collective-permute-start | bytes 24584 | tf_op jit(solution)/shard_map/ppermute | solution.py:255
  81.5 1.7 %pad_maximum_fusion.rim_ref = bf16[65,8,1024]{2,1,0:T(8,128)(2,1)S(1)} fusion(bf16[65,2,1024]{2,1,0:T(2,128)(2,1)} %collective-permute-done.3, bf16[65,2,1024]{2,1,0:T(2,128)(2,1)} %collective-permute-done.2, bf16[8]{0:T(256)(128)(2,1)S(1)} %copy-done.15), kind=kLoop, calls=%fused_computation.2 | loop fusion | flops 3194880 | bytes 1597456 | tf_op jit(solution)/shard_map/concatenate | solution.py:278
  83.2 3.6 %collective-permute-done.7 = f32[16,128]{1,0:T(8,128)S(1)} collective-permute-done((f32[16,128]{1,0:T(8,128)S(1)}, f32[16,128]{1,0:T(8,128)S(1)}, u32[]{:S(2)}, u32[]{:S(2)}) %collective-permute-start.7) | collective-permute-done | bytes 8224 | tf_op jit(solution)/shard_map/ppermute | solution.py:255
  86.9 18.6 %all-gather = f32[1280,128]{1,0:T(8,128)S(1)} all-gather(f32[160,128]{1,0:T(8,128)S(1)} %pad_maximum_fusion.3), channel_id=2, replica_groups=mesh['x'=4,'core'=2,'z'=16,'y'=4] {'x','core'}, dimensions={0}, use_global_device_ids=true | all-gather | bytes 737280 | tf_op jit(solution)/shard_map/all_gather | solution.py:257
  105.5 7.7 %shard_map.124 = (f32[4,6,16,1024]{3,2,1,0:T(8,128)}, f32[8,64,128]{2,1,0:T(8,128)S(1)}) custom-call(f32[40]{0:T(128)S(1)} %reshape.195.decay_ref, f32[10]{0:T(128)S(1)} %pad_maximum_fusion.5.gain_ref, f32[24]{0:T(128)S(1)} %reshape.196.profile_ref, f32[4,6,16,1024]{3,2,1,0:T(8,128)S(1)} %copy-done, f32[6,16,1024]{2,1,0:T(8,128)S(1)} %get-tuple-element.11.kz_ref, ...), custom_call_target="tpu_custom_call" | custom-call | tf_op jit(solution)/shard_map/pallas_call | solution.py:290
  113.2 11.4 %all_to_all.10 = f32[8,64,128]{2,1,0:T(8,128)S(1)} all-to-all(f32[8,64,128]{2,1,0:T(8,128)S(1)} %get-tuple-element.5), channel_id=1, replica_groups=mesh['x'=4,'core'=2,'z'=16,'y'=4] {'x','core'}, dimensions={0} | all-to-all | bytes 524288 | tf_op jit(solution)/shard_map/all_to_all | solution.py:323
  (117 shorter events, 18.2 us)
Async XLA Ops:
  4.7 2.0 %copy-start.10 = (f32[6,16,1024]{2,1,0:T(8,128)S(1)}, f32[6,16,1024]{2,1,0:T(8,128)}, u32[]{:S(2)}) copy-start(f32[6,16,1024]{2,1,0:T(8,128)} %param.14) | copy-start | bytes 1179652
  5.1 3.0 %copy-start.12 = (f32[6,16,1024]{2,1,0:T(8,128)S(1)}, f32[6,16,1024]{2,1,0:T(8,128)}, u32[]{:S(2)}) copy-start(f32[6,16,1024]{2,1,0:T(8,128)} %param.13) | copy-start | bytes 1179652
  5.9 2.2 %copy-start.11 = (f32[6,16,1024]{2,1,0:T(8,128)S(1)}, f32[6,16,1024]{2,1,0:T(8,128)}, u32[]{:S(2)}) copy-start(f32[6,16,1024]{2,1,0:T(8,128)} %param.12) | copy-start | bytes 1179652
  6.7 8.8 %copy-start.6 = (s32[16]{0:T(128)S(1)}, s32[16]{0:T(128)}, u32[]{:S(2)}) copy-start(s32[16]{0:T(128)} %constant.85.clone) | copy-start | bytes 196
  6.8 9.6 %copy-start.3 = (bf16[1024,128]{1,0:T(8,128)(2,1)S(1)}, bf16[1024,128]{1,0:T(8,128)(2,1)}, u32[]{:S(2)}) copy-start(bf16[1024,128]{1,0:T(8,128)(2,1)} %obs_ref.1) | copy-start | bytes 786436
  6.8 9.6 %copy-start.4 = (s32[1024,1]{0,1:T(1,128)S(1)}, s32[1024,1]{0,1:T(1,128)}, u32[]{:S(2)}) copy-start(s32[1024,1]{0,1:T(1,128)} %param.19) | copy-start | bytes 12292
  6.8 9.6 %copy-start.5 = (s32[1024]{0:T(1024)S(1)}, s32[1024]{0:T(1024)}, u32[]{:S(2)}) copy-start(s32[1024]{0:T(1024)} %param.20) | copy-start | bytes 12292
  10.2 21.9 %collective-permute-start.1 = (bf16[12,16,1024]{2,1,0:T(8,128)(2,1)}, bf16[12,16,1024]{2,1,0:T(8,128)(2,1)S(1)}, u32[]{:S(2)}, u32[]{:S(2)}) collective-permute-start(bf16[12,16,1024]{2,1,0:T(8,128)(2,1)} %constant_dynamic-update-slice_fusion.4), channel_id=1, source_target_pairs={{64,0},{128,64},{192,128},{256,192},{320,256},{384,320},{448,384},... | collective-permute-start | bytes 1179656 | tf_op jit(solution)/shard_map/ppermute | solution.py:221
  12.3 21.3 %collective-permute-start = (bf16[13,16,1024]{2,1,0:T(8,128)(2,1)}, bf16[13,16,1024]{2,1,0:T(8,128)(2,1)S(1)}, u32[]{:S(2)}, u32[]{:S(2)}) collective-permute-start(bf16[13,16,1024]{2,1,0:T(8,128)(2,1)} %constant_dynamic-update-slice_fusion), channel_id=1, source_target_pairs={{0,64},{64,128},{128,192},{192,256},{256,320},{320,384},{384,448},... | collective-permute-start | bytes 1277960 | tf_op jit(solution)/shard_map/ppermute | solution.py:220
  16.5 13.3 %copy-start.14 = (f32[4,6]{1,0:T(4,128)S(1)}, f32[4,6]{1,0:T(4,128)}, u32[]{:S(2)}) copy-start(f32[4,6]{1,0:T(4,128)} %param.16) | copy-start | bytes 292
  21.8 31.8 %all-to-all-start = ((bf16[32,144,128]{2,1,0:T(8,128)(2,1)}), bf16[32,144,128]{2,1,0:T(8,128)(2,1)S(1)}, u32[]{:S(2)}, u32[]{:S(2)}) async-start(bf16[32,144,128]{2,1,0:T(8,128)(2,1)} %shard_map.122), calls=%async_computation | async-start | bytes 2359296 | tf_op jit(solution)/shard_map/all_to_all | solution.py:235
  32.2 13.1 %copy-start.1 = (bf16[12,16,1024]{2,1,0:T(8,128)(2,1)}, bf16[12,16,1024]{2,1,0:T(8,128)(2,1)S(1)}, u32[]{:S(2)}) copy-start(bf16[12,16,1024]{2,1,0:T(8,128)(2,1)S(1)} %collective-permute-done.1.high_ref) | copy-start | bytes 1179652
  35.1 18.4 %copy-start.18 = (f32[1,10]{1,0:T(1,128)S(1)}, f32[1,10]{1,0:T(1,128)}, u32[]{:S(2)}) copy-start(f32[1,10]{1,0:T(1,128)} %copy-done.17) | copy-start | bytes 124
  36.6 33.1 %copy-start.13 = (f32[6]{0:T(128)S(1)}, f32[6]{0:T(128)}, u32[]{:S(2)}) copy-start(f32[6]{0:T(128)} %param.17) | copy-start | bytes 76
  36.6 33.1 %copy-start.16 = (f32[2]{0:T(128)S(1)}, f32[2]{0:T(128)}, u32[]{:S(2)}) copy-start(f32[2]{0:T(128)} %slice_bitcast_fusion.4) | copy-start | bytes 28
  37.4 44.2 %copy-start.15 = (bf16[8]{0:T(256)(128)(2,1)S(1)}, bf16[8]{0:T(256)(128)(2,1)}, u32[]{:S(2)}) copy-start(bf16[8]{0:T(256)(128)(2,1)} %pad.24.clone) | copy-start | bytes 52
  45.8 35.7 %collective-permute-start.2 = (bf16[65,2,1024]{2,1,0:T(2,128)(2,1)}, bf16[65,2,1024]{2,1,0:T(2,128)(2,1)}, u32[]{:S(2)}, u32[]{:S(2)}) collective-permute-start(bf16[65,2,1024]{2,1,0:T(2,128)(2,1)} %get-tuple-element.22), channel_id=1, source_target_pairs={{1,0},{2,1},{3,2},{4,3},{5,4},{6,5},{7,6},{8,7},{9,8},{10,9},{11,1... | collective-permute-start | bytes 798728 | tf_op jit(solution)/shard_map/ppermute | solution.py:275
  51.5 30.0 %collective-permute-start.3 = (bf16[65,2,1024]{2,1,0:T(2,128)(2,1)}, bf16[65,2,1024]{2,1,0:T(2,128)(2,1)}, u32[]{:S(2)}, u32[]{:S(2)}) collective-permute-start(bf16[65,2,1024]{2,1,0:T(2,128)(2,1)} %get-tuple-element.23), channel_id=1, source_target_pairs={{0,1},{1,2},{2,3},{3,4},{4,5},{5,6},{6,7},{7,8},{8,9},{9,10},{10,1... | collective-permute-start | bytes 798728 | tf_op jit(solution)/shard_map/ppermute | solution.py:276
  54.3 51.2 %copy-start = (f32[4,6,16,1024]{3,2,1,0:T(8,128)S(1)}, f32[4,6,16,1024]{3,2,1,0:T(8,128)}, u32[]{:S(2)}) copy-start(f32[4,6,16,1024]{3,2,1,0:T(8,128)} %lam_ref.1) | copy-start | bytes 4718596
  54.3 21.3 %collective-permute-start.5 = (f32[128,128]{1,0:T(8,128)S(1)}, f32[128,128]{1,0:T(8,128)S(1)}, u32[]{:S(2)}, u32[]{:S(2)}) collective-permute-start(f32[128,128]{1,0:T(8,128)S(1)} %get-tuple-element.42), channel_id=1, source_target_pairs={{0,32},{4,36},{8,40},{12,44},{16,48},{20,52},{24,56},{28,60},{32,0... | collective-permute-start | bytes 196616 | tf_op jit(solution)/shard_map/ppermute | solution.py:250
  69.0 6.7 %collective-permute-start.4 = (f32[128,128]{1,0:T(8,128)S(1)}, f32[128,128]{1,0:T(8,128)S(1)}, u32[]{:S(2)}, u32[]{:S(2)}) collective-permute-start(f32[128,128]{1,0:T(8,128)S(1)} %get-tuple-element.43), channel_id=1, source_target_pairs={{0,0},{4,4},{8,8},{12,12},{16,16},{20,20},{24,24},{28,28},{32,32},... | collective-permute-start | bytes 196616 | tf_op jit(solution)/shard_map/ppermute | solution.py:250
  69.8 35.7 %copy-start.2 = (bf16[12,16,1024]{2,1,0:T(8,128)(2,1)S(1)}, bf16[12,16,1024]{2,1,0:T(8,128)(2,1)}, u32[]{:S(2)}) copy-start(bf16[12,16,1024]{2,1,0:T(8,128)(2,1)} %copy-done.1) | copy-start | bytes 1179652
  75.7 7.6 %collective-permute-start.6 = (f32[16,128]{1,0:T(8,128)S(1)}, f32[16,128]{1,0:T(8,128)S(1)}, u32[]{:S(2)}, u32[]{:S(2)}) collective-permute-start(f32[16,128]{1,0:T(8,128)S(1)} %get-tuple-element.44), channel_id=1, source_target_pairs={{1,0},{2,1},{3,2},{4,3},{5,4},{6,5},{7,6},{8,7},{9,8},{10,9},{11,1... | collective-permute-start | bytes 24584 | tf_op jit(solution)/shard_map/ppermute | solution.py:254
  79.2 7.7 %collective-permute-start.7 = (f32[16,128]{1,0:T(8,128)S(1)}, f32[16,128]{1,0:T(8,128)S(1)}, u32[]{:S(2)}, u32[]{:S(2)}) collective-permute-start(f32[16,128]{1,0:T(8,128)S(1)} %get-tuple-element.45), channel_id=1, source_target_pairs={{0,1},{1,2},{2,3},{3,4},{4,5},{5,6},{6,7},{7,8},{8,9},{9,10},{10,1... | collective-permute-start | bytes 24584 | tf_op jit(solution)/shard_map/ppermute | solution.py:255
  (4 other events, 4.7 us)

commit v2 on v0

v2 whole, which is shorter than its diff:
```python
import functools

import jax
import jax.numpy as jnp
import numpy as np
from jax import lax
from jax.experimental import pallas as pl
from jax.experimental.pallas import tpu as pltpu
from jax.sharding import Mesh
from jax.sharding import PartitionSpec as P

SPLIT = (4, 2, 16, 4)
SHIFTS = ((0, 8), (4, 12), (1, 9), (7, 15), (2, 10), (6, 14), (3, 11), (5, 13))
CAP = 64
LEV = ("x", "core")
TILE = ("z", "y")
ROWS = 24
STRIP = 144
VMEM = 24 * 1024 * 1024
F32, BF16 = jnp.float32, jnp.bfloat16


def chain(axes, count, steps):
    first, last = max(0, -steps), min(count, count - steps)
    return functools.partial(
        lax.ppermute, axis_name=axes, perm=[(i, i + steps) for i in range(first, last)]
    )


def iota(shape, dim):
    return lax.broadcasted_iota(jnp.int32, shape, dim)


def pack_kernel(where_ref, tile_ref, block_ref, obs_ref, out_ref):
    size_z, size_y = SPLIT[2:]
    tiles = size_z * size_y
    members, depth, _ = out_ref.shape
    count = obs_ref.shape[0]
    pair, part = 2 * CAP, 256
    tile = tile_ref[...]
    block = block_ref[...]
    t = iota((tiles, 1), 0)
    distance = t // size_y - where_ref[0]
    distance = jnp.where(distance < 0, distance + size_z, distance)
    order = 2 * (t % size_y)
    for k, both in enumerate(SHIFTS):
        for j, d in enumerate(both):
            order = order + jnp.where(distance == d, 2 * size_y * k + j, 0)
    start = (CAP * order).astype(F32)
    hot = (iota((tiles, count), 0) == tile).astype(F32)
    cuts = [hot[:, i : i + part] for i in range(0, count, part)]
    before = (iota((part, part), 0) < iota((part, part), 1)).astype(BF16)
    rank = jnp.dot(
        jnp.concatenate(cuts, axis=0).astype(BF16), before, preferred_element_type=F32
    )
    places = []
    for i, cut in enumerate(cuts):
        here = cut * (rank[i * tiles : (i + 1) * tiles] + start)
        places.append(jnp.sum(here, axis=0, keepdims=True))
        start = start + jnp.sum(cut, axis=1, keepdims=True)
    place = jnp.concatenate(places, axis=1).astype(jnp.int32)
    member = place // pair
    slot = place - member * pair
    code = (block + 1 + jnp.where(slot >= CAP, 128, 0)).astype(F32)
    owns = (iota((members, count), 0) == member).astype(F32)
    at = iota((pair, count), 0) == slot
    codes = lax.dot_general(
        owns.astype(BF16),
        jnp.where(at, code, 0.0).astype(BF16),
        (((1,), (1,)), ((), ())),
        preferred_element_type=F32,
    ).astype(BF16)
    out_ref[:, pair:, :] = jnp.broadcast_to(codes[:, None, :], (members, depth - pair, 128))
    slots = at.astype(F32).astype(BF16)
    group = 4
    for g in range(0, members, group):
        pick = jnp.concatenate(
            [slots * owns[m : m + 1].astype(BF16) for m in range(g, g + group)], axis=0
        )
        got = jnp.dot(pick, obs_ref[...], preferred_element_type=F32).astype(BF16)
        out_ref[g : g + group, :pair, :] = got.reshape(group, pair, 128)


def sum_kernel(got_ref, out_ref):
    sources = got_ref.shape[0]
    pair = 2 * CAP
    total = jnp.zeros((256, 128), F32)
    for s in range(0, sources, 2):
        code = jnp.concatenate(
            [got_ref[s + i, pair : pair + 16, :].astype(F32)[:1] for i in range(2)], axis=1
        )
        pick = iota((256, 2 * pair), 0) + 1 == code.astype(jnp.int32)
        rows = jnp.concatenate([got_ref[s + i, :pair, :] for i in range(2)], axis=0)
        total += jnp.dot(pick.astype(BF16), rows, preferred_element_type=F32)
    out_ref[...] = total.reshape(2, 128, 128)


def masks(where_ref):
    def kz(value, level):
        return jnp.where(where_ref[2] == 1, 0.0, value) if level == 5 else value

    def cx(value, first):
        last = iota(value.shape, 0) + first == 15
        return jnp.where(last & (where_ref[1] == 1), 0.0, value)

    def cy(value):
        return jnp.where(iota(value.shape, 1) == value.shape[1] - 1, 0.0, value)

    return kz, cx, cy


def level_kernel(
    where_ref, decay_ref, gain_ref, lam_ref, kz_ref, cx_ref, cy_ref, after_ref, up_ref, down_ref
):
    mask_kz, mask_cx, mask_cy = masks(where_ref)
    for ref, first in ((up_ref, 4), (down_ref, 0)):
        for c in range(4):
            for i in range(2):
                ref[c * 2 + i] = lam_ref[c, first + i].astype(BF16)
        levels = (4, 5) if first else (0,)
        for i, level in enumerate(levels):
            ref[8 + i] = mask_kz(kz_ref[level], level).astype(BF16)
        at = 8 + len(levels)
        ref[at] = mask_cx(cx_ref[levels[-1]], 0).astype(BF16)
        ref[at + 1] = mask_cy(cy_ref[levels[-1]]).astype(BF16)
        row = iota(ref.shape[1:], 0)
        plane = jnp.zeros(ref.shape[1:], F32)
        for i in range(2):
            plane = jnp.where(row == 8 + i, gain_ref[first + i], plane)
            for c in range(4):
                plane = jnp.where(row == c * 2 + i, decay_ref[c * 6 + first + i], plane)
        rough = plane.astype(BF16)
        ref[at + 2] = rough
        ref[at + 3] = (plane - rough.astype(F32)).astype(BF16)


def row_kernel(
    where_ref, lam_ref, kz_ref, cx_ref, cy_ref, low_ref, high_ref, prior_ref, next_ref, strip
):
    mask_kz, mask_cx, mask_cy = masks(where_ref)
    for ref, first in ((prior_ref, 0), (next_ref, 14)):
        rows = slice(first, first + 2)

        def put(plane, value):
            strip[2 * plane : 2 * plane + 2, :] = value

        strip[130:144, :] = jnp.zeros((14, strip.shape[1]), F32)
        for c in range(4):
            for l in range(10):
                if l < 2:
                    value = low_ref[c * 2 + l].astype(F32)[rows]
                elif l < 8:
                    value = lam_ref[c, l - 2, rows, :]
                else:
                    value = high_ref[c * 2 + l - 8].astype(F32)[rows]
                put(c * 10 + l, value)
        for l in range(9):
            if l < 2:
                value = low_ref[8 + l].astype(F32)[rows]
            elif l < 8:
                value = mask_kz(kz_ref[l - 2, rows, :], l - 2)
            else:
                value = high_ref[8].astype(F32)[rows]
            put(40 + l, value)
        for l in range(8):
            if l < 1:
                x, y = low_ref[10].astype(F32)[rows], low_ref[11].astype(F32)[rows]
            elif l < 7:
                x = mask_cx(cx_ref[l - 1, rows, :], first)
                y = mask_cy(cy_ref[l - 1, rows, :])
            else:
                x, y = high_ref[9].astype(F32)[rows], high_ref[10].astype(F32)[rows]
            put(49 + l, x)
            put(57 + l, y)
        ref[...] = strip[...].astype(BF16)


def ready_kernel(
    where_ref,
    decay_ref,
    gain_ref,
    profile_ref,
    lam_ref,
    kz_ref,
    cx_ref,
    cy_ref,
    low_ref,
    high_ref,
    after_ref,
    prior_ref,
    kzs,
    cxs,
    cys,
    mixed_ref,
    coef_ref,
    surface_ref,
    decays,
    strip_after,
    strip_prior,
    gains,
    scaled,
):
    mask_kz, mask_cx, mask_cy = masks(where_ref)
    cols = lam_ref.shape[3]
    strip_after[...] = after_ref[...].astype(F32)
    strip_prior[...] = prior_ref[...].astype(F32)

    def rim(ref, plane):
        if ref.shape[0] == ROWS:
            ref[16:24, :] = jnp.zeros((8, cols), F32)
            ref[16:18, :] = strip_after[2 * plane : 2 * plane + 2, :]
            ref[22:24, :] = strip_prior[2 * plane : 2 * plane + 2, :]

    for l in range(9):
        if l < 2:
            body = low_ref[8 + l].astype(F32)
        elif l < 8:
            body = mask_kz(kz_ref[l - 2], l - 2)
        else:
            body = high_ref[8].astype(F32)
        kzs[l, 0:16, :] = body
        rim(kzs.at[l], 40 + l)
    for l in range(8):
        if l < 1:
            x, y = low_ref[10].astype(F32), low_ref[11].astype(F32)
        elif l < 7:
            x, y = mask_cx(cx_ref[l - 1], 0), mask_cy(cy_ref[l - 1])
        else:
            x, y = high_ref[9].astype(F32), high_ref[10].astype(F32)
        cxs[l, 0:16, :] = x
        cys[l, 0:16, :] = y
        rim(cxs.at[l], 49 + l)
        rim(cys.at[l], 57 + l)
    low_row = low_ref[12].astype(F32) + low_ref[13].astype(F32)
    high_row = high_ref[11].astype(F32) + high_ref[12].astype(F32)
    for l in range(10):
        for c in range(4):
            at = slice(c * 10 + l, c * 10 + l + 1)
            if l < 2:
                decays[at, :] = low_row[c * 2 + l : c * 2 + l + 1]
            elif l < 8:
                decays[at, :] = jnp.full((1, cols), decay_ref[c * 6 + l - 2], F32)
            else:
                decays[at, :] = high_row[c * 2 + l - 8 : c * 2 + l - 7]
        if l < 2:
            gains[l : l + 1, :] = low_row[8 + l : 9 + l]
        elif l < 8:
            gains[l : l + 1, :] = jnp.full((1, cols), gain_ref[l - 2], F32)
        else:
            gains[l : l + 1, :] = high_row[l : l + 1]
    for c in range(4):
        total = jnp.zeros((16, cols), F32)
        for l in range(10):
            if l < 2:
                body = low_ref[c * 2 + l].astype(F32)
            elif l < 8:
                body = lam_ref[c, l - 2]
                total = total + profile_ref[c * 6 + l - 2] * body
            else:
                body = high_ref[c * 2 + l - 8].astype(F32)
            scaled[l, 0:16, :] = body
            rim(scaled.at[l], c * 10 + l)
            scaled[l] = scaled[l] * decays[c * 10 + l : c * 10 + l + 1, :]
        surface_ref[c] = total

        def both(l):
            at = c * 10 + l
            return decays[at : at + 1, :] * gains[l : l + 1, :]

        for l in range(1, 9):
            here = scaled[l]
            above, below = kzs[l], kzs[l - 1]
            mixed_ref[c, l - 1] = (
                here + above * (scaled[l + 1] - here) - below * (here - scaled[l - 1])
            )
            gain = both(l)
            coef_ref[c, l - 1] = (
                gain + above * (both(l + 1) - gain) - below * (gain - both(l - 1))
            )


def roll(x, shift, axis):
    return pltpu.roll(x, shift % x.shape[axis], axis)


def advect(m, cx, cy, rows):
    gx = roll(m, -1, 0) - m
    back = roll(jnp.minimum(cx, 0.0) * gx, 1, 0)
    value = m[:rows] + jnp.maximum(cx[:rows], 0.0) * gx[:rows] + back[:rows]
    m, cy = m[:rows], cy[:rows]
    gy = roll(m, -1, 1) - m
    return value + jnp.maximum(cy, 0.0) * gy + roll(jnp.minimum(cy, 0.0) * gy, 1, 1)


def first_kernel(
    gain_ref,
    profile_ref,
    cxs,
    cys,
    mixed_ref,
    coef_ref,
    early_ref,
    decays,
    map_ref,
    later_ref,
    surface_ref,
    blocks,
    field,
):
    cols = early_ref.shape[2]
    groups, parts = cols // 128, map_ref.shape[0]
    total = map_ref[0]
    for k in range(1, parts):
        total = total + map_ref[k]
    blocks[0:144, :] = total[0:144]
    blocks[144:176, :] = jnp.zeros((32, 128), F32)
    blocks[176:192, :] = total[144:160]
    for q in range(groups):
        field[:, q * 128 : (q + 1) * 128] = blocks[pl.ds(q, ROWS, stride=groups), :]

    def tracer(c, _):
        weight = 0.0
        for l in range(6):
            weight = weight + profile_ref[c * 6 + l] * gain_ref[l]
        total = early_ref[c] + weight * field[0:16, :]
        for l in range(8):
            m = mixed_ref[c, l] + coef_ref[c, l] * field[...]
            value = advect(m, cxs[l], cys[l], ROWS)
            if 1 <= l < 7:
                total = total + profile_ref[c * 6 + l - 1] * value[0:16]
            later_ref[c, l] = decays[pl.ds(c * 10 + l + 1, 1), :] * value
        for q in range(groups):
            surface_ref[q, pl.ds(c * 16, 16), :] = total[:, q * 128 : (q + 1) * 128]
        return 0

    lax.fori_loop(0, early_ref.shape[0], tracer, 0)


def second_kernel(kzs, cxs, cys, later_ref, out_ref):
    def tracer(c, _):
        for l in range(6):
            here = later_ref[c, l + 1]
            m = (
                here
                + kzs[l + 2] * (later_ref[c, l + 2] - here)
                - kzs[l + 1] * (here - later_ref[c, l])
            )
            out_ref[c, l] = advect(m, cxs[l + 1], cys[l + 1], 16)
        return 0

    lax.fori_loop(0, out_ref.shape[0], tracer, 0)


def on_device(
    lam_in,
    courant_x,
    courant_y,
    kz_face,
    loss_rate,
    profile,
    kernel,
    obs_values,
    obs_tile,
    obs_block,
):
    size_x, size_core, size_z, size_y = SPLIT
    lev_count, tile_count = size_x * size_core, size_z * size_y
    members = lev_count * size_y
    tracers, levels, rows, cols = lam_in.shape
    blocks = rows * cols // 128
    vmem = pl.BlockSpec(memory_space=pltpu.VMEM)
    smem = pl.BlockSpec(memory_space=pltpu.SMEM)
    anywhere = pl.BlockSpec(memory_space=pl.ANY)
    shape = jax.ShapeDtypeStruct

    def call(body, outs, specs, scratch=(), flops=0, moved=0):
        return pl.pallas_call(
            body,
            out_shape=outs,
            in_specs=specs,
            out_specs=jax.tree.map(lambda _: vmem, outs),
            scratch_shapes=[pltpu.VMEM(s, F32) for s in scratch],
            compiler_params=pltpu.CompilerParams(vmem_limit_bytes=VMEM),
            cost_estimate=pl.CostEstimate(flops=flops, bytes_accessed=moved, transcendentals=0),
        )

    where = jnp.stack(
        [
            lax.axis_index("z"),
            (lax.axis_index(TILE) == tile_count - 1).astype(jnp.int32),
            (lax.axis_index(LEV) == lev_count - 1).astype(jnp.int32),
        ]
    )
    decay = jnp.exp(-loss_rate).reshape(-1)
    weights = profile.reshape(-1)

    packed = call(
        pack_kernel,
        shape((members, 2 * CAP + 16, 128), BF16),
        [smem] + [vmem] * 3,
        flops=1 << 30,
        moved=2 << 20,
    )(where, obs_tile.reshape(1, -1), obs_block.reshape(1, -1), obs_values)
    got = lax.all_to_all(packed, LEV + ("y",), 0, 0, tiled=True)

    up, down = call(
        level_kernel,
        (shape((14, rows, cols), BF16), shape((13, rows, cols), BF16)),
        [smem] * 3 + [vmem] * 4 + [anywhere],
        moved=4 << 20,
    )(where, decay, kernel, lam_in, kz_face, courant_x, courant_y, packed)
    low = chain(LEV, lev_count, 1)(up)
    high = chain(LEV, lev_count, -1)(down)
    first_rows, last_rows = call(
        row_kernel,
        (shape((STRIP, cols), BF16), shape((STRIP, cols), BF16)),
        [smem] + [vmem] * 6,
        scratch=[(STRIP, cols)],
        moved=5 << 20,
    )(where, lam_in, kz_face, courant_x, courant_y, low, high)
    after = chain(TILE, tile_count, -1)(first_rows)
    prior = chain(TILE, tile_count, 1)(last_rows)
    kzs, cxs, cys, mixed, coef, early, decays = call(
        ready_kernel,
        (
            shape((9, ROWS, cols), F32),
            shape((8, ROWS, cols), F32),
            shape((8, ROWS, cols), F32),
            shape((tracers, 8, ROWS, cols), F32),
            shape((tracers, 8, ROWS, cols), F32),
            shape((tracers, rows, cols), F32),
            shape((10 * tracers, cols), F32),
        ),
        [smem] * 4 + [vmem] * 8,
        scratch=[(STRIP, cols), (STRIP, cols), (16, cols), (10, ROWS, cols)],
        moved=12 << 20,
    )(
        where,
        decay,
        kernel,
        weights,
        lam_in,
        kz_face,
        courant_x,
        courant_y,
        low,
        high,
        after,
        prior,
    )

    sums = call(
        sum_kernel, shape((2, blocks, 128), F32), [vmem], flops=1 << 28, moved=1 << 20
    )(got)

    def along_z(value, j):
        perm = [
            (k * size_z + z, k * size_z + (z + SHIFTS[k][j]) % size_z)
            for k in range(lev_count)
            for z in range(size_z)
        ]
        return lax.ppermute(value, LEV + ("z",), perm)

    part = along_z(sums[0], 0) + along_z(sums[1], 1)
    edge = 2 * cols // 128
    part_after = chain(TILE, tile_count, -1)(part[:edge])
    part_prior = chain(TILE, tile_count, 1)(part[-edge:])
    parts = lax.all_gather(jnp.concatenate([part, part_after, part_prior]), LEV, axis=0)

    later, surface = call(
        first_kernel,
        (
            shape((tracers, 8, ROWS, cols), F32),
            shape((lev_count, tracers * rows, cols // lev_count), F32),
        ),
        [smem] * 2 + [vmem] * 7,
        scratch=[(ROWS * cols // 128, 128), (ROWS, cols)],
        moved=8 << 20,
    )(kernel, weights, cxs, cys, mixed, coef, early, decays, parts)
    shares = lax.all_to_all(surface, LEV, 0, 0, tiled=True)
    lam_out = call(
        second_kernel, shape(lam_in.shape, F32), [vmem] * 4, moved=6 << 20
    )(kzs, cxs, cys, later)
    gradient = jnp.sum(shares, axis=0).reshape(tracers, rows, cols // lev_count)
    return lam_out, gradient


def solution(mesh):
    grid = Mesh(np.asarray(mesh.devices).reshape(SPLIT), ("x", "core", "z", "y"))
    in_specs = (
        P(None, LEV, TILE, None),
        P(LEV, TILE, None),
        P(LEV, TILE, None),
        P(LEV, TILE, None),
        P(None, LEV),
        P(None, LEV),
        P(LEV),
        P(LEV + TILE, None),
        P(LEV + TILE, None),
        P(LEV + TILE),
    )
    out_specs = (P(None, LEV, TILE, None), P(None, TILE, LEV))
    return jax.shard_map(
        on_device, mesh=grid, in_specs=in_specs, out_specs=out_specs, check_vma=False
    )
```

time: 881 us -> 104 us (0.12)
  waiting for transfers between devices: 818 us -> 11.6 us
  starting transfers between devices: 24.6 us -> 47.3 us
  Pallas kernels: 0 us -> 20.7 us
  between operations: 14.3 us -> 0.89 us
  blocking collectives: 0 us -> 13.2 us
  other arithmetic: 12.7 us -> 0.73 us
    reduce_scatter x2 -> x0, waiting for transfers between devices: 731 us -> none  [the longest x1 695 us: on_device(): lax.psum_scatter(jnp.dot(selector, obs_values, preferred_element_type=jnp...]
    psum x1 -> x0, waiting for transfers between devices: 73.1 us -> none  [on_device(): pixel_map = lax.psum(partial_map, 'lev')]
    pallas_call x0 -> x7, Pallas kernels: none -> 20.7 us  [the longest x1 4.59 us: on_device(): call(first_kernel, (shape((tracers, 8, ROWS, cols), F32), shape((lev_coun...]
    ppermute x10 -> x8, waiting for transfers between devices: 14.3 us -> 0.02 us  [the longest x2 0.01 us: along_z(): return lax.ppermute(value, LEV + ('z',), perm)]
    all_gather x0 -> x1, blocking collectives: none -> 13.2 us  [on_device(): lax.all_gather(jnp.concatenate([part, part_after, part_prior]), LEV, axis=0)]
    all_to_all x0 -> x2, starting transfers between devices: none -> 12.8 us  [the longest x1 9.34 us: on_device(): got = lax.all_to_all(packed, LEV + ('y',), 0, 0, tiled=True)]
    all_to_all x0 -> x2, waiting for transfers between devices: none -> 11.5 us  [the longest x1 10.6 us: on_device(): got = lax.all_to_all(packed, LEV + ('y',), 0, 0, tiled=True)]
    ppermute x10 -> x8, starting transfers between devices: 24.5 us -> 34.5 us  [the longest x2 14.5 us: along_z(): return lax.ppermute(value, LEV + ('z',), perm)]
  transfers between devices with their start and end apart: 13 -> 10, of which waited for: 8 -> 2; matrix products, arithmetic and copies ran while one was open for 1% -> 1% of each run, Pallas kernels for 0% -> 12%
where the time goes in v2:
time: 104 us; the launch traced here: 103 us
  starting transfers between devices  47.3 us (45%)
  Pallas kernels  20.7 us (20%)
  blocking collectives  13.2 us (13%)
  waiting for transfers between devices  11.6 us (11%)
  local copies, waits for them, and re-layouts  8.55 us (8%)
    ppermute x2, starting transfers between devices, along_z(): return lax.ppermute(value, LEV + ('z',), perm)  14.5 us
    all_gather x1, blocking collectives, on_device(): lax.all_gather(jnp.concatenate([part, part_after, part_prior]), LEV, axis=0)  13.2 us
    all_to_all x1, waiting for transfers between devices, on_device(): got = lax.all_to_all(packed, LEV + ('y',), 0, 0, tiled=True)  10.6 us
    all_to_all x1, starting transfers between devices, on_device(): got = lax.all_to_all(packed, LEV + ('y',), 0, 0, tiled=True)  9.34 us
    unnamed x34, local copies, waits for them, and re-layouts  7.68 us
    ppermute x1, starting transfers between devices, on_device(): part_prior = chain(TILE, tile_count, 1)(part[-edge:])  6.03 us
    ppermute x1, starting transfers between devices, on_device(): prior = chain(TILE, tile_count, 1)(last_rows)  5.23 us
    pallas_call x1, Pallas kernels, on_device(): call(first_kernel, (shape((tracers, 8, ROWS, cols), F32), shape((lev_coun...  4.59 us
  transfers between devices with their start and end apart: 10, of which 2 were waited for; matrix products, arithmetic and copies ran while one was open for 1% of the time, Pallas kernels for 12%

profile of v2, /device:TPU:24, one launch (start us, length us, event | category | flops | bytes accessed | tf_op | source)
XLA Modules:
  0.0 103.0 jit_solution(10851381656112443030)
XLA Ops:
  0.7 0.9 copy-done.13
  3.0 4.3 %shard_map.113.after_ref = bf16[32,144,128]{2,1,0:T(8,128)(2,1)} custom-call(s32[3]{0:T(128)S(1)} %pad_add_fusion.where_ref, s32[1,1024]{1,0:T(1,128)S(1)} %bitcast.12, s32[1,1024]{1,0:T(1,128)S(1)} %bitcast.13, bf16[1024,128]{1,0:T(8,128)(2,1)S(1)} %copy-done.13), custom_call_target="tpu_custom_call" | custom-call | flops 1073741824 | bytes 2097152 | tf_op jit(solution)/shard_map/pallas_call | solution.py:397
  7.3 9.3 %all-to-all-start = ((bf16[32,144,128]{2,1,0:T(8,128)(2,1)}), bf16[32,144,128]{2,1,0:T(8,128)(2,1)S(1)}, u32[]{:S(2)}, u32[]{:S(2)}) async-start(bf16[32,144,128]{2,1,0:T(8,128)(2,1)} %shard_map.113.after_ref), calls=%async_computation | async-start | bytes 2359296 | tf_op jit(solution)/shard_map/all_to_all | solution.py:404
  16.8 1.0 copy-done.3
  17.8 1.6 %shard_map.114 = (bf16[14,16,1024]{2,1,0:T(8,128)(2,1)}, bf16[13,16,1024]{2,1,0:T(8,128)(2,1)}) custom-call(s32[3]{0:T(128)S(1)} %pad_add_fusion.where_ref, f32[24]{0:T(128)S(1)} %reshape.19.decay_ref, f32[6]{0:T(128)S(1)} %copy-done.12, f32[4,6,16,1024]{3,2,1,0:T(8,128)S(1)} %copy-done, f32[6,16,1024]{2,1,0:T(8,128)S(1)} %copy-done.1, ...), custom_call_target="tpu_custom_call" | custom-call | bytes 4194304 | tf_op jit(solution)/shard_map/pallas_call | solution.py:406
  19.4 2.8 %collective-permute-start = (bf16[14,16,1024]{2,1,0:T(8,128)(2,1)}, bf16[14,16,1024]{2,1,0:T(8,128)(2,1)}, u32[]{:S(2)}, u32[]{:S(2)}) collective-permute-start(bf16[14,16,1024]{2,1,0:T(8,128)(2,1)} %get-tuple-element.15), channel_id=1, source_target_pairs={{0,64},{64,128},{128,192},{192,256},{256,320},{320,384},{384,448},... | collective-permute-start | bytes 1376264 | tf_op jit(solution)/shard_map/ppermute | solution.py:412
  22.2 1.3 %collective-permute-start.1 = (bf16[13,16,1024]{2,1,0:T(8,128)(2,1)}, bf16[13,16,1024]{2,1,0:T(8,128)(2,1)}, u32[]{:S(2)}, u32[]{:S(2)}) collective-permute-start(bf16[13,16,1024]{2,1,0:T(8,128)(2,1)} %get-tuple-element.16), channel_id=1, source_target_pairs={{64,0},{128,64},{192,128},{256,192},{320,256},{384,320},{448,384},... | collective-permute-start | bytes 1277960 | tf_op jit(solution)/shard_map/ppermute | solution.py:413
  23.5 10.6 %all-to-all-done.got_ref = bf16[32,144,128]{2,1,0:T(8,128)(2,1)S(1)} async-done(((bf16[32,144,128]{2,1,0:T(8,128)(2,1)}), bf16[32,144,128]{2,1,0:T(8,128)(2,1)S(1)}, u32[]{:S(2)}, u32[]{:S(2)}) %all-to-all-start) | async-done | bytes 1179680 | tf_op jit(solution)/shard_map/all_to_all | solution.py:404
  34.8 13.7 %collective-permute-start.5 = (f32[128,128]{1,0:T(8,128)S(1)}, f32[128,128]{1,0:T(8,128)S(1)}, u32[]{:S(2)}, u32[]{:S(2)}) collective-permute-start(f32[128,128]{1,0:T(8,128)S(1)} %get-tuple-element.28), channel_id=1, source_target_pairs={{0,32},{4,36},{8,40},{12,44},{16,48},{20,52},{24,56},{28,60},{32,0... | collective-permute-start | bytes 196616 | tf_op jit(solution)/shard_map/ppermute | solution.py:462
  49.4 2.4 %shard_map.115 = (bf16[144,1024]{1,0:T(8,128)(2,1)}, bf16[144,1024]{1,0:T(8,128)(2,1)}) custom-call(s32[3]{0:T(128)S(1)} %pad_add_fusion.where_ref, f32[4,6,16,1024]{3,2,1,0:T(8,128)S(1)} %copy-done, f32[6,16,1024]{2,1,0:T(8,128)S(1)} %copy-done.1, f32[6,16,1024]{2,1,0:T(8,128)S(1)} %copy-done.2, f32[6,16,1024]{2,1,0:T(8,128)S(1)} %copy-done.4, ...), custom_call_target="tpu_custom_call" | custom-call | bytes 5242880 | tf_op jit(solution)/shard_map/pallas_call | solution.py:414
  51.8 2.7 %collective-permute-start.2 = (bf16[144,1024]{1,0:T(8,128)(2,1)}, bf16[144,1024]{1,0:T(8,128)(2,1)S(1)}, u32[]{:S(2)}, u32[]{:S(2)}) collective-permute-start(bf16[144,1024]{1,0:T(8,128)(2,1)} %get-tuple-element.17), channel_id=1, source_target_pairs={{1,0},{2,1},{3,2},{4,3},{5,4},{6,5},{7,6},{8,7},{9,8},{10,9},{11,1... | collective-permute-start | bytes 884744 | tf_op jit(solution)/shard_map/ppermute | solution.py:421
  54.5 5.2 %collective-permute-start.3 = (bf16[144,1024]{1,0:T(8,128)(2,1)}, bf16[144,1024]{1,0:T(8,128)(2,1)S(1)}, u32[]{:S(2)}, u32[]{:S(2)}) collective-permute-start(bf16[144,1024]{1,0:T(8,128)(2,1)} %get-tuple-element.18), channel_id=1, source_target_pairs={{0,1},{1,2},{2,3},{3,4},{4,5},{5,6},{6,7},{7,8},{8,9},{9,10},{10,1... | collective-permute-start | bytes 884744 | tf_op jit(solution)/shard_map/ppermute | solution.py:422
  59.8 1.9 %collective-permute-start.6 = (f32[16,128]{1,0:T(8,128)S(1)}, f32[16,128]{1,0:T(8,128)S(1)}, u32[]{:S(2)}, u32[]{:S(2)}) collective-permute-start(f32[16,128]{1,0:T(8,128)S(1)} %get-tuple-element.30), channel_id=1, source_target_pairs={{1,0},{2,1},{3,2},{4,3},{5,4},{6,5},{7,6},{8,7},{9,8},{10,9},{11,1... | collective-permute-start | bytes 24584 | tf_op jit(solution)/shard_map/ppermute | solution.py:466
  61.7 6.0 %collective-permute-start.7 = (f32[16,128]{1,0:T(8,128)S(1)}, f32[16,128]{1,0:T(8,128)S(1)}, u32[]{:S(2)}, u32[]{:S(2)}) collective-permute-start(f32[16,128]{1,0:T(8,128)S(1)} %get-tuple-element.31), channel_id=1, source_target_pairs={{0,1},{1,2},{2,3},{3,4},{4,5},{5,6},{6,7},{7,8},{8,9},{9,10},{10,1... | collective-permute-start | bytes 24584 | tf_op jit(solution)/shard_map/ppermute | solution.py:467
  68.5 4.1 %shard_map.116 = (f32[9,24,1024]{2,1,0:T(8,128)S(1)}, f32[8,24,1024]{2,1,0:T(8,128)S(1)}, f32[8,24,1024]{2,1,0:T(8,128)S(1)}, f32[4,8,24,1024]{3,2,1,0:T(8,128)S...) custom-call(s32[3]{0:T(128)S(1)} %pad_add_fusion.where_ref, ...), custom_call_target="tpu_custom_call" | custom-call | bytes 12582912 | tf_op jit(solution)/shard_map/pallas_call | solution.py:423
  72.7 0.9 copy-done.10
  73.6 13.2 %all-gather = f32[1280,128]{1,0:T(8,128)S(1)} all-gather(f32[160,128]{1,0:T(8,128)S(1)} %pad_maximum_fusion), channel_id=2, replica_groups=mesh['x'=4,'core'=2,'z'=16,'y'=4] {'x','core'}, dimensions={0}, use_global_device_ids=true | all-gather | bytes 737280 | tf_op jit(solution)/shard_map/all_gather | solution.py:468
  86.9 4.6 %shard_map.118 = (f32[4,8,24,1024]{3,2,1,0:T(8,128)S(1)}, f32[8,64,128]{2,1,0:T(8,128)}) custom-call(f32[6]{0:T(128)S(1)} %copy-done.12, f32[24]{0:T(128)S(1)} %reshape.20.profile_ref, f32[8,24,1024]{2,1,0:T(8,128)S(1)} %get-tuple-element.20.cxs, f32[8,24,1024]{2,1,0:T(8,128)S(1)} %get-tuple-element.21.cys, ...), custom_call_target="tpu_custom_call" | custom-call | bytes 8388608 | tf_op jit(solution)/shard_map/pallas_call | solution.py:470
  91.5 3.4 %all-to-all-start.1 = ((f32[8,64,128]{2,1,0:T(8,128)}), f32[8,64,128]{2,1,0:T(8,128)S(1)}, u32[]{:S(2)}, u32[]{:S(2)}) async-start(f32[8,64,128]{2,1,0:T(8,128)} %get-tuple-element.27), calls=%async_computation.1 | async-start | bytes 524288 | tf_op jit(solution)/shard_map/all_to_all | solution.py:480
  94.9 1.1 %copy-done.7 = f32[8,24,1024]{2,1,0:T(8,128)S(1)} copy-done((f32[8,24,1024]{2,1,0:T(8,128)S(1)}, f32[8,24,1024]{2,1,0:T(8,128)}, u32[]{:S(2)}) %copy-start.7) | copy-done | bytes 786456
  96.0 1.1 %copy-done.9 = f32[8,24,1024]{2,1,0:T(8,128)S(1)} copy-done((f32[8,24,1024]{2,1,0:T(8,128)S(1)}, f32[8,24,1024]{2,1,0:T(8,128)}, u32[]{:S(2)}) %copy-start.9) | copy-done | bytes 786456
  97.2 1.2 %copy-done.11 = f32[9,24,1024]{2,1,0:T(8,128)S(1)} copy-done((f32[9,24,1024]{2,1,0:T(8,128)S(1)}, f32[9,24,1024]{2,1,0:T(8,128)}, u32[]{:S(2)}) %copy-start.11) | copy-done | bytes 884760
  98.3 3.0 %shard_map.119 = f32[4,6,16,1024]{3,2,1,0:T(8,128)} custom-call(f32[9,24,1024]{2,1,0:T(8,128)S(1)} %copy-done.11, f32[8,24,1024]{2,1,0:T(8,128)S(1)} %copy-done.7, f32[8,24,1024]{2,1,0:T(8,128)S(1)} %copy-done.9, f32[4,8,24,1024]{3,2,1,0:T(8,128)S(1)} %get-tuple-element.26.later_ref), custom_call_target="tpu_custom_call" | custom-call | bytes 6291456 | tf_op jit(solution)/shard_map/pallas_call | solution.py:481
  101.4 1.0 all-to-all-done.1
  (47 shorter events, 4.5 us)
Async XLA Ops:
  0.7 1.0 copy-start.13
  3.0 13.6 %copy-start.16 = (f32[4,6]{1,0:T(4,128)S(1)}, f32[4,6]{1,0:T(4,128)}, u32[]{:S(2)}) copy-start(f32[4,6]{1,0:T(4,128)} %param.14) | copy-start | bytes 292
  7.3 9.5 %copy-start = (f32[4,6,16,1024]{3,2,1,0:T(8,128)S(1)}, f32[4,6,16,1024]{3,2,1,0:T(8,128)}, u32[]{:S(2)}) copy-start(f32[4,6,16,1024]{3,2,1,0:T(8,128)} %lam_ref.5) | copy-start | bytes 4718596
  7.3 9.5 %copy-start.1 = (f32[6,16,1024]{2,1,0:T(8,128)S(1)}, f32[6,16,1024]{2,1,0:T(8,128)}, u32[]{:S(2)}) copy-start(f32[6,16,1024]{2,1,0:T(8,128)} %kz_ref.5) | copy-start | bytes 1179652
  7.3 9.5 %copy-start.2 = (f32[6,16,1024]{2,1,0:T(8,128)S(1)}, f32[6,16,1024]{2,1,0:T(8,128)}, u32[]{:S(2)}) copy-start(f32[6,16,1024]{2,1,0:T(8,128)} %cx_ref.5) | copy-start | bytes 1179652
  7.3 9.5 %copy-start.12 = (f32[6]{0:T(128)S(1)}, f32[6]{0:T(128)}, u32[]{:S(2)}) copy-start(f32[6]{0:T(128)} %gain_ref.5) | copy-start | bytes 76
  7.3 26.7 %all-to-all-start = ((bf16[32,144,128]{2,1,0:T(8,128)(2,1)}), bf16[32,144,128]{2,1,0:T(8,128)(2,1)S(1)}, u32[]{:S(2)}, u32[]{:S(2)}) async-start(bf16[32,144,128]{2,1,0:T(8,128)(2,1)} %shard_map.113.after_ref), calls=%async_computation | async-start | bytes 2359296 | tf_op jit(solution)/shard_map/all_to_all | solution.py:404
  16.8 1.0 copy-start.3
  19.4 30.0 %collective-permute-start = (bf16[14,16,1024]{2,1,0:T(8,128)(2,1)}, bf16[14,16,1024]{2,1,0:T(8,128)(2,1)}, u32[]{:S(2)}, u32[]{:S(2)}) collective-permute-start(bf16[14,16,1024]{2,1,0:T(8,128)(2,1)} %get-tuple-element.15), channel_id=1, source_target_pairs={{0,64},{64,128},{128,192},{192,256},{256,320},{320,384},{384,448},... | collective-permute-start | bytes 1376264 | tf_op jit(solution)/shard_map/ppermute | solution.py:412
  22.2 27.1 %collective-permute-start.1 = (bf16[13,16,1024]{2,1,0:T(8,128)(2,1)}, bf16[13,16,1024]{2,1,0:T(8,128)(2,1)}, u32[]{:S(2)}, u32[]{:S(2)}) collective-permute-start(bf16[13,16,1024]{2,1,0:T(8,128)(2,1)} %get-tuple-element.16), channel_id=1, source_target_pairs={{64,0},{128,64},{192,128},{256,192},{320,256},{384,320},{448,384},... | collective-permute-start | bytes 1277960 | tf_op jit(solution)/shard_map/ppermute | solution.py:413
  34.1 15.3 %copy-start.4 = (f32[6,16,1024]{2,1,0:T(8,128)S(1)}, f32[6,16,1024]{2,1,0:T(8,128)}, u32[]{:S(2)}) copy-start(f32[6,16,1024]{2,1,0:T(8,128)} %cy_ref.5) | copy-start | bytes 1179652
  34.8 25.0 %collective-permute-start.5 = (f32[128,128]{1,0:T(8,128)S(1)}, f32[128,128]{1,0:T(8,128)S(1)}, u32[]{:S(2)}, u32[]{:S(2)}) collective-permute-start(f32[128,128]{1,0:T(8,128)S(1)} %get-tuple-element.28), channel_id=1, source_target_pairs={{0,32},{4,36},{8,40},{12,44},{16,48},{20,52},{24,56},{28,60},{32,0... | collective-permute-start | bytes 196616 | tf_op jit(solution)/shard_map/ppermute | solution.py:462
  48.5 20.0 %copy-start.5 = (f32[6,16,1024]{2,1,0:T(8,128)S(1)}, f32[6,16,1024]{2,1,0:T(8,128)}, u32[]{:S(2)}) copy-start(f32[6,16,1024]{2,1,0:T(8,128)} %cy_ref.5) | copy-start | bytes 1179652
  48.5 11.2 %collective-permute-start.4 = (f32[128,128]{1,0:T(8,128)S(1)}, f32[128,128]{1,0:T(8,128)S(1)}, u32[]{:S(2)}, u32[]{:S(2)}) collective-permute-start(f32[128,128]{1,0:T(8,128)S(1)} %get-tuple-element.29), channel_id=1, source_target_pairs={{0,0},{4,4},{8,8},{12,12},{16,16},{20,20},{24,24},{28,28},{32,32},... | collective-permute-start | bytes 196616 | tf_op jit(solution)/shard_map/ppermute | solution.py:462
  51.8 16.7 %collective-permute-start.2 = (bf16[144,1024]{1,0:T(8,128)(2,1)}, bf16[144,1024]{1,0:T(8,128)(2,1)S(1)}, u32[]{:S(2)}, u32[]{:S(2)}) collective-permute-start(bf16[144,1024]{1,0:T(8,128)(2,1)} %get-tuple-element.17), channel_id=1, source_target_pairs={{1,0},{2,1},{3,2},{4,3},{5,4},{6,5},{7,6},{8,7},{9,8},{10,9},{11,1... | collective-permute-start | bytes 884744 | tf_op jit(solution)/shard_map/ppermute | solution.py:421
  54.5 14.0 %collective-permute-start.3 = (bf16[144,1024]{1,0:T(8,128)(2,1)}, bf16[144,1024]{1,0:T(8,128)(2,1)S(1)}, u32[]{:S(2)}, u32[]{:S(2)}) collective-permute-start(bf16[144,1024]{1,0:T(8,128)(2,1)} %get-tuple-element.18), channel_id=1, source_target_pairs={{0,1},{1,2},{2,3},{3,4},{4,5},{5,6},{6,7},{7,8},{8,9},{9,10},{10,1... | collective-permute-start | bytes 884744 | tf_op jit(solution)/shard_map/ppermute | solution.py:422
  59.8 13.8 %collective-permute-start.6 = (f32[16,128]{1,0:T(8,128)S(1)}, f32[16,128]{1,0:T(8,128)S(1)}, u32[]{:S(2)}, u32[]{:S(2)}) collective-permute-start(f32[16,128]{1,0:T(8,128)S(1)} %get-tuple-element.30), channel_id=1, source_target_pairs={{1,0},{2,1},{3,2},{4,3},{5,4},{6,5},{7,6},{8,7},{9,8},{10,9},{11,1... | collective-permute-start | bytes 24584 | tf_op jit(solution)/shard_map/ppermute | solution.py:466
  61.7 11.9 %collective-permute-start.7 = (f32[16,128]{1,0:T(8,128)S(1)}, f32[16,128]{1,0:T(8,128)S(1)}, u32[]{:S(2)}, u32[]{:S(2)}) collective-permute-start(f32[16,128]{1,0:T(8,128)S(1)} %get-tuple-element.31), channel_id=1, source_target_pairs={{0,1},{1,2},{2,3},{3,4},{4,5},{5,6},{6,7},{7,8},{8,9},{9,10},{10,1... | collective-permute-start | bytes 24584 | tf_op jit(solution)/shard_map/ppermute | solution.py:467
  73.6 17.9 %copy-start.6 = (f32[8,24,1024]{2,1,0:T(8,128)}, f32[8,24,1024]{2,1,0:T(8,128)S(1)}, u32[]{:S(2)}) copy-start(f32[8,24,1024]{2,1,0:T(8,128)S(1)} %get-tuple-element.20.cxs) | copy-start | bytes 2359300
  73.6 17.9 %copy-start.8 = (f32[8,24,1024]{2,1,0:T(8,128)}, f32[8,24,1024]{2,1,0:T(8,128)S(1)}, u32[]{:S(2)}) copy-start(f32[8,24,1024]{2,1,0:T(8,128)S(1)} %get-tuple-element.21.cys) | copy-start | bytes 2359300
  91.5 10.9 %all-to-all-start.1 = ((f32[8,64,128]{2,1,0:T(8,128)}), f32[8,64,128]{2,1,0:T(8,128)S(1)}, u32[]{:S(2)}, u32[]{:S(2)}) async-start(f32[8,64,128]{2,1,0:T(8,128)} %get-tuple-element.27), calls=%async_computation.1 | async-start | bytes 524288 | tf_op jit(solution)/shard_map/all_to_all | solution.py:480
  94.9 1.1 %copy-start.7 = (f32[8,24,1024]{2,1,0:T(8,128)S(1)}, f32[8,24,1024]{2,1,0:T(8,128)}, u32[]{:S(2)}) copy-start(f32[8,24,1024]{2,1,0:T(8,128)} %copy-done.6) | copy-start | bytes 2359300
  96.0 1.1 %copy-start.9 = (f32[8,24,1024]{2,1,0:T(8,128)S(1)}, f32[8,24,1024]{2,1,0:T(8,128)}, u32[]{:S(2)}) copy-start(f32[8,24,1024]{2,1,0:T(8,128)} %copy-done.8) | copy-start | bytes 2359300
  97.2 1.2 %copy-start.11 = (f32[9,24,1024]{2,1,0:T(8,128)S(1)}, f32[9,24,1024]{2,1,0:T(8,128)}, u32[]{:S(2)}) copy-start(f32[9,24,1024]{2,1,0:T(8,128)} %copy-done.10) | copy-start | bytes 2654212
  (3 other events, 2.3 us)

commit v3 on v2

--- a/solution.py
+++ b/solution.py
@@ -17,6 +17,7 @@
 ROWS = 24
 STRIP = 144
 VMEM = 24 * 1024 * 1024
+MOST = 63487488
 F32, BF16 = jnp.float32, jnp.bfloat16
 
 
@@ -31,54 +32,96 @@
     return lax.broadcasted_iota(jnp.int32, shape, dim)
 
 
-def pack_kernel(where_ref, tile_ref, block_ref, obs_ref, out_ref):
+def rank_of(tile, here, size_z, size_y):
+    distance = tile // size_y - here
+    distance = jnp.where(distance < 0, distance + size_z, distance)
+    order = 2 * (tile % size_y)
+    for k, both in enumerate(SHIFTS):
+        for j, d in enumerate(both):
+            order = order + jnp.where(distance == d, 2 * size_y * k + j, 0)
+    return order
+
+
+def one(mask):
+    return mask.astype(F32).astype(BF16)
+
+
+def pack_kernel(
+    where_ref,
+    tile_hbm,
+    block_hbm,
+    obs_hbm,
+    out_ref,
+    tile_ref,
+    block_ref,
+    obs_ref,
+    ordered,
+    starts,
+    starts_smem,
+    sems,
+):
     size_z, size_y = SPLIT[2:]
     tiles = size_z * size_y
     members, depth, _ = out_ref.shape
     count = obs_ref.shape[0]
     pair, part = 2 * CAP, 256
-    tile = tile_ref[...]
-    block = block_ref[...]
-    t = iota((tiles, 1), 0)
-    distance = t // size_y - where_ref[0]
-    distance = jnp.where(distance < 0, distance + size_z, distance)
-    order = 2 * (t % size_y)
-    for k, both in enumerate(SHIFTS):
-        for j, d in enumerate(both):
-            order = order + jnp.where(distance == d, 2 * size_y * k + j, 0)
-    start = (CAP * order).astype(F32)
-    hot = (iota((tiles, count), 0) == tile).astype(F32)
+    copies = [
+        pltpu.make_async_copy(tile_hbm, tile_ref, sems.at[0]),
+        pltpu.make_async_copy(block_hbm, block_ref, sems.at[1]),
+        pltpu.make_async_copy(obs_hbm, obs_ref, sems.at[2]),
+    ]
+    for copy in copies:
+        copy.start()
+    order = rank_of(iota((tiles, 1), 0), where_ref[0], size_z, size_y)
+    order_row = rank_of(iota((1, tiles), 1), where_ref[0], size_z, size_y)
+    before = (iota((part, part), 0) < iota((part, part), 1)).astype(BF16)
+    copies[0].wait()
+    hot = (iota((tiles, count), 0) == tile_ref[...]).astype(F32)
     cuts = [hot[:, i : i + part] for i in range(0, count, part)]
-    before = (iota((part, part), 0) < iota((part, part), 1)).astype(BF16)
+    counts = [jnp.sum(cut, axis=1, keepdims=True) for cut in cuts]
+    amount = counts[0]
+    for more in counts[1:]:
+        amount = amount + more
+    amounts = jnp.broadcast_to(amount, (tiles, 128)).astype(BF16)
+    first = jnp.dot(one(order_row < order), amounts, preferred_element_type=F32)[:, :1]
+    opening = jnp.dot(one(order_row // 2 < order // 2), amounts, preferred_element_type=F32)[:, :1]
+    ahead = jnp.where(order < 2 * iota((tiles, 128), 1), amount, 0.0)
+    ahead = jnp.sum(ahead, axis=0, keepdims=True)
+    starts[...] = jnp.broadcast_to(ahead, (8, 128)).astype(jnp.int32)
+    sent = pltpu.make_async_copy(starts, starts_smem, sems.at[3])
+    sent.start()
     rank = jnp.dot(
         jnp.concatenate(cuts, axis=0).astype(BF16), before, preferred_element_type=F32
     )
-    places = []
+    tag = (pair * order).astype(F32)
+    places, slots = [], []
     for i, cut in enumerate(cuts):
-        here = cut * (rank[i * tiles : (i + 1) * tiles] + start)
-        places.append(jnp.sum(here, axis=0, keepdims=True))
-        start = start + jnp.sum(cut, axis=1, keepdims=True)
+        at = rank[i * tiles : (i + 1) * tiles] + first
+        places.append(jnp.sum(cut * at, axis=0, keepdims=True))
+        slots.append(jnp.sum(cut * (at - opening + tag), axis=0, keepdims=True))
+        first = first + counts[i]
     place = jnp.concatenate(places, axis=1).astype(jnp.int32)
-    member = place // pair
-    slot = place - member * pair
-    code = (block + 1 + jnp.where(slot >= CAP, 128, 0)).astype(F32)
-    owns = (iota((members, count), 0) == member).astype(F32)
-    at = iota((pair, count), 0) == slot
+    slot = jnp.concatenate(slots, axis=1).astype(jnp.int32)
+    tile_order = slot // pair
+    slot = slot - tile_order * pair
+    copies[1].wait()
+    code = (block_ref[...] + 1 + 128 * (tile_order % 2)).astype(F32)
     codes = lax.dot_general(
-        owns.astype(BF16),
-        jnp.where(at, code, 0.0).astype(BF16),
+        one(iota((members, count), 0) == tile_order // 2),
+        jnp.where(iota((pair, count), 0) == slot, code, 0.0).astype(BF16),
         (((1,), (1,)), ((), ())),
         preferred_element_type=F32,
     ).astype(BF16)
     out_ref[:, pair:, :] = jnp.broadcast_to(codes[:, None, :], (members, depth - pair, 128))
-    slots = at.astype(F32).astype(BF16)
-    group = 4
-    for g in range(0, members, group):
-        pick = jnp.concatenate(
-            [slots * owns[m : m + 1].astype(BF16) for m in range(g, g + group)], axis=0
-        )
-        got = jnp.dot(pick, obs_ref[...], preferred_element_type=F32).astype(BF16)
-        out_ref[g : g + group, :pair, :] = got.reshape(group, pair, 128)
+    copies[2].wait()
+    for i in range(0, count, part):
+        pick = one(iota((part, count), 0) + i == place)
+        ordered[i : i + part, :] = jnp.dot(pick, obs_ref[...], preferred_element_type=F32)
+    ordered[count : count + pair, :] = jnp.zeros((pair, 128), F32)
+    sent.wait()
+    for m in range(members):
+        rows = ordered[pl.ds(starts_smem[0, m], pair), :]
+        out_ref[m, :pair, :] = rows.astype(BF16)
 
 
 def sum_kernel(got_ref, out_ref):
@@ -128,7 +171,7 @@
         for i in range(2):
             plane = jnp.where(row == 8 + i, gain_ref[first + i], plane)
             for c in range(4):
-                plane = jnp.where(row == c * 2 + i, decay_ref[c * 6 + first + i], plane)
+                plane = jnp.where(row == c * 2 + i, decay_ref[c, first + i], plane)
         rough = plane.astype(BF16)
         ref[at + 2] = rough
         ref[at + 3] = (plane - rough.astype(F32)).astype(BF16)
@@ -239,7 +282,7 @@
             if l < 2:
                 decays[at, :] = low_row[c * 2 + l : c * 2 + l + 1]
             elif l < 8:
-                decays[at, :] = jnp.full((1, cols), decay_ref[c * 6 + l - 2], F32)
+                decays[at, :] = jnp.full((1, cols), decay_ref[c, l - 2], F32)
             else:
                 decays[at, :] = high_row[c * 2 + l - 8 : c * 2 + l - 7]
         if l < 2:
@@ -255,7 +298,7 @@
                 body = low_ref[c * 2 + l].astype(F32)
             elif l < 8:
                 body = lam_ref[c, l - 2]
-                total = total + profile_ref[c * 6 + l - 2] * body
+                total = total + profile_ref[c, l - 2] * body
             else:
                 body = high_ref[c * 2 + l - 8].astype(F32)
             scaled[l, 0:16, :] = body
@@ -321,13 +364,13 @@
     def tracer(c, _):
         weight = 0.0
         for l in range(6):
-            weight = weight + profile_ref[c * 6 + l] * gain_ref[l]
+            weight = weight + profile_ref[c, l] * gain_ref[l]
         total = early_ref[c] + weight * field[0:16, :]
         for l in range(8):
             m = mixed_ref[c, l] + coef_ref[c, l] * field[...]
             value = advect(m, cxs[l], cys[l], ROWS)
             if 1 <= l < 7:
-                total = total + profile_ref[c * 6 + l - 1] * value[0:16]
+                total = total + profile_ref[c, l - 1] * value[0:16]
             later_ref[c, l] = decays[pl.ds(c * 10 + l + 1, 1), :] * value
         for q in range(groups):
             surface_ref[q, pl.ds(c * 16, 16), :] = total[:, q * 128 : (q + 1) * 128]
@@ -373,14 +416,14 @@
     anywhere = pl.BlockSpec(memory_space=pl.ANY)
     shape = jax.ShapeDtypeStruct
 
-    def call(body, outs, specs, scratch=(), flops=0, moved=0):
+    def call(body, outs, specs, scratch=(), flops=0, moved=0, limit=VMEM):
         return pl.pallas_call(
             body,
             out_shape=outs,
             in_specs=specs,
             out_specs=jax.tree.map(lambda _: vmem, outs),
-            scratch_shapes=[pltpu.VMEM(s, F32) for s in scratch],
-            compiler_params=pltpu.CompilerParams(vmem_limit_bytes=VMEM),
+            scratch_shapes=[pltpu.VMEM(s, F32) if isinstance(s, tuple) else s for s in scratch],
+            compiler_params=pltpu.CompilerParams(vmem_limit_bytes=limit),
             cost_estimate=pl.CostEstimate(flops=flops, bytes_accessed=moved, transcendentals=0),
         )
 
@@ -391,15 +434,24 @@
             (lax.axis_index(LEV) == lev_count - 1).astype(jnp.int32),
         ]
     )
-    decay = jnp.exp(-loss_rate).reshape(-1)
-    weights = profile.reshape(-1)
+    decay = jnp.exp(-loss_rate)
 
     packed = call(
         pack_kernel,
         shape((members, 2 * CAP + 16, 128), BF16),
-        [smem] + [vmem] * 3,
+        [smem] + [anywhere] * 3,
+        scratch=[
+            pltpu.VMEM((1, obs_values.shape[0]), jnp.int32),
+            pltpu.VMEM((1, obs_values.shape[0]), jnp.int32),
+            pltpu.VMEM(obs_values.shape, BF16),
+            (obs_values.shape[0] + 2 * CAP, 128),
+            pltpu.VMEM((8, 128), jnp.int32),
+            pltpu.SMEM((8, 128), jnp.int32),
+            pltpu.SemaphoreType.DMA((4,)),
+        ],
         flops=1 << 30,
         moved=2 << 20,
+        limit=MOST,
     )(where, obs_tile.reshape(1, -1), obs_block.reshape(1, -1), obs_values)
     got = lax.all_to_all(packed, LEV + ("y",), 0, 0, tiled=True)
 
@@ -438,7 +490,7 @@
         where,
         decay,
         kernel,
-        weights,
+        profile,
         lam_in,
         kz_face,
         courant_x,
@@ -476,7 +528,7 @@
         [smem] * 2 + [vmem] * 7,
         scratch=[(ROWS * cols // 128, 128), (ROWS, cols)],
         moved=8 << 20,
-    )(kernel, weights, cxs, cys, mixed, coef, early, decays, parts)
+    )(kernel, profile, cxs, cys, mixed, coef, early, decays, parts)
     shares = lax.all_to_all(surface, LEV, 0, 0, tiled=True)
     lam_out = call(
         second_kernel, shape(lam_in.shape, F32), [vmem] * 4, moved=6 << 20

time: 104 us -> 99.9 us (0.961)
  local copies, waits for them, and re-layouts: 8.55 us -> 6.66 us
  waiting for transfers between devices: 11.6 us -> 10.3 us
  Pallas kernels: 20.7 us -> 19.5 us
    all_to_all x1, waiting for transfers between devices: 10.6 us -> 9.33 us  [on_device(): got = lax.all_to_all(packed, LEV + ('y',), 0, 0, tiled=True)]
    unnamed x34 -> x32, local copies, waits for them, and re-layouts: 7.68 us -> 6.64 us
  transfers between devices with their start and end apart: 10 -> 10, of which waited for: 2 -> 2; matrix products, arithmetic and copies ran while one was open for 1% -> 0% of each run, Pallas kernels for 12% -> 11%
where the time goes in v3:
time: 99.9 us; the launch traced here: 99.1 us
  starting transfers between devices  47.2 us (47%)
  Pallas kernels  19.5 us (20%)
  blocking collectives  13.2 us (13%)
  waiting for transfers between devices  10.3 us (10%)
  local copies, waits for them, and re-layouts  6.66 us (7%)
  other arithmetic  1.23 us (1%)
    ppermute x2, starting transfers between devices, along_z(): return lax.ppermute(value, LEV + ('z',), perm)  14.4 us
    all_gather x1, blocking collectives, on_device(): lax.all_gather(jnp.concatenate([part, part_after, part_prior]), LEV, axis=0)  13.2 us
    all_to_all x1, starting transfers between devices, on_device(): got = lax.all_to_all(packed, LEV + ('y',), 0, 0, tiled=True)  9.35 us
    all_to_all x1, waiting for transfers between devices, on_device(): got = lax.all_to_all(packed, LEV + ('y',), 0, 0, tiled=True)  9.33 us
    unnamed x32, local copies, waits for them, and re-layouts  6.64 us
    ppermute x1, starting transfers between devices, on_device(): part_prior = chain(TILE, tile_count, 1)(part[-edge:])  6.03 us
    ppermute x1, starting transfers between devices, on_device(): prior = chain(TILE, tile_count, 1)(last_rows)  5.23 us
    pallas_call x1, Pallas kernels, on_device(): call(first_kernel, (shape((tracers, 8, ROWS, cols), F32), shape((lev_coun...  4.43 us
  transfers between devices with their start and end apart: 10, of which 2 were waited for; matrix products, arithmetic and copies ran while one was open for 0% of the time, Pallas kernels for 11%

profile of v3, /device:TPU:24, one launch (start us, length us, event | category | flops | bytes accessed | tf_op | source)
XLA Modules:
  0.0 99.1 jit_solution(5723526657880375869)
XLA Ops:
  1.2 4.1 %shard_map.113.after_ref = bf16[32,144,128]{2,1,0:T(8,128)(2,1)} custom-call(s32[3]{0:T(128)} %pad_add_fusion.where_ref, s32[1,1024]{1,0:T(1,128)} %bitcast.13, s32[1,1024]{1,0:T(1,128)} %bitcast.14, bf16[1024,128]{1,0:T(8,128)(2,1)} %obs_hbm.1), custom_call_target="tpu_custom_call" | custom-call | flops 1073741824 | bytes 2097152 | tf_op jit(solution)/shard_map/pallas_call | solution.py:439
  5.4 9.3 %all-to-all-start = ((bf16[32,144,128]{2,1,0:T(8,128)(2,1)}), bf16[32,144,128]{2,1,0:T(8,128)(2,1)S(1)}, u32[]{:S(2)}, u32[]{:S(2)}) async-start(bf16[32,144,128]{2,1,0:T(8,128)(2,1)} %shard_map.113.after_ref), calls=%async_computation | async-start | bytes 2359296 | tf_op jit(solution)/shard_map/all_to_all | solution.py:456
  14.8 1.3 %copy-done.1 = bf16[32,144,128]{2,1,0:T(8,128)(2,1)S(1)} copy-done((bf16[32,144,128]{2,1,0:T(8,128)(2,1)S(1)}, bf16[32,144,128]{2,1,0:T(8,128)(2,1)}, u32[]{:S(2)}) %copy-start.1) | copy-done | bytes 1179672
  16.1 1.0 %copy-done.4 = f32[6,16,1024]{2,1,0:T(8,128)S(1)} copy-done((f32[6,16,1024]{2,1,0:T(8,128)S(1)}, f32[6,16,1024]{2,1,0:T(8,128)}, u32[]{:S(2)}) %copy-start.4) | copy-done | bytes 393240
  17.1 1.6 %shard_map.114 = (bf16[14,16,1024]{2,1,0:T(8,128)(2,1)}, bf16[13,16,1024]{2,1,0:T(8,128)(2,1)}) custom-call(s32[3]{0:T(128)S(1)} %copy-done.13, f32[4,6]{1,0:T(4,128)S(1)} %negate_exponential_fusion.decay_ref, f32[6]{0:T(128)S(1)} %copy-done.14, f32[4,6,16,1024]{3,2,1,0:T(8,128)S(1)} %copy-done, f32[6,16,1024]{2,1,0:T(8,128)S(1)} %copy-done.2, ...), custom_call_target="tpu_custom_call" | custom-call | bytes 4194304 | tf_op jit(solution)/shard_map/pallas_call | solution.py:458
  18.7 2.8 %collective-permute-start = (bf16[14,16,1024]{2,1,0:T(8,128)(2,1)}, bf16[14,16,1024]{2,1,0:T(8,128)(2,1)}, u32[]{:S(2)}, u32[]{:S(2)}) collective-permute-start(bf16[14,16,1024]{2,1,0:T(8,128)(2,1)} %get-tuple-element.15), channel_id=1, source_target_pairs={{0,64},{64,128},{128,192},{192,256},{256,320},{320,384},{384,448},... | collective-permute-start | bytes 1376264 | tf_op jit(solution)/shard_map/ppermute | solution.py:464
  21.5 1.3 %collective-permute-start.1 = (bf16[13,16,1024]{2,1,0:T(8,128)(2,1)}, bf16[13,16,1024]{2,1,0:T(8,128)(2,1)}, u32[]{:S(2)}, u32[]{:S(2)}) collective-permute-start(bf16[13,16,1024]{2,1,0:T(8,128)(2,1)} %get-tuple-element.16), channel_id=1, source_target_pairs={{64,0},{128,64},{192,128},{256,192},{320,256},{384,320},{448,384},... | collective-permute-start | bytes 1277960 | tf_op jit(solution)/shard_map/ppermute | solution.py:465
  22.8 9.3 %all-to-all-done.got_ref = bf16[32,144,128]{2,1,0:T(8,128)(2,1)S(1)} async-done(((bf16[32,144,128]{2,1,0:T(8,128)(2,1)}), bf16[32,144,128]{2,1,0:T(8,128)(2,1)S(1)}, u32[]{:S(2)}, u32[]{:S(2)}) %all-to-all-start) | async-done | bytes 1179680 | tf_op jit(solution)/shard_map/all_to_all | solution.py:456
  32.8 13.7 %collective-permute-start.5 = (f32[128,128]{1,0:T(8,128)S(1)}, f32[128,128]{1,0:T(8,128)S(1)}, u32[]{:S(2)}, u32[]{:S(2)}) collective-permute-start(f32[128,128]{1,0:T(8,128)S(1)} %get-tuple-element.28), channel_id=1, source_target_pairs={{0,32},{4,36},{8,40},{12,44},{16,48},{20,52},{24,56},{28,60},{32,0... | collective-permute-start | bytes 196616 | tf_op jit(solution)/shard_map/ppermute | solution.py:514
  47.3 1.6 %shard_map.115 = (bf16[144,1024]{1,0:T(8,128)(2,1)S(1)}, bf16[144,1024]{1,0:T(8,128)(2,1)S(1)}) custom-call(s32[3]{0:T(128)S(1)} %copy-done.13, f32[4,6,16,1024]{3,2,1,0:T(8,128)S(1)} %copy-done, f32[6,16,1024]{2,1,0:T(8,128)S(1)} %copy-done.2, f32[6,16,1024]{2,1,0:T(8,128)S(1)} %copy-done.3, f32[6,16,1024]{2,1,0:T(8,128)S(1)} %copy-done.5, ...), custom_call_target="tpu_custom_call" | custom-call | bytes 5242880 | tf_op jit(solution)/shard_map/pallas_call | solution.py:466
  48.9 2.7 %collective-permute-start.2 = (bf16[144,1024]{1,0:T(8,128)(2,1)S(1)}, bf16[144,1024]{1,0:T(8,128)(2,1)S(1)}, u32[]{:S(2)}, u32[]{:S(2)}) collective-permute-start(bf16[144,1024]{1,0:T(8,128)(2,1)S(1)} %get-tuple-element.17), channel_id=1, source_target_pairs={{1,0},{2,1},{3,2},{4,3},{5,4},{6,5},{7,6},{8,7},{9,8},{10,9},{11,1... | collective-permute-start | bytes 884744 | tf_op jit(solution)/shard_map/ppermute | solution.py:473
  51.6 5.2 %collective-permute-start.3 = (bf16[144,1024]{1,0:T(8,128)(2,1)S(1)}, bf16[144,1024]{1,0:T(8,128)(2,1)S(1)}, u32[]{:S(2)}, u32[]{:S(2)}) collective-permute-start(bf16[144,1024]{1,0:T(8,128)(2,1)S(1)} %get-tuple-element.18), channel_id=1, source_target_pairs={{0,1},{1,2},{2,3},{3,4},{4,5},{5,6},{6,7},{7,8},{8,9},{9,10},{10,1... | collective-permute-start | bytes 884744 | tf_op jit(solution)/shard_map/ppermute | solution.py:474
  56.9 1.9 %collective-permute-start.6 = (f32[16,128]{1,0:T(8,128)S(1)}, f32[16,128]{1,0:T(8,128)S(1)}, u32[]{:S(2)}, u32[]{:S(2)}) collective-permute-start(f32[16,128]{1,0:T(8,128)S(1)} %get-tuple-element.30), channel_id=1, source_target_pairs={{1,0},{2,1},{3,2},{4,3},{5,4},{6,5},{7,6},{8,7},{9,8},{10,9},{11,1... | collective-permute-start | bytes 24584 | tf_op jit(solution)/shard_map/ppermute | solution.py:518
  58.8 6.0 %collective-permute-start.7 = (f32[16,128]{1,0:T(8,128)S(1)}, f32[16,128]{1,0:T(8,128)S(1)}, u32[]{:S(2)}, u32[]{:S(2)}) collective-permute-start(f32[16,128]{1,0:T(8,128)S(1)} %get-tuple-element.31), channel_id=1, source_target_pairs={{0,1},{1,2},{2,3},{3,4},{4,5},{5,6},{6,7},{7,8},{8,9},{9,10},{10,1... | collective-permute-start | bytes 24584 | tf_op jit(solution)/shard_map/ppermute | solution.py:519
  64.9 4.0 %shard_map.116 = (f32[9,24,1024]{2,1,0:T(8,128)S(1)}, f32[8,24,1024]{2,1,0:T(8,128)S(1)}, f32[8,24,1024]{2,1,0:T(8,128)S(1)}, f32[4,8,24,1024]{3,2,1,0:T(8,128)S...) custom-call(s32[3]{0:T(128)S(1)} %copy-done.13, ...), custom_call_target="tpu_custom_call" | custom-call | bytes 12582912 | tf_op jit(solution)/shard_map/pallas_call | solution.py:475
  69.0 0.9 copy-done.10
  69.9 13.2 %all-gather = f32[1280,128]{1,0:T(8,128)S(1)} all-gather(f32[160,128]{1,0:T(8,128)S(1)} %pad_maximum_fusion), channel_id=2, replica_groups=mesh['x'=4,'core'=2,'z'=16,'y'=4] {'x','core'}, dimensions={0}, use_global_device_ids=true | all-gather | bytes 737280 | tf_op jit(solution)/shard_map/all_gather | solution.py:520
  83.1 4.4 %shard_map.118 = (f32[4,8,24,1024]{3,2,1,0:T(8,128)S(1)}, f32[8,64,128]{2,1,0:T(8,128)}) custom-call(f32[6]{0:T(128)S(1)} %copy-done.14, f32[4,6]{1,0:T(4,128)S(1)} %copy-done.12, f32[8,24,1024]{2,1,0:T(8,128)S(1)} %get-tuple-element.20.cxs, f32[8,24,1024]{2,1,0:T(8,128)S(1)} %get-tuple-element.21.cys, f32[4,8,24,1024]{3,2,1,0:T(8,128)S(1)} %get-tuple-element.22.mixed_ref, ...), custom_call_target="tpu_custom_call" | custom-call | bytes 8388608 | tf_op jit(solution)/shard_map/pallas_call | solution.py:522
  87.6 3.4 %all-to-all-start.1 = ((f32[8,64,128]{2,1,0:T(8,128)}), f32[8,64,128]{2,1,0:T(8,128)S(1)}, u32[]{:S(2)}, u32[]{:S(2)}) async-start(f32[8,64,128]{2,1,0:T(8,128)} %get-tuple-element.27), calls=%async_computation.1 | async-start | bytes 524288 | tf_op jit(solution)/shard_map/all_to_all | solution.py:532
  91.0 1.1 %copy-done.7 = f32[8,24,1024]{2,1,0:T(8,128)S(1)} copy-done((f32[8,24,1024]{2,1,0:T(8,128)S(1)}, f32[8,24,1024]{2,1,0:T(8,128)}, u32[]{:S(2)}) %copy-start.7) | copy-done | bytes 786456
  92.1 1.1 %copy-done.9 = f32[8,24,1024]{2,1,0:T(8,128)S(1)} copy-done((f32[8,24,1024]{2,1,0:T(8,128)S(1)}, f32[8,24,1024]{2,1,0:T(8,128)}, u32[]{:S(2)}) %copy-start.9) | copy-done | bytes 786456
  93.3 1.2 %copy-done.11 = f32[9,24,1024]{2,1,0:T(8,128)S(1)} copy-done((f32[9,24,1024]{2,1,0:T(8,128)S(1)}, f32[9,24,1024]{2,1,0:T(8,128)}, u32[]{:S(2)}) %copy-start.11) | copy-done | bytes 884760
  94.4 3.0 %shard_map.119 = f32[4,6,16,1024]{3,2,1,0:T(8,128)} custom-call(f32[9,24,1024]{2,1,0:T(8,128)S(1)} %copy-done.11, f32[8,24,1024]{2,1,0:T(8,128)S(1)} %copy-done.7, f32[8,24,1024]{2,1,0:T(8,128)S(1)} %copy-done.9, f32[4,8,24,1024]{3,2,1,0:T(8,128)S(1)} %get-tuple-element.26.later_ref), custom_call_target="tpu_custom_call" | custom-call | bytes 6291456 | tf_op jit(solution)/shard_map/pallas_call | solution.py:533
  97.5 1.0 all-to-all-done.1
  (43 shorter events, 2.7 us)
Async XLA Ops:
  1.2 13.5 %copy-start.15 = (f32[4,6]{1,0:T(4,128)S(1)}, f32[4,6]{1,0:T(4,128)}, u32[]{:S(2)}) copy-start(f32[4,6]{1,0:T(4,128)} %param.14) | copy-start | bytes 292
  5.3 9.4 %copy-start = (f32[4,6,16,1024]{3,2,1,0:T(8,128)S(1)}, f32[4,6,16,1024]{3,2,1,0:T(8,128)}, u32[]{:S(2)}) copy-start(f32[4,6,16,1024]{3,2,1,0:T(8,128)} %lam_ref.5) | copy-start | bytes 4718596
  5.3 9.4 %copy-start.2 = (f32[6,16,1024]{2,1,0:T(8,128)S(1)}, f32[6,16,1024]{2,1,0:T(8,128)}, u32[]{:S(2)}) copy-start(f32[6,16,1024]{2,1,0:T(8,128)} %kz_ref.5) | copy-start | bytes 1179652
  5.3 9.4 %copy-start.3 = (f32[6,16,1024]{2,1,0:T(8,128)S(1)}, f32[6,16,1024]{2,1,0:T(8,128)}, u32[]{:S(2)}) copy-start(f32[6,16,1024]{2,1,0:T(8,128)} %cx_ref.5) | copy-start | bytes 1179652
  5.4 9.4 %copy-start.13 = (s32[3]{0:T(128)S(1)}, s32[3]{0:T(128)}, u32[]{:S(2)}) copy-start(s32[3]{0:T(128)} %pad_add_fusion.where_ref) | copy-start | bytes 40
  5.4 9.4 %copy-start.14 = (f32[6]{0:T(128)S(1)}, f32[6]{0:T(128)}, u32[]{:S(2)}) copy-start(f32[6]{0:T(128)} %gain_ref.5) | copy-start | bytes 76
  5.4 26.7 %all-to-all-start = ((bf16[32,144,128]{2,1,0:T(8,128)(2,1)}), bf16[32,144,128]{2,1,0:T(8,128)(2,1)S(1)}, u32[]{:S(2)}, u32[]{:S(2)}) async-start(bf16[32,144,128]{2,1,0:T(8,128)(2,1)} %shard_map.113.after_ref), calls=%async_computation | async-start | bytes 2359296 | tf_op jit(solution)/shard_map/all_to_all | solution.py:456
  14.8 1.3 %copy-start.1 = (bf16[32,144,128]{2,1,0:T(8,128)(2,1)S(1)}, bf16[32,144,128]{2,1,0:T(8,128)(2,1)}, u32[]{:S(2)}) copy-start(bf16[32,144,128]{2,1,0:T(8,128)(2,1)} %shard_map.113.after_ref) | copy-start | bytes 3538948
  18.7 28.6 %collective-permute-start = (bf16[14,16,1024]{2,1,0:T(8,128)(2,1)}, bf16[14,16,1024]{2,1,0:T(8,128)(2,1)}, u32[]{:S(2)}, u32[]{:S(2)}) collective-permute-start(bf16[14,16,1024]{2,1,0:T(8,128)(2,1)} %get-tuple-element.15), channel_id=1, source_target_pairs={{0,64},{64,128},{128,192},{192,256},{256,320},{320,384},{384,448},... | collective-permute-start | bytes 1376264 | tf_op jit(solution)/shard_map/ppermute | solution.py:464
  21.5 25.8 %collective-permute-start.1 = (bf16[13,16,1024]{2,1,0:T(8,128)(2,1)}, bf16[13,16,1024]{2,1,0:T(8,128)(2,1)}, u32[]{:S(2)}, u32[]{:S(2)}) collective-permute-start(bf16[13,16,1024]{2,1,0:T(8,128)(2,1)} %get-tuple-element.16), channel_id=1, source_target_pairs={{64,0},{128,64},{192,128},{256,192},{320,256},{384,320},{448,384},... | collective-permute-start | bytes 1277960 | tf_op jit(solution)/shard_map/ppermute | solution.py:465
  32.1 15.2 %copy-start.5 = (f32[6,16,1024]{2,1,0:T(8,128)S(1)}, f32[6,16,1024]{2,1,0:T(8,128)}, u32[]{:S(2)}) copy-start(f32[6,16,1024]{2,1,0:T(8,128)} %cy_ref.5) | copy-start | bytes 1179652
  32.8 24.0 %collective-permute-start.5 = (f32[128,128]{1,0:T(8,128)S(1)}, f32[128,128]{1,0:T(8,128)S(1)}, u32[]{:S(2)}, u32[]{:S(2)}) collective-permute-start(f32[128,128]{1,0:T(8,128)S(1)} %get-tuple-element.28), channel_id=1, source_target_pairs={{0,32},{4,36},{8,40},{12,44},{16,48},{20,52},{24,56},{28,60},{32,0... | collective-permute-start | bytes 196616 | tf_op jit(solution)/shard_map/ppermute | solution.py:514
  46.6 18.3 %copy-start.12 = (f32[4,6]{1,0:T(4,128)S(1)}, f32[4,6]{1,0:T(4,128)}, u32[]{:S(2)}) copy-start(f32[4,6]{1,0:T(4,128)} %profile_ref.3) | copy-start | bytes 292
  46.6 10.3 %collective-permute-start.4 = (f32[128,128]{1,0:T(8,128)S(1)}, f32[128,128]{1,0:T(8,128)S(1)}, u32[]{:S(2)}, u32[]{:S(2)}) collective-permute-start(f32[128,128]{1,0:T(8,128)S(1)} %get-tuple-element.29), channel_id=1, source_target_pairs={{0,0},{4,4},{8,8},{12,12},{16,16},{20,20},{24,24},{28,28},{32,32},... | collective-permute-start | bytes 196616 | tf_op jit(solution)/shard_map/ppermute | solution.py:514
  48.9 16.0 %collective-permute-start.2 = (bf16[144,1024]{1,0:T(8,128)(2,1)S(1)}, bf16[144,1024]{1,0:T(8,128)(2,1)S(1)}, u32[]{:S(2)}, u32[]{:S(2)}) collective-permute-start(bf16[144,1024]{1,0:T(8,128)(2,1)S(1)} %get-tuple-element.17), channel_id=1, source_target_pairs={{1,0},{2,1},{3,2},{4,3},{5,4},{6,5},{7,6},{8,7},{9,8},{10,9},{11,1... | collective-permute-start | bytes 884744 | tf_op jit(solution)/shard_map/ppermute | solution.py:473
  51.6 13.3 %collective-permute-start.3 = (bf16[144,1024]{1,0:T(8,128)(2,1)S(1)}, bf16[144,1024]{1,0:T(8,128)(2,1)S(1)}, u32[]{:S(2)}, u32[]{:S(2)}) collective-permute-start(bf16[144,1024]{1,0:T(8,128)(2,1)S(1)} %get-tuple-element.18), channel_id=1, source_target_pairs={{0,1},{1,2},{2,3},{3,4},{4,5},{5,6},{6,7},{7,8},{8,9},{9,10},{10,1... | collective-permute-start | bytes 884744 | tf_op jit(solution)/shard_map/ppermute | solution.py:474
  56.9 13.0 %collective-permute-start.6 = (f32[16,128]{1,0:T(8,128)S(1)}, f32[16,128]{1,0:T(8,128)S(1)}, u32[]{:S(2)}, u32[]{:S(2)}) collective-permute-start(f32[16,128]{1,0:T(8,128)S(1)} %get-tuple-element.30), channel_id=1, source_target_pairs={{1,0},{2,1},{3,2},{4,3},{5,4},{6,5},{7,6},{8,7},{9,8},{10,9},{11,1... | collective-permute-start | bytes 24584 | tf_op jit(solution)/shard_map/ppermute | solution.py:518
  58.8 11.0 %collective-permute-start.7 = (f32[16,128]{1,0:T(8,128)S(1)}, f32[16,128]{1,0:T(8,128)S(1)}, u32[]{:S(2)}, u32[]{:S(2)}) collective-permute-start(f32[16,128]{1,0:T(8,128)S(1)} %get-tuple-element.31), channel_id=1, source_target_pairs={{0,1},{1,2},{2,3},{3,4},{4,5},{5,6},{6,7},{7,8},{8,9},{9,10},{10,1... | collective-permute-start | bytes 24584 | tf_op jit(solution)/shard_map/ppermute | solution.py:519
  69.9 17.7 %copy-start.6 = (f32[8,24,1024]{2,1,0:T(8,128)}, f32[8,24,1024]{2,1,0:T(8,128)S(1)}, u32[]{:S(2)}) copy-start(f32[8,24,1024]{2,1,0:T(8,128)S(1)} %get-tuple-element.20.cxs) | copy-start | bytes 2359300
  69.9 17.7 %copy-start.8 = (f32[8,24,1024]{2,1,0:T(8,128)}, f32[8,24,1024]{2,1,0:T(8,128)S(1)}, u32[]{:S(2)}) copy-start(f32[8,24,1024]{2,1,0:T(8,128)S(1)} %get-tuple-element.21.cys) | copy-start | bytes 2359300
  87.6 10.9 %all-to-all-start.1 = ((f32[8,64,128]{2,1,0:T(8,128)}), f32[8,64,128]{2,1,0:T(8,128)S(1)}, u32[]{:S(2)}, u32[]{:S(2)}) async-start(f32[8,64,128]{2,1,0:T(8,128)} %get-tuple-element.27), calls=%async_computation.1 | async-start | bytes 524288 | tf_op jit(solution)/shard_map/all_to_all | solution.py:532
  91.0 1.1 %copy-start.7 = (f32[8,24,1024]{2,1,0:T(8,128)S(1)}, f32[8,24,1024]{2,1,0:T(8,128)}, u32[]{:S(2)}) copy-start(f32[8,24,1024]{2,1,0:T(8,128)} %copy-done.6) | copy-start | bytes 2359300
  92.1 1.1 %copy-start.9 = (f32[8,24,1024]{2,1,0:T(8,128)S(1)}, f32[8,24,1024]{2,1,0:T(8,128)}, u32[]{:S(2)}) copy-start(f32[8,24,1024]{2,1,0:T(8,128)} %copy-done.8) | copy-start | bytes 2359300
  93.3 1.2 %copy-start.11 = (f32[9,24,1024]{2,1,0:T(8,128)S(1)}, f32[9,24,1024]{2,1,0:T(8,128)}, u32[]{:S(2)}) copy-start(f32[9,24,1024]{2,1,0:T(8,128)} %copy-done.10) | copy-start | bytes 2654212
  (2 other events, 1.9 us)

commit v4 on v3

--- a/solution.py
+++ b/solution.py
@@ -10,7 +10,7 @@
 from jax.sharding import PartitionSpec as P
 
 SPLIT = (4, 2, 16, 4)
-SHIFTS = ((0, 8), (4, 12), (1, 9), (7, 15), (2, 10), (6, 14), (3, 11), (5, 13))
+SHIFTS = ((0, 8), (1, 15), (2, 14), (7, 9), (3, 13), (6, 10), (4, 12), (5, 11))
 CAP = 64
 LEV = ("x", "core")
 TILE = ("z", "y")
@@ -47,7 +47,6 @@
 
 
 def pack_kernel(
-    where_ref,
     tile_hbm,
     block_hbm,
     obs_hbm,
@@ -72,8 +71,9 @@
     ]
     for copy in copies:
         copy.start()
-    order = rank_of(iota((tiles, 1), 0), where_ref[0], size_z, size_y)
-    order_row = rank_of(iota((1, tiles), 1), where_ref[0], size_z, size_y)
+    here = lax.axis_index("z")
+    order = rank_of(iota((tiles, 1), 0), here, size_z, size_y)
+    order_row = rank_of(iota((1, tiles), 1), here, size_z, size_y)
     before = (iota((part, part), 0) < iota((part, part), 1)).astype(BF16)
     copies[0].wait()
     hot = (iota((tiles, count), 0) == tile_ref[...]).astype(F32)
@@ -140,11 +140,11 @@
 
 def masks(where_ref):
     def kz(value, level):
-        return jnp.where(where_ref[2] == 1, 0.0, value) if level == 5 else value
+        return jnp.where(where_ref[1] == 1, 0.0, value) if level == 5 else value
 
     def cx(value, first):
         last = iota(value.shape, 0) + first == 15
-        return jnp.where(last & (where_ref[1] == 1), 0.0, value)
+        return jnp.where(last & (where_ref[0] == 1), 0.0, value)
 
     def cy(value):
         return jnp.where(iota(value.shape, 1) == value.shape[1] - 1, 0.0, value)
@@ -429,7 +429,6 @@
 
     where = jnp.stack(
         [
-            lax.axis_index("z"),
             (lax.axis_index(TILE) == tile_count - 1).astype(jnp.int32),
             (lax.axis_index(LEV) == lev_count - 1).astype(jnp.int32),
         ]
@@ -439,7 +438,7 @@
     packed = call(
         pack_kernel,
         shape((members, 2 * CAP + 16, 128), BF16),
-        [smem] + [anywhere] * 3,
+        [anywhere] * 3,
         scratch=[
             pltpu.VMEM((1, obs_values.shape[0]), jnp.int32),
             pltpu.VMEM((1, obs_values.shape[0]), jnp.int32),
@@ -452,7 +451,7 @@
         flops=1 << 30,
         moved=2 << 20,
         limit=MOST,
-    )(where, obs_tile.reshape(1, -1), obs_block.reshape(1, -1), obs_values)
+    )(obs_tile.reshape(1, -1), obs_block.reshape(1, -1), obs_values)
     got = lax.all_to_all(packed, LEV + ("y",), 0, 0, tiled=True)
 
     up, down = call(

time: 99.9 us -> 101 us (1.011)
  local copies, waits for them, and re-layouts: 6.66 us -> 7.87 us
    unnamed x32 -> x30, local copies, waits for them, and re-layouts: 6.64 us -> 7.86 us
where the time goes in v4:
time: 101 us; the launch traced here: 99.9 us
  starting transfers between devices  47.2 us (47%)
  Pallas kernels  18.7 us (19%)
  blocking collectives  13.8 us (14%)
  waiting for transfers between devices  10.6 us (10%)
  local copies, waits for them, and re-layouts  7.87 us (8%)
    ppermute x2, starting transfers between devices, along_z(): return lax.ppermute(value, LEV + ('z',), perm)  14.4 us
    all_gather x1, blocking collectives, on_device(): lax.all_gather(jnp.concatenate([part, part_after, part_prior]), LEV, axis=0)  13.8 us
    all_to_all x1, starting transfers between devices, on_device(): got = lax.all_to_all(packed, LEV + ('y',), 0, 0, tiled=True)  9.35 us
    all_to_all x1, waiting for transfers between devices, on_device(): got = lax.all_to_all(packed, LEV + ('y',), 0, 0, tiled=True)  9.24 us
    unnamed x30, local copies, waits for them, and re-layouts  7.86 us
    ppermute x1, starting transfers between devices, on_device(): part_prior = chain(TILE, tile_count, 1)(part[-edge:])  6.03 us
    ppermute x1, starting transfers between devices, on_device(): prior = chain(TILE, tile_count, 1)(last_rows)  5.23 us
    pallas_call x1, Pallas kernels, on_device(): call(first_kernel, (shape((tracers, 8, ROWS, cols), F32), shape((lev_coun...  4.43 us
  transfers between devices with their start and end apart: 10, of which 2 were waited for; matrix products, arithmetic and copies ran while one was open for 0% of the time, Pallas kernels for 11%

profile of v4, /device:TPU:24, one launch (start us, length us, event | category | flops | bytes accessed | tf_op | source)
XLA Modules:
  0.0 99.9 jit_solution(16107519295532081358)
XLA Ops:
  0.6 3.3 %shard_map.113.after_ref = bf16[32,144,128]{2,1,0:T(8,128)(2,1)} custom-call(s32[1,1024]{1,0:T(1,128)} %bitcast.12, s32[1,1024]{1,0:T(1,128)} %bitcast.13, bf16[1024,128]{1,0:T(8,128)(2,1)} %obs_hbm.1), custom_call_target="tpu_custom_call" | custom-call | flops 1073741824 | bytes 2097152 | tf_op jit(solution)/shard_map/pallas_call | solution.py:438
  4.0 9.3 %all-to-all-start = ((bf16[32,144,128]{2,1,0:T(8,128)(2,1)}), bf16[32,144,128]{2,1,0:T(8,128)(2,1)S(1)}, u32[]{:S(2)}, u32[]{:S(2)}) async-start(bf16[32,144,128]{2,1,0:T(8,128)(2,1)} %shard_map.113.after_ref), calls=%async_computation | async-start | bytes 2359296 | tf_op jit(solution)/shard_map/all_to_all | solution.py:455
  13.5 1.3 %copy-done.1 = bf16[32,144,128]{2,1,0:T(8,128)(2,1)S(1)} copy-done((bf16[32,144,128]{2,1,0:T(8,128)(2,1)S(1)}, bf16[32,144,128]{2,1,0:T(8,128)(2,1)}, u32[]{:S(2)}) %copy-start.1) | copy-done | bytes 1179672
  14.7 1.0 copy-done.4
  15.7 1.6 %shard_map.114 = (bf16[14,16,1024]{2,1,0:T(8,128)(2,1)}, bf16[13,16,1024]{2,1,0:T(8,128)(2,1)}) custom-call(s32[2]{0:T(128)S(1)} %add_convert_fusion.where_ref, f32[4,6]{1,0:T(4,128)S(1)} %negate_exponential_fusion.decay_ref, f32[6]{0:T(128)S(1)} %copy-done.13, f32[4,6,16,1024]{3,2,1,0:T(8,128)S(1)} %copy-done, f32[6,16,1024]{2,1,0:T(8,128)S(1)} %copy-done.2, ...), custom_call_target="tpu_custom_call" | custom-call | bytes 4194304 | tf_op jit(solution)/shard_map/pallas_call | solution.py:457
  17.4 2.8 %collective-permute-start = (bf16[14,16,1024]{2,1,0:T(8,128)(2,1)}, bf16[14,16,1024]{2,1,0:T(8,128)(2,1)}, u32[]{:S(2)}, u32[]{:S(2)}) collective-permute-start(bf16[14,16,1024]{2,1,0:T(8,128)(2,1)} %get-tuple-element.15), channel_id=1, source_target_pairs={{0,64},{64,128},{128,192},{192,256},{256,320},{320,384},{384,448},... | collective-permute-start | bytes 1376264 | tf_op jit(solution)/shard_map/ppermute | solution.py:463
  20.2 1.3 %collective-permute-start.1 = (bf16[13,16,1024]{2,1,0:T(8,128)(2,1)}, bf16[13,16,1024]{2,1,0:T(8,128)(2,1)}, u32[]{:S(2)}, u32[]{:S(2)}) collective-permute-start(bf16[13,16,1024]{2,1,0:T(8,128)(2,1)} %get-tuple-element.16), channel_id=1, source_target_pairs={{64,0},{128,64},{192,128},{256,192},{320,256},{384,320},{448,384},... | collective-permute-start | bytes 1277960 | tf_op jit(solution)/shard_map/ppermute | solution.py:464
  21.5 9.2 %all-to-all-done.got_ref = bf16[32,144,128]{2,1,0:T(8,128)(2,1)S(1)} async-done(((bf16[32,144,128]{2,1,0:T(8,128)(2,1)}), bf16[32,144,128]{2,1,0:T(8,128)(2,1)S(1)}, u32[]{:S(2)}, u32[]{:S(2)}) %all-to-all-start) | async-done | bytes 1179680 | tf_op jit(solution)/shard_map/all_to_all | solution.py:455
  31.4 13.7 %collective-permute-start.5 = (f32[128,128]{1,0:T(8,128)S(1)}, f32[128,128]{1,0:T(8,128)S(1)}, u32[]{:S(2)}, u32[]{:S(2)}) collective-permute-start(f32[128,128]{1,0:T(8,128)S(1)} %get-tuple-element.28), channel_id=1, source_target_pairs={{0,32},{4,36},{8,40},{12,44},{16,48},{20,52},{24,56},{28,60},{32,0... | collective-permute-start | bytes 196616 | tf_op jit(solution)/shard_map/ppermute | solution.py:513
  45.9 1.6 %shard_map.115 = (bf16[144,1024]{1,0:T(8,128)(2,1)S(1)}, bf16[144,1024]{1,0:T(8,128)(2,1)S(1)}) custom-call(s32[2]{0:T(128)S(1)} %add_convert_fusion.where_ref, f32[4,6,16,1024]{3,2,1,0:T(8,128)S(1)} %copy-done, f32[6,16,1024]{2,1,0:T(8,128)S(1)} %copy-done.2, f32[6,16,1024]{2,1,0:T(8,128)S(1)} %copy-done.3, f32[6,16,1024]{2,1,0:T(8,128)S(1)} %copy-done.5, ...), custom_call_target="tpu_custom_call" | custom-call | bytes 5242880 | tf_op jit(solution)/shard_map/pallas_call | solution.py:465
  47.5 2.7 %collective-permute-start.2 = (bf16[144,1024]{1,0:T(8,128)(2,1)S(1)}, bf16[144,1024]{1,0:T(8,128)(2,1)S(1)}, u32[]{:S(2)}, u32[]{:S(2)}) collective-permute-start(bf16[144,1024]{1,0:T(8,128)(2,1)S(1)} %get-tuple-element.17), channel_id=1, source_target_pairs={{1,0},{2,1},{3,2},{4,3},{5,4},{6,5},{7,6},{8,7},{9,8},{10,9},{11,1... | collective-permute-start | bytes 884744 | tf_op jit(solution)/shard_map/ppermute | solution.py:472
  50.2 5.2 %collective-permute-start.3 = (bf16[144,1024]{1,0:T(8,128)(2,1)S(1)}, bf16[144,1024]{1,0:T(8,128)(2,1)S(1)}, u32[]{:S(2)}, u32[]{:S(2)}) collective-permute-start(bf16[144,1024]{1,0:T(8,128)(2,1)S(1)} %get-tuple-element.18), channel_id=1, source_target_pairs={{0,1},{1,2},{2,3},{3,4},{4,5},{5,6},{6,7},{7,8},{8,9},{9,10},{10,1... | collective-permute-start | bytes 884744 | tf_op jit(solution)/shard_map/ppermute | solution.py:473
  55.5 1.9 %collective-permute-start.6 = (f32[16,128]{1,0:T(8,128)S(1)}, f32[16,128]{1,0:T(8,128)S(1)}, u32[]{:S(2)}, u32[]{:S(2)}) collective-permute-start(f32[16,128]{1,0:T(8,128)S(1)} %get-tuple-element.30), channel_id=1, source_target_pairs={{1,0},{2,1},{3,2},{4,3},{5,4},{6,5},{7,6},{8,7},{9,8},{10,9},{11,1... | collective-permute-start | bytes 24584 | tf_op jit(solution)/shard_map/ppermute | solution.py:517
  57.5 6.0 %collective-permute-start.7 = (f32[16,128]{1,0:T(8,128)S(1)}, f32[16,128]{1,0:T(8,128)S(1)}, u32[]{:S(2)}, u32[]{:S(2)}) collective-permute-start(f32[16,128]{1,0:T(8,128)S(1)} %get-tuple-element.31), channel_id=1, source_target_pairs={{0,1},{1,2},{2,3},{3,4},{4,5},{5,6},{6,7},{7,8},{8,9},{9,10},{10,1... | collective-permute-start | bytes 24584 | tf_op jit(solution)/shard_map/ppermute | solution.py:518
  63.5 4.0 %shard_map.116 = (f32[9,24,1024]{2,1,0:T(8,128)S(1)}, f32[8,24,1024]{2,1,0:T(8,128)S(1)}, f32[8,24,1024]{2,1,0:T(8,128)S(1)}, f32[4,8,24,1024]{3,2,1,0:T(8,128)S...) custom-call(s32[2]{0:T(128)S(1)} %add_convert_fusion.where_ref, ...), custom_call_target="tpu_custom_call" | custom-call | bytes 12582912 | tf_op jit(solution)/shard_map/pallas_call | solution.py:474
  67.6 0.9 copy-done.10
  68.5 13.8 %all-gather = f32[1280,128]{1,0:T(8,128)S(1)} all-gather(f32[160,128]{1,0:T(8,128)S(1)} %pad_maximum_fusion), channel_id=2, replica_groups=mesh['x'=4,'core'=2,'z'=16,'y'=4] {'x','core'}, dimensions={0}, use_global_device_ids=true | all-gather | bytes 737280 | tf_op jit(solution)/shard_map/all_gather | solution.py:519
  82.4 4.4 %shard_map.118 = (f32[4,8,24,1024]{3,2,1,0:T(8,128)S(1)}, f32[8,64,128]{2,1,0:T(8,128)}) custom-call(f32[6]{0:T(128)S(1)} %copy-done.13, f32[4,6]{1,0:T(4,128)S(1)} %copy-done.12, f32[8,24,1024]{2,1,0:T(8,128)S(1)} %get-tuple-element.20.cxs, f32[8,24,1024]{2,1,0:T(8,128)S(1)} %get-tuple-element.21.cys, f32[4,8,24,1024]{3,2,1,0:T(8,128)S(1)} %get-tuple-element.22.mixed_ref, ...), custom_call_target="tpu_custom_call" | custom-call | bytes 8388608 | tf_op jit(solution)/shard_map/pallas_call | solution.py:521
  86.8 1.6 %copy-done.6 = f32[4,8,24,1024]{3,2,1,0:T(8,128)} copy-done((f32[4,8,24,1024]{3,2,1,0:T(8,128)}, f32[4,8,24,1024]{3,2,1,0:T(8,128)S(1)}, u32[]{:S(2)}) %copy-start.6) | copy-done | bytes 3145752
  88.4 3.4 %all-to-all-start.1 = ((f32[8,64,128]{2,1,0:T(8,128)}), f32[8,64,128]{2,1,0:T(8,128)S(1)}, u32[]{:S(2)}, u32[]{:S(2)}) async-start(f32[8,64,128]{2,1,0:T(8,128)} %get-tuple-element.27), calls=%async_computation.1 | async-start | bytes 524288 | tf_op jit(solution)/shard_map/all_to_all | solution.py:531
  91.9 1.9 %copy-done.7 = f32[4,8,24,1024]{3,2,1,0:T(8,128)S(1)} copy-done((f32[4,8,24,1024]{3,2,1,0:T(8,128)S(1)}, f32[4,8,24,1024]{3,2,1,0:T(8,128)}, u32[]{:S(2)}) %copy-start.7) | copy-done | bytes 3145752
  93.7 1.1 %copy-done.9 = f32[8,24,1024]{2,1,0:T(8,128)S(1)} copy-done((f32[8,24,1024]{2,1,0:T(8,128)S(1)}, f32[8,24,1024]{2,1,0:T(8,128)}, u32[]{:S(2)}) %copy-start.9) | copy-done | bytes 786456
  94.9 3.0 %shard_map.119 = f32[4,6,16,1024]{3,2,1,0:T(8,128)} custom-call(f32[9,24,1024]{2,1,0:T(8,128)S(1)} %copy-done.11, f32[8,24,1024]{2,1,0:T(8,128)S(1)} %get-tuple-element.20.cxs, f32[8,24,1024]{2,1,0:T(8,128)S(1)} %copy-done.9, f32[4,8,24,1024]{3,2,1,0:T(8,128)S(1)} %copy-done.7), custom_call_target="tpu_custom_call" | custom-call | bytes 6291456 | tf_op jit(solution)/shard_map/pallas_call | solution.py:532
  97.9 1.4 %all-to-all-done.1 = f32[8,64,128]{2,1,0:T(8,128)S(1)} async-done(((f32[8,64,128]{2,1,0:T(8,128)}), f32[8,64,128]{2,1,0:T(8,128)S(1)}, u32[]{:S(2)}, u32[]{:S(2)}) %all-to-all-start.1) | async-done | bytes 262176 | tf_op jit(solution)/shard_map/all_to_all | solution.py:531
  (41 shorter events, 2.2 us)
Async XLA Ops:
  3.9 9.5 %copy-start.14 = (f32[4,6]{1,0:T(4,128)S(1)}, f32[4,6]{1,0:T(4,128)}, u32[]{:S(2)}) copy-start(f32[4,6]{1,0:T(4,128)} %param.14) | copy-start | bytes 292
  3.9 9.5 %copy-start = (f32[4,6,16,1024]{3,2,1,0:T(8,128)S(1)}, f32[4,6,16,1024]{3,2,1,0:T(8,128)}, u32[]{:S(2)}) copy-start(f32[4,6,16,1024]{3,2,1,0:T(8,128)} %lam_ref.5) | copy-start | bytes 4718596
  4.0 9.5 %copy-start.2 = (f32[6,16,1024]{2,1,0:T(8,128)S(1)}, f32[6,16,1024]{2,1,0:T(8,128)}, u32[]{:S(2)}) copy-start(f32[6,16,1024]{2,1,0:T(8,128)} %kz_ref.5) | copy-start | bytes 1179652
  4.0 9.5 %copy-start.3 = (f32[6,16,1024]{2,1,0:T(8,128)S(1)}, f32[6,16,1024]{2,1,0:T(8,128)}, u32[]{:S(2)}) copy-start(f32[6,16,1024]{2,1,0:T(8,128)} %cx_ref.5) | copy-start | bytes 1179652
  4.0 9.5 %copy-start.13 = (f32[6]{0:T(128)S(1)}, f32[6]{0:T(128)}, u32[]{:S(2)}) copy-start(f32[6]{0:T(128)} %gain_ref.5) | copy-start | bytes 76
  4.0 26.7 %all-to-all-start = ((bf16[32,144,128]{2,1,0:T(8,128)(2,1)}), bf16[32,144,128]{2,1,0:T(8,128)(2,1)S(1)}, u32[]{:S(2)}, u32[]{:S(2)}) async-start(bf16[32,144,128]{2,1,0:T(8,128)(2,1)} %shard_map.113.after_ref), calls=%async_computation | async-start | bytes 2359296 | tf_op jit(solution)/shard_map/all_to_all | solution.py:455
  13.5 1.3 %copy-start.1 = (bf16[32,144,128]{2,1,0:T(8,128)(2,1)S(1)}, bf16[32,144,128]{2,1,0:T(8,128)(2,1)}, u32[]{:S(2)}) copy-start(bf16[32,144,128]{2,1,0:T(8,128)(2,1)} %shard_map.113.after_ref) | copy-start | bytes 3538948
  14.7 1.0 copy-start.4
  17.4 28.5 %collective-permute-start = (bf16[14,16,1024]{2,1,0:T(8,128)(2,1)}, bf16[14,16,1024]{2,1,0:T(8,128)(2,1)}, u32[]{:S(2)}, u32[]{:S(2)}) collective-permute-start(bf16[14,16,1024]{2,1,0:T(8,128)(2,1)} %get-tuple-element.15), channel_id=1, source_target_pairs={{0,64},{64,128},{128,192},{192,256},{256,320},{320,384},{384,448},... | collective-permute-start | bytes 1376264 | tf_op jit(solution)/shard_map/ppermute | solution.py:463
  20.2 25.7 %collective-permute-start.1 = (bf16[13,16,1024]{2,1,0:T(8,128)(2,1)}, bf16[13,16,1024]{2,1,0:T(8,128)(2,1)}, u32[]{:S(2)}, u32[]{:S(2)}) collective-permute-start(bf16[13,16,1024]{2,1,0:T(8,128)(2,1)} %get-tuple-element.16), channel_id=1, source_target_pairs={{64,0},{128,64},{192,128},{256,192},{320,256},{384,320},{448,384},... | collective-permute-start | bytes 1277960 | tf_op jit(solution)/shard_map/ppermute | solution.py:464
  30.7 15.2 %copy-start.5 = (f32[6,16,1024]{2,1,0:T(8,128)S(1)}, f32[6,16,1024]{2,1,0:T(8,128)}, u32[]{:S(2)}) copy-start(f32[6,16,1024]{2,1,0:T(8,128)} %cy_ref.5) | copy-start | bytes 1179652
  31.4 24.0 %collective-permute-start.5 = (f32[128,128]{1,0:T(8,128)S(1)}, f32[128,128]{1,0:T(8,128)S(1)}, u32[]{:S(2)}, u32[]{:S(2)}) collective-permute-start(f32[128,128]{1,0:T(8,128)S(1)} %get-tuple-element.28), channel_id=1, source_target_pairs={{0,32},{4,36},{8,40},{12,44},{16,48},{20,52},{24,56},{28,60},{32,0... | collective-permute-start | bytes 196616 | tf_op jit(solution)/shard_map/ppermute | solution.py:513
  45.2 18.3 %copy-start.12 = (f32[4,6]{1,0:T(4,128)S(1)}, f32[4,6]{1,0:T(4,128)}, u32[]{:S(2)}) copy-start(f32[4,6]{1,0:T(4,128)} %profile_ref.3) | copy-start | bytes 292
  45.2 10.3 %collective-permute-start.4 = (f32[128,128]{1,0:T(8,128)S(1)}, f32[128,128]{1,0:T(8,128)S(1)}, u32[]{:S(2)}, u32[]{:S(2)}) collective-permute-start(f32[128,128]{1,0:T(8,128)S(1)} %get-tuple-element.29), channel_id=1, source_target_pairs={{0,0},{4,4},{8,8},{12,12},{16,16},{20,20},{24,24},{28,28},{32,32},... | collective-permute-start | bytes 196616 | tf_op jit(solution)/shard_map/ppermute | solution.py:513
  47.5 16.0 %collective-permute-start.2 = (bf16[144,1024]{1,0:T(8,128)(2,1)S(1)}, bf16[144,1024]{1,0:T(8,128)(2,1)S(1)}, u32[]{:S(2)}, u32[]{:S(2)}) collective-permute-start(bf16[144,1024]{1,0:T(8,128)(2,1)S(1)} %get-tuple-element.17), channel_id=1, source_target_pairs={{1,0},{2,1},{3,2},{4,3},{5,4},{6,5},{7,6},{8,7},{9,8},{10,9},{11,1... | collective-permute-start | bytes 884744 | tf_op jit(solution)/shard_map/ppermute | solution.py:472
  50.2 13.3 %collective-permute-start.3 = (bf16[144,1024]{1,0:T(8,128)(2,1)S(1)}, bf16[144,1024]{1,0:T(8,128)(2,1)S(1)}, u32[]{:S(2)}, u32[]{:S(2)}) collective-permute-start(bf16[144,1024]{1,0:T(8,128)(2,1)S(1)} %get-tuple-element.18), channel_id=1, source_target_pairs={{0,1},{1,2},{2,3},{3,4},{4,5},{5,6},{6,7},{7,8},{8,9},{9,10},{10,1... | collective-permute-start | bytes 884744 | tf_op jit(solution)/shard_map/ppermute | solution.py:473
  55.5 13.0 %collective-permute-start.6 = (f32[16,128]{1,0:T(8,128)S(1)}, f32[16,128]{1,0:T(8,128)S(1)}, u32[]{:S(2)}, u32[]{:S(2)}) collective-permute-start(f32[16,128]{1,0:T(8,128)S(1)} %get-tuple-element.30), channel_id=1, source_target_pairs={{1,0},{2,1},{3,2},{4,3},{5,4},{6,5},{7,6},{8,7},{9,8},{10,9},{11,1... | collective-permute-start | bytes 24584 | tf_op jit(solution)/shard_map/ppermute | solution.py:517
  57.5 11.0 %collective-permute-start.7 = (f32[16,128]{1,0:T(8,128)S(1)}, f32[16,128]{1,0:T(8,128)S(1)}, u32[]{:S(2)}, u32[]{:S(2)}) collective-permute-start(f32[16,128]{1,0:T(8,128)S(1)} %get-tuple-element.31), channel_id=1, source_target_pairs={{0,1},{1,2},{2,3},{3,4},{4,5},{5,6},{6,7},{7,8},{8,9},{9,10},{10,1... | collective-permute-start | bytes 24584 | tf_op jit(solution)/shard_map/ppermute | solution.py:518
  68.5 18.3 %copy-start.8 = (f32[8,24,1024]{2,1,0:T(8,128)}, f32[8,24,1024]{2,1,0:T(8,128)S(1)}, u32[]{:S(2)}) copy-start(f32[8,24,1024]{2,1,0:T(8,128)S(1)} %get-tuple-element.21.cys) | copy-start | bytes 2359300
  82.3 9.5 %copy-start.11 = (f32[9,24,1024]{2,1,0:T(8,128)S(1)}, f32[9,24,1024]{2,1,0:T(8,128)}, u32[]{:S(2)}) copy-start(f32[9,24,1024]{2,1,0:T(8,128)} %copy-done.10) | copy-start | bytes 2654212
  86.8 1.6 %copy-start.6 = (f32[4,8,24,1024]{3,2,1,0:T(8,128)}, f32[4,8,24,1024]{3,2,1,0:T(8,128)S(1)}, u32[]{:S(2)}) copy-start(f32[4,8,24,1024]{3,2,1,0:T(8,128)S(1)} %get-tuple-element.26.later_ref) | copy-start | bytes 9437188
  88.4 10.9 %all-to-all-start.1 = ((f32[8,64,128]{2,1,0:T(8,128)}), f32[8,64,128]{2,1,0:T(8,128)S(1)}, u32[]{:S(2)}, u32[]{:S(2)}) async-start(f32[8,64,128]{2,1,0:T(8,128)} %get-tuple-element.27), calls=%async_computation.1 | async-start | bytes 524288 | tf_op jit(solution)/shard_map/all_to_all | solution.py:531
  91.8 1.9 %copy-start.7 = (f32[4,8,24,1024]{3,2,1,0:T(8,128)S(1)}, f32[4,8,24,1024]{3,2,1,0:T(8,128)}, u32[]{:S(2)}) copy-start(f32[4,8,24,1024]{3,2,1,0:T(8,128)} %copy-done.6) | copy-start | bytes 9437188
  93.7 1.1 %copy-start.9 = (f32[8,24,1024]{2,1,0:T(8,128)S(1)}, f32[8,24,1024]{2,1,0:T(8,128)}, u32[]{:S(2)}) copy-start(f32[8,24,1024]{2,1,0:T(8,128)} %copy-done.8) | copy-start | bytes 2359300
  (1 other events, 0.9 us)

commit v5 on v4

--- a/solution.py
+++ b/solution.py
@@ -459,6 +459,7 @@
         (shape((14, rows, cols), BF16), shape((13, rows, cols), BF16)),
         [smem] * 3 + [vmem] * 4 + [anywhere],
         moved=4 << 20,
+        limit=MOST,
     )(where, decay, kernel, lam_in, kz_face, courant_x, courant_y, packed)
     low = chain(LEV, lev_count, 1)(up)
     high = chain(LEV, lev_count, -1)(down)

time: 101 us -> 98.8 us (0.978)
  local copies, waits for them, and re-layouts: 7.87 us -> 4.48 us
  Pallas kernels: 18.7 us -> 20.1 us
  other arithmetic: 0.73 us -> 1.89 us
    unnamed x30, local copies, waits for them, and re-layouts: 7.86 us -> 4.47 us
    pallas_call x1, Pallas kernels: 1.61 us -> 2.74 us  [on_device(): call(level_kernel, (shape((14, rows, cols), BF16), shape((13, rows, cols)...]
  transfers between devices with their start and end apart: 10 -> 10, of which waited for: 2 -> 2; matrix products, arithmetic and copies ran while one was open for 0% -> 1% of each run, Pallas kernels for 11% -> 12%
where the time goes in v5:
time: 98.8 us; the launch traced here: 98 us
  starting transfers between devices  47.2 us (48%)
  Pallas kernels  20.1 us (20%)
  blocking collectives  13.2 us (13%)
  waiting for transfers between devices  10.1 us (10%)
  local copies, waits for them, and re-layouts  4.48 us (5%)
  other arithmetic  1.89 us (2%)
    ppermute x2, starting transfers between devices, along_z(): return lax.ppermute(value, LEV + ('z',), perm)  14.4 us
    all_gather x1, blocking collectives, on_device(): lax.all_gather(jnp.concatenate([part, part_after, part_prior]), LEV, axis=0)  13.2 us
    all_to_all x1, starting transfers between devices, on_device(): got = lax.all_to_all(packed, LEV + ('y',), 0, 0, tiled=True)  9.22 us
    all_to_all x1, waiting for transfers between devices, on_device(): got = lax.all_to_all(packed, LEV + ('y',), 0, 0, tiled=True)  9.13 us
    ppermute x1, starting transfers between devices, on_device(): part_prior = chain(TILE, tile_count, 1)(part[-edge:])  6.03 us
    ppermute x1, starting transfers between devices, on_device(): prior = chain(TILE, tile_count, 1)(last_rows)  5.23 us
    pallas_call x1, Pallas kernels, on_device(): call(first_kernel, (shape((tracers, 8, ROWS, cols), F32), shape((lev_coun...  4.58 us
    unnamed x30, local copies, waits for them, and re-layouts  4.47 us
  transfers between devices with their start and end apart: 10, of which 2 were waited for; matrix products, arithmetic and copies ran while one was open for 1% of the time, Pallas kernels for 12%

profile of v5, /device:TPU:24, one launch (start us, length us, event | category | flops | bytes accessed | tf_op | source)
XLA Modules:
  0.0 98.0 jit_solution(2437972124984112257)
XLA Ops:
  0.6 3.3 %shard_map.113.after_ref = bf16[32,144,128]{2,1,0:T(8,128)(2,1)} custom-call(s32[1,1024]{1,0:T(1,128)} %bitcast.12, s32[1,1024]{1,0:T(1,128)} %bitcast.13, bf16[1024,128]{1,0:T(8,128)(2,1)} %obs_hbm.1), custom_call_target="tpu_custom_call" | custom-call | flops 1073741824 | bytes 2097152 | tf_op jit(solution)/shard_map/pallas_call | solution.py:438
  3.9 9.2 %all-to-all-start = ((bf16[32,144,128]{2,1,0:T(8,128)(2,1)}), bf16[32,144,128]{2,1,0:T(8,128)(2,1)S(1)}, u32[]{:S(2)}, u32[]{:S(2)}) async-start(bf16[32,144,128]{2,1,0:T(8,128)(2,1)} %shard_map.113.after_ref), calls=%async_computation | async-start | bytes 2359296 | tf_op jit(solution)/shard_map/all_to_all | solution.py:455
  14.4 2.7 %shard_map.114 = (bf16[14,16,1024]{2,1,0:T(8,128)(2,1)}, bf16[13,16,1024]{2,1,0:T(8,128)(2,1)}) custom-call(s32[2]{0:T(128)} %add_convert_fusion.where_ref, f32[4,6]{1,0:T(4,128)} %negate_exponential_fusion.decay_ref, f32[6]{0:T(128)} %gain_ref.5, f32[4,6,16,1024]{3,2,1,0:T(8,128)} %lam_ref.5, f32[6,16,1024]{2,1,0:T(8,128)} %kz_ref.5, ...), custom_call_target="tpu_custom_call" | custom-call | bytes 4194304 | tf_op jit(solution)/shard_map/pallas_call | solution.py:457
  17.2 3.0 %collective-permute-start = (bf16[14,16,1024]{2,1,0:T(8,128)(2,1)}, bf16[14,16,1024]{2,1,0:T(8,128)(2,1)}, u32[]{:S(2)}, u32[]{:S(2)}) collective-permute-start(bf16[14,16,1024]{2,1,0:T(8,128)(2,1)} %get-tuple-element.15), channel_id=1, source_target_pairs={{0,64},{64,128},{128,192},{192,256},{256,320},{320,384},{384,448},... | collective-permute-start | bytes 1376264 | tf_op jit(solution)/shard_map/ppermute | solution.py:464
  20.1 1.3 %collective-permute-start.1 = (bf16[13,16,1024]{2,1,0:T(8,128)(2,1)}, bf16[13,16,1024]{2,1,0:T(8,128)(2,1)}, u32[]{:S(2)}, u32[]{:S(2)}) collective-permute-start(bf16[13,16,1024]{2,1,0:T(8,128)(2,1)} %get-tuple-element.16), channel_id=1, source_target_pairs={{64,0},{128,64},{192,128},{256,192},{320,256},{384,320},{448,384},... | collective-permute-start | bytes 1277960 | tf_op jit(solution)/shard_map/ppermute | solution.py:465
  21.4 9.1 %all-to-all-done.got_ref = bf16[32,144,128]{2,1,0:T(8,128)(2,1)S(1)} async-done(((bf16[32,144,128]{2,1,0:T(8,128)(2,1)}), bf16[32,144,128]{2,1,0:T(8,128)(2,1)S(1)}, u32[]{:S(2)}, u32[]{:S(2)}) %all-to-all-start) | async-done | bytes 1179680 | tf_op jit(solution)/shard_map/all_to_all | solution.py:455
  30.5 0.7 shard_map.117
  31.3 13.7 %collective-permute-start.5 = (f32[128,128]{1,0:T(8,128)S(1)}, f32[128,128]{1,0:T(8,128)S(1)}, u32[]{:S(2)}, u32[]{:S(2)}) collective-permute-start(f32[128,128]{1,0:T(8,128)S(1)} %get-tuple-element.28), channel_id=1, source_target_pairs={{0,32},{4,36},{8,40},{12,44},{16,48},{20,52},{24,56},{28,60},{32,0... | collective-permute-start | bytes 196616 | tf_op jit(solution)/shard_map/ppermute | solution.py:514
  45.0 0.7 collective-permute-start.4
  45.7 1.0 %copy-done.3 = f32[6,16,1024]{2,1,0:T(8,128)S(1)} copy-done((f32[6,16,1024]{2,1,0:T(8,128)S(1)}, f32[6,16,1024]{2,1,0:T(8,128)}, u32[]{:S(2)}) %copy-start.3) | copy-done | bytes 393240
  46.7 1.6 %shard_map.115 = (bf16[144,1024]{1,0:T(8,128)(2,1)S(1)}, bf16[144,1024]{1,0:T(8,128)(2,1)S(1)}) custom-call(s32[2]{0:T(128)S(1)} %copy-done.13, f32[4,6,16,1024]{3,2,1,0:T(8,128)S(1)} %copy-done, f32[6,16,1024]{2,1,0:T(8,128)S(1)} %copy-done.1, f32[6,16,1024]{2,1,0:T(8,128)S(1)} %copy-done.2, f32[6,16,1024]{2,1,0:T(8,128)S(1)} %copy-done.3, ...), custom_call_target="tpu_custom_call" | custom-call | bytes 5242880 | tf_op jit(solution)/shard_map/pallas_call | solution.py:466
  48.4 2.7 %collective-permute-start.2 = (bf16[144,1024]{1,0:T(8,128)(2,1)S(1)}, bf16[144,1024]{1,0:T(8,128)(2,1)S(1)}, u32[]{:S(2)}, u32[]{:S(2)}) collective-permute-start(bf16[144,1024]{1,0:T(8,128)(2,1)S(1)} %get-tuple-element.17), channel_id=1, source_target_pairs={{1,0},{2,1},{3,2},{4,3},{5,4},{6,5},{7,6},{8,7},{9,8},{10,9},{11,1... | collective-permute-start | bytes 884744 | tf_op jit(solution)/shard_map/ppermute | solution.py:473
  51.1 5.2 %collective-permute-start.3 = (bf16[144,1024]{1,0:T(8,128)(2,1)S(1)}, bf16[144,1024]{1,0:T(8,128)(2,1)S(1)}, u32[]{:S(2)}, u32[]{:S(2)}) collective-permute-start(bf16[144,1024]{1,0:T(8,128)(2,1)S(1)} %get-tuple-element.18), channel_id=1, source_target_pairs={{0,1},{1,2},{2,3},{3,4},{4,5},{5,6},{6,7},{7,8},{8,9},{9,10},{10,1... | collective-permute-start | bytes 884744 | tf_op jit(solution)/shard_map/ppermute | solution.py:474
  56.4 1.9 %collective-permute-start.6 = (f32[16,128]{1,0:T(8,128)S(1)}, f32[16,128]{1,0:T(8,128)S(1)}, u32[]{:S(2)}, u32[]{:S(2)}) collective-permute-start(f32[16,128]{1,0:T(8,128)S(1)} %get-tuple-element.30), channel_id=1, source_target_pairs={{1,0},{2,1},{3,2},{4,3},{5,4},{6,5},{7,6},{8,7},{9,8},{10,9},{11,1... | collective-permute-start | bytes 24584 | tf_op jit(solution)/shard_map/ppermute | solution.py:518
  58.3 6.0 %collective-permute-start.7 = (f32[16,128]{1,0:T(8,128)S(1)}, f32[16,128]{1,0:T(8,128)S(1)}, u32[]{:S(2)}, u32[]{:S(2)}) collective-permute-start(f32[16,128]{1,0:T(8,128)S(1)} %get-tuple-element.31), channel_id=1, source_target_pairs={{0,1},{1,2},{2,3},{3,4},{4,5},{5,6},{6,7},{7,8},{8,9},{9,10},{10,1... | collective-permute-start | bytes 24584 | tf_op jit(solution)/shard_map/ppermute | solution.py:519
  64.4 4.1 %shard_map.116 = (f32[9,24,1024]{2,1,0:T(8,128)S(1)}, f32[8,24,1024]{2,1,0:T(8,128)S(1)}, f32[8,24,1024]{2,1,0:T(8,128)S(1)}, f32[4,8,24,1024]{3,2,1,0:T(8,128)S...) custom-call(s32[2]{0:T(128)S(1)} %copy-done.13, f32[4,6]{1,0:T(4,128)S(1)} %copy-done.10, ...), custom_call_target="tpu_custom_call" | custom-call | bytes 12582912 | tf_op jit(solution)/shard_map/pallas_call | solution.py:475
  68.6 13.2 %all-gather = f32[1280,128]{1,0:T(8,128)S(1)} all-gather(f32[160,128]{1,0:T(8,128)S(1)} %pad_maximum_fusion), channel_id=2, replica_groups=mesh['x'=4,'core'=2,'z'=16,'y'=4] {'x','core'}, dimensions={0}, use_global_device_ids=true | all-gather | bytes 737280 | tf_op jit(solution)/shard_map/all_gather | solution.py:520
  81.9 4.6 %shard_map.118 = (f32[4,8,24,1024]{3,2,1,0:T(8,128)S(1)}, f32[8,64,128]{2,1,0:T(8,128)}) custom-call(f32[6]{0:T(128)S(1)} %copy-done.12, f32[4,6]{1,0:T(4,128)S(1)} %copy-done.11, f32[8,24,1024]{2,1,0:T(8,128)S(1)} %get-tuple-element.20.cxs, f32[8,24,1024]{2,1,0:T(8,128)S(1)} %get-tuple-element.21.cys, f32[4,8,24,1024]{3,2,1,0:T(8,128)S(1)} %get-tuple-element.22.mixed_ref, ...), custom_call_target="tpu_custom_call" | custom-call | bytes 8388608 | tf_op jit(solution)/shard_map/pallas_call | solution.py:522
  86.5 3.4 %all-to-all-start.1 = ((f32[8,64,128]{2,1,0:T(8,128)}), f32[8,64,128]{2,1,0:T(8,128)S(1)}, u32[]{:S(2)}, u32[]{:S(2)}) async-start(f32[8,64,128]{2,1,0:T(8,128)} %get-tuple-element.27), calls=%async_computation.1 | async-start | bytes 524288 | tf_op jit(solution)/shard_map/all_to_all | solution.py:532
  89.9 1.1 %copy-done.5 = f32[8,24,1024]{2,1,0:T(8,128)S(1)} copy-done((f32[8,24,1024]{2,1,0:T(8,128)S(1)}, f32[8,24,1024]{2,1,0:T(8,128)}, u32[]{:S(2)}) %copy-start.5) | copy-done | bytes 786456
  91.1 1.1 %copy-done.7 = f32[8,24,1024]{2,1,0:T(8,128)S(1)} copy-done((f32[8,24,1024]{2,1,0:T(8,128)S(1)}, f32[8,24,1024]{2,1,0:T(8,128)}, u32[]{:S(2)}) %copy-start.7) | copy-done | bytes 786456
  92.2 1.2 %copy-done.9 = f32[9,24,1024]{2,1,0:T(8,128)S(1)} copy-done((f32[9,24,1024]{2,1,0:T(8,128)S(1)}, f32[9,24,1024]{2,1,0:T(8,128)}, u32[]{:S(2)}) %copy-start.9) | copy-done | bytes 884760
  93.4 3.0 %shard_map.119 = f32[4,6,16,1024]{3,2,1,0:T(8,128)} custom-call(f32[9,24,1024]{2,1,0:T(8,128)S(1)} %copy-done.9, f32[8,24,1024]{2,1,0:T(8,128)S(1)} %copy-done.5, f32[8,24,1024]{2,1,0:T(8,128)S(1)} %copy-done.7, f32[4,8,24,1024]{3,2,1,0:T(8,128)S(1)} %get-tuple-element.26.later_ref), custom_call_target="tpu_custom_call" | custom-call | bytes 6291456 | tf_op jit(solution)/shard_map/pallas_call | solution.py:533
  96.4 1.0 %all-to-all-done.1 = f32[8,64,128]{2,1,0:T(8,128)S(1)} async-done(((f32[8,64,128]{2,1,0:T(8,128)}), f32[8,64,128]{2,1,0:T(8,128)S(1)}, u32[]{:S(2)}, u32[]{:S(2)}) %all-to-all-start.1) | async-done | bytes 262176 | tf_op jit(solution)/shard_map/all_to_all | solution.py:532
  (41 shorter events, 2.0 us)
Async XLA Ops:
  3.9 9.9 %copy-start.14 = (f32[4,6]{1,0:T(4,128)S(1)}, f32[4,6]{1,0:T(4,128)}, u32[]{:S(2)}) copy-start(f32[4,6]{1,0:T(4,128)} %param.14) | copy-start | bytes 292
  3.9 26.6 %all-to-all-start = ((bf16[32,144,128]{2,1,0:T(8,128)(2,1)}), bf16[32,144,128]{2,1,0:T(8,128)(2,1)S(1)}, u32[]{:S(2)}, u32[]{:S(2)}) async-start(bf16[32,144,128]{2,1,0:T(8,128)(2,1)} %shard_map.113.after_ref), calls=%async_computation | async-start | bytes 2359296 | tf_op jit(solution)/shard_map/all_to_all | solution.py:455
  14.4 31.3 %copy-start.1 = (f32[6,16,1024]{2,1,0:T(8,128)S(1)}, f32[6,16,1024]{2,1,0:T(8,128)}, u32[]{:S(2)}) copy-start(f32[6,16,1024]{2,1,0:T(8,128)} %kz_ref.5) | copy-start | bytes 1179652
  14.4 31.3 %copy-start.2 = (f32[6,16,1024]{2,1,0:T(8,128)S(1)}, f32[6,16,1024]{2,1,0:T(8,128)}, u32[]{:S(2)}) copy-start(f32[6,16,1024]{2,1,0:T(8,128)} %cx_ref.5) | copy-start | bytes 1179652
  17.2 28.6 %copy-start = (f32[4,6,16,1024]{3,2,1,0:T(8,128)S(1)}, f32[4,6,16,1024]{3,2,1,0:T(8,128)}, u32[]{:S(2)}) copy-start(f32[4,6,16,1024]{3,2,1,0:T(8,128)} %lam_ref.5) | copy-start | bytes 4718596
  17.2 28.6 %copy-start.13 = (s32[2]{0:T(128)S(1)}, s32[2]{0:T(128)}, u32[]{:S(2)}) copy-start(s32[2]{0:T(128)} %add_convert_fusion.where_ref) | copy-start | bytes 28
  17.2 28.5 %collective-permute-start = (bf16[14,16,1024]{2,1,0:T(8,128)(2,1)}, bf16[14,16,1024]{2,1,0:T(8,128)(2,1)}, u32[]{:S(2)}, u32[]{:S(2)}) collective-permute-start(bf16[14,16,1024]{2,1,0:T(8,128)(2,1)} %get-tuple-element.15), channel_id=1, source_target_pairs={{0,64},{64,128},{128,192},{192,256},{256,320},{320,384},{384,448},... | collective-permute-start | bytes 1376264 | tf_op jit(solution)/shard_map/ppermute | solution.py:464
  20.1 25.6 %collective-permute-start.1 = (bf16[13,16,1024]{2,1,0:T(8,128)(2,1)}, bf16[13,16,1024]{2,1,0:T(8,128)(2,1)}, u32[]{:S(2)}, u32[]{:S(2)}) collective-permute-start(bf16[13,16,1024]{2,1,0:T(8,128)(2,1)} %get-tuple-element.16), channel_id=1, source_target_pairs={{64,0},{128,64},{192,128},{256,192},{320,256},{384,320},{448,384},... | collective-permute-start | bytes 1277960 | tf_op jit(solution)/shard_map/ppermute | solution.py:465
  31.3 25.1 %collective-permute-start.5 = (f32[128,128]{1,0:T(8,128)S(1)}, f32[128,128]{1,0:T(8,128)S(1)}, u32[]{:S(2)}, u32[]{:S(2)}) collective-permute-start(f32[128,128]{1,0:T(8,128)S(1)} %get-tuple-element.28), channel_id=1, source_target_pairs={{0,32},{4,36},{8,40},{12,44},{16,48},{20,52},{24,56},{28,60},{32,0... | collective-permute-start | bytes 196616 | tf_op jit(solution)/shard_map/ppermute | solution.py:514
  45.0 19.4 %copy-start.12 = (f32[6]{0:T(128)S(1)}, f32[6]{0:T(128)}, u32[]{:S(2)}) copy-start(f32[6]{0:T(128)} %gain_ref.5) | copy-start | bytes 76
  45.0 11.4 %collective-permute-start.4 = (f32[128,128]{1,0:T(8,128)S(1)}, f32[128,128]{1,0:T(8,128)S(1)}, u32[]{:S(2)}, u32[]{:S(2)}) collective-permute-start(f32[128,128]{1,0:T(8,128)S(1)} %get-tuple-element.29), channel_id=1, source_target_pairs={{0,0},{4,4},{8,8},{12,12},{16,16},{20,20},{24,24},{28,28},{32,32},... | collective-permute-start | bytes 196616 | tf_op jit(solution)/shard_map/ppermute | solution.py:514
  46.7 17.7 %copy-start.10 = (f32[4,6]{1,0:T(4,128)S(1)}, f32[4,6]{1,0:T(4,128)}, u32[]{:S(2)}) copy-start(f32[4,6]{1,0:T(4,128)} %negate_exponential_fusion.decay_ref) | copy-start | bytes 292
  46.7 17.7 %copy-start.11 = (f32[4,6]{1,0:T(4,128)S(1)}, f32[4,6]{1,0:T(4,128)}, u32[]{:S(2)}) copy-start(f32[4,6]{1,0:T(4,128)} %profile_ref.3) | copy-start | bytes 292
  48.4 16.0 %collective-permute-start.2 = (bf16[144,1024]{1,0:T(8,128)(2,1)S(1)}, bf16[144,1024]{1,0:T(8,128)(2,1)S(1)}, u32[]{:S(2)}, u32[]{:S(2)}) collective-permute-start(bf16[144,1024]{1,0:T(8,128)(2,1)S(1)} %get-tuple-element.17), channel_id=1, source_target_pairs={{1,0},{2,1},{3,2},{4,3},{5,4},{6,5},{7,6},{8,7},{9,8},{10,9},{11,1... | collective-permute-start | bytes 884744 | tf_op jit(solution)/shard_map/ppermute | solution.py:473
  51.1 13.3 %collective-permute-start.3 = (bf16[144,1024]{1,0:T(8,128)(2,1)S(1)}, bf16[144,1024]{1,0:T(8,128)(2,1)S(1)}, u32[]{:S(2)}, u32[]{:S(2)}) collective-permute-start(bf16[144,1024]{1,0:T(8,128)(2,1)S(1)} %get-tuple-element.18), channel_id=1, source_target_pairs={{0,1},{1,2},{2,3},{3,4},{4,5},{5,6},{6,7},{7,8},{8,9},{9,10},{10,1... | collective-permute-start | bytes 884744 | tf_op jit(solution)/shard_map/ppermute | solution.py:474
  56.4 12.2 %collective-permute-start.6 = (f32[16,128]{1,0:T(8,128)S(1)}, f32[16,128]{1,0:T(8,128)S(1)}, u32[]{:S(2)}, u32[]{:S(2)}) collective-permute-start(f32[16,128]{1,0:T(8,128)S(1)} %get-tuple-element.30), channel_id=1, source_target_pairs={{1,0},{2,1},{3,2},{4,3},{5,4},{6,5},{7,6},{8,7},{9,8},{10,9},{11,1... | collective-permute-start | bytes 24584 | tf_op jit(solution)/shard_map/ppermute | solution.py:518
  58.3 10.3 %collective-permute-start.7 = (f32[16,128]{1,0:T(8,128)S(1)}, f32[16,128]{1,0:T(8,128)S(1)}, u32[]{:S(2)}, u32[]{:S(2)}) collective-permute-start(f32[16,128]{1,0:T(8,128)S(1)} %get-tuple-element.31), channel_id=1, source_target_pairs={{0,1},{1,2},{2,3},{3,4},{4,5},{5,6},{6,7},{7,8},{8,9},{9,10},{10,1... | collective-permute-start | bytes 24584 | tf_op jit(solution)/shard_map/ppermute | solution.py:519
  68.6 17.9 %copy-start.4 = (f32[8,24,1024]{2,1,0:T(8,128)}, f32[8,24,1024]{2,1,0:T(8,128)S(1)}, u32[]{:S(2)}) copy-start(f32[8,24,1024]{2,1,0:T(8,128)S(1)} %get-tuple-element.20.cxs) | copy-start | bytes 2359300
  68.6 17.9 %copy-start.6 = (f32[8,24,1024]{2,1,0:T(8,128)}, f32[8,24,1024]{2,1,0:T(8,128)S(1)}, u32[]{:S(2)}) copy-start(f32[8,24,1024]{2,1,0:T(8,128)S(1)} %get-tuple-element.21.cys) | copy-start | bytes 2359300
  68.6 17.9 %copy-start.8 = (f32[9,24,1024]{2,1,0:T(8,128)}, f32[9,24,1024]{2,1,0:T(8,128)S(1)}, u32[]{:S(2)}) copy-start(f32[9,24,1024]{2,1,0:T(8,128)S(1)} %get-tuple-element.19.kzs) | copy-start | bytes 2654212
  86.5 10.9 %all-to-all-start.1 = ((f32[8,64,128]{2,1,0:T(8,128)}), f32[8,64,128]{2,1,0:T(8,128)S(1)}, u32[]{:S(2)}, u32[]{:S(2)}) async-start(f32[8,64,128]{2,1,0:T(8,128)} %get-tuple-element.27), calls=%async_computation.1 | async-start | bytes 524288 | tf_op jit(solution)/shard_map/all_to_all | solution.py:532
  89.9 1.1 %copy-start.5 = (f32[8,24,1024]{2,1,0:T(8,128)S(1)}, f32[8,24,1024]{2,1,0:T(8,128)}, u32[]{:S(2)}) copy-start(f32[8,24,1024]{2,1,0:T(8,128)} %copy-done.4) | copy-start | bytes 2359300
  91.1 1.1 %copy-start.7 = (f32[8,24,1024]{2,1,0:T(8,128)S(1)}, f32[8,24,1024]{2,1,0:T(8,128)}, u32[]{:S(2)}) copy-start(f32[8,24,1024]{2,1,0:T(8,128)} %copy-done.6) | copy-start | bytes 2359300
  92.2 1.2 %copy-start.9 = (f32[9,24,1024]{2,1,0:T(8,128)S(1)}, f32[9,24,1024]{2,1,0:T(8,128)}, u32[]{:S(2)}) copy-start(f32[9,24,1024]{2,1,0:T(8,128)} %copy-done.8) | copy-start | bytes 2654212
  (1 other events, 1.0 us)

commit v6 on v5

--- a/solution.py
+++ b/solution.py
@@ -16,6 +16,7 @@
 TILE = ("z", "y")
 ROWS = 24
 STRIP = 144
+OWN = 96
 VMEM = 24 * 1024 * 1024
 MOST = 63487488
 F32, BF16 = jnp.float32, jnp.bfloat16
@@ -153,9 +154,23 @@
 
 
 def level_kernel(
-    where_ref, decay_ref, gain_ref, lam_ref, kz_ref, cx_ref, cy_ref, after_ref, up_ref, down_ref
+    where_ref, decay_ref, gain_ref, lam_ref, kz_ref, cx_ref, cy_ref, after_ref, up_ref, down_ref, prior_ref, next_ref, strip
 ):
     mask_kz, mask_cx, mask_cy = masks(where_ref)
+    for ref, first in ((prior_ref, 0), (next_ref, 14)):
+        rows = slice(first, first + 2)
+
+        def put(plane, value):
+            strip[2 * plane : 2 * plane + 2, :] = value
+
+        strip[84:OWN, :] = jnp.zeros((OWN - 84, strip.shape[1]), F32)
+        for l in range(6):
+            for c in range(4):
+                put(c * 6 + l, lam_ref[c, l, rows, :])
+            put(24 + l, mask_kz(kz_ref[l, rows, :], l))
+            put(30 + l, mask_cx(cx_ref[l, rows, :], first))
+            put(36 + l, mask_cy(cy_ref[l, rows, :]))
+        ref[...] = strip[...].astype(BF16)
     for ref, first in ((up_ref, 4), (down_ref, 0)):
         for c in range(4):
             for i in range(2):
@@ -177,45 +192,16 @@
         ref[at + 3] = (plane - rough.astype(F32)).astype(BF16)
 
 
-def row_kernel(
-    where_ref, lam_ref, kz_ref, cx_ref, cy_ref, low_ref, high_ref, prior_ref, next_ref, strip
-):
-    mask_kz, mask_cx, mask_cy = masks(where_ref)
-    for ref, first in ((prior_ref, 0), (next_ref, 14)):
-        rows = slice(first, first + 2)
-
-        def put(plane, value):
-            strip[2 * plane : 2 * plane + 2, :] = value
-
-        strip[130:144, :] = jnp.zeros((14, strip.shape[1]), F32)
-        for c in range(4):
-            for l in range(10):
-                if l < 2:
-                    value = low_ref[c * 2 + l].astype(F32)[rows]
-                elif l < 8:
-                    value = lam_ref[c, l - 2, rows, :]
-                else:
-                    value = high_ref[c * 2 + l - 8].astype(F32)[rows]
-                put(c * 10 + l, value)
-        for l in range(9):
-            if l < 2:
-                value = low_ref[8 + l].astype(F32)[rows]
-            elif l < 8:
-                value = mask_kz(kz_ref[l - 2, rows, :], l - 2)
-            else:
-                value = high_ref[8].astype(F32)[rows]
-            put(40 + l, value)
-        for l in range(8):
-            if l < 1:
-                x, y = low_ref[10].astype(F32)[rows], low_ref[11].astype(F32)[rows]
-            elif l < 7:
-                x = mask_cx(cx_ref[l - 1, rows, :], first)
-                y = mask_cy(cy_ref[l - 1, rows, :])
-            else:
-                x, y = high_ref[9].astype(F32)[rows], high_ref[10].astype(F32)[rows]
-            put(49 + l, x)
-            put(57 + l, y)
-        ref[...] = strip[...].astype(BF16)
+def row_kernel(own_prior, own_next, low_ref, high_ref, prior_ref, next_ref, strip):
+    sources = [(low_ref, i) for i in range(8)] + [(high_ref, i) for i in range(8)]
+    sources += [(low_ref, 8), (low_ref, 9), (high_ref, 8), (low_ref, 10), (high_ref, 9)]
+    sources += [(low_ref, 11), (high_ref, 10)]
+    for ref, own, first in ((prior_ref, own_prior, 0), (next_ref, own_next, 14)):
+        ref[0:OWN, :] = own[...]
+        for i, (source, plane) in enumerate(sources):
+            strip[2 * i : 2 * i + 2, :] = source[plane].astype(F32)[first : first + 2]
+        strip[46:48, :] = jnp.zeros((2, strip.shape[1]), F32)
+        ref[OWN:STRIP, :] = strip[...].astype(BF16)
 
 
 def ready_kernel(
@@ -262,7 +248,7 @@
         else:
             body = high_ref[8].astype(F32)
         kzs[l, 0:16, :] = body
-        rim(kzs.at[l], 40 + l)
+        rim(kzs.at[l], 64 + l if l < 2 else (22 + l if l < 8 else 66))
     for l in range(8):
         if l < 1:
             x, y = low_ref[10].astype(F32), low_ref[11].astype(F32)
@@ -272,8 +258,8 @@
             x, y = high_ref[9].astype(F32), high_ref[10].astype(F32)
         cxs[l, 0:16, :] = x
         cys[l, 0:16, :] = y
-        rim(cxs.at[l], 49 + l)
-        rim(cys.at[l], 57 + l)
+        rim(cxs.at[l], 67 if l < 1 else (29 + l if l < 7 else 68))
+        rim(cys.at[l], 69 if l < 1 else (35 + l if l < 7 else 70))
     low_row = low_ref[12].astype(F32) + low_ref[13].astype(F32)
     high_row = high_ref[11].astype(F32) + high_ref[12].astype(F32)
     for l in range(10):
@@ -302,7 +288,10 @@
             else:
                 body = high_ref[c * 2 + l - 8].astype(F32)
             scaled[l, 0:16, :] = body
-            rim(scaled.at[l], c * 10 + l)
+            rim(
+                scaled.at[l],
+                48 + c * 2 + l if l < 2 else (c * 6 + l - 2 if l < 8 else 48 + c * 2 + l),
+            )
             scaled[l] = scaled[l] * decays[c * 10 + l : c * 10 + l + 1, :]
         surface_ref[c] = total
 
@@ -454,10 +443,16 @@
     )(obs_tile.reshape(1, -1), obs_block.reshape(1, -1), obs_values)
     got = lax.all_to_all(packed, LEV + ("y",), 0, 0, tiled=True)
 
-    up, down = call(
+    up, down, own_prior, own_next = call(
         level_kernel,
-        (shape((14, rows, cols), BF16), shape((13, rows, cols), BF16)),
+        (
+            shape((14, rows, cols), BF16),
+            shape((13, rows, cols), BF16),
+            shape((OWN, cols), BF16),
+            shape((OWN, cols), BF16),
+        ),
         [smem] * 3 + [vmem] * 4 + [anywhere],
+        scratch=[(OWN, cols)],
         moved=4 << 20,
         limit=MOST,
     )(where, decay, kernel, lam_in, kz_face, courant_x, courant_y, packed)
@@ -466,10 +461,10 @@
     first_rows, last_rows = call(
         row_kernel,
         (shape((STRIP, cols), BF16), shape((STRIP, cols), BF16)),
-        [smem] + [vmem] * 6,
-        scratch=[(STRIP, cols)],
-        moved=5 << 20,
-    )(where, lam_in, kz_face, courant_x, courant_y, low, high)
+        [vmem] * 4,
+        scratch=[(STRIP - OWN, cols)],
+        moved=2 << 20,
+    )(own_prior, own_next, low, high)
     after = chain(TILE, tile_count, -1)(first_rows)
     prior = chain(TILE, tile_count, 1)(last_rows)
     kzs, cxs, cys, mixed, coef, early, decays = call(

time: 98.8 us -> 99 us (level)
    unnamed x30 -> x34, local copies, waits for them, and re-layouts: 4.47 us -> 5.32 us
where the time goes in v6:
time: 99 us; the launch traced here: 98.1 us
  starting transfers between devices  46.4 us (47%)
  Pallas kernels  19.6 us (20%)
  blocking collectives  13.2 us (13%)
  waiting for transfers between devices  10.6 us (11%)
  local copies, waits for them, and re-layouts  5.34 us (5%)
  other arithmetic  1.89 us (2%)
    ppermute x2, starting transfers between devices, along_z(): return lax.ppermute(value, LEV + ('z',), perm)  14.4 us
    all_gather x1, blocking collectives, on_device(): lax.all_gather(jnp.concatenate([part, part_after, part_prior]), LEV, axis=0)  13.2 us
    all_to_all x1, waiting for transfers between devices, on_device(): got = lax.all_to_all(packed, LEV + ('y',), 0, 0, tiled=True)  9.55 us
    all_to_all x1, starting transfers between devices, on_device(): got = lax.all_to_all(packed, LEV + ('y',), 0, 0, tiled=True)  9.22 us
    ppermute x1, starting transfers between devices, on_device(): part_prior = chain(TILE, tile_count, 1)(part[-edge:])  6.03 us
    unnamed x34, local copies, waits for them, and re-layouts  5.32 us
    ppermute x1, starting transfers between devices, on_device(): prior = chain(TILE, tile_count, 1)(last_rows)  5.23 us
    pallas_call x1, Pallas kernels, on_device(): call(first_kernel, (shape((tracers, 8, ROWS, cols), F32), shape((lev_coun...  4.51 us
  transfers between devices with their start and end apart: 10, of which 2 were waited for; matrix products, arithmetic and copies ran while one was open for 1% of the time, Pallas kernels for 12%

profile of v6, /device:TPU:24, one launch (start us, length us, event | category | flops | bytes accessed | tf_op | source)
XLA Modules:
  0.0 98.1 jit_solution(4163636809497495939)
XLA Ops:
  0.6 3.3 %shard_map.113.after_ref = bf16[32,144,128]{2,1,0:T(8,128)(2,1)} custom-call(s32[1,1024]{1,0:T(1,128)} %bitcast.12, s32[1,1024]{1,0:T(1,128)} %bitcast.13, bf16[1024,128]{1,0:T(8,128)(2,1)} %obs_hbm.1), custom_call_target="tpu_custom_call" | custom-call | flops 1073741824 | bytes 2097152 | tf_op jit(solution)/shard_map/pallas_call | solution.py:427
  3.9 9.2 %all-to-all-start = ((bf16[32,144,128]{2,1,0:T(8,128)(2,1)}), bf16[32,144,128]{2,1,0:T(8,128)(2,1)S(1)}, u32[]{:S(2)}, u32[]{:S(2)}) async-start(bf16[32,144,128]{2,1,0:T(8,128)(2,1)} %shard_map.113.after_ref), calls=%async_computation | async-start | bytes 2359296 | tf_op jit(solution)/shard_map/all_to_all | solution.py:444
  14.4 3.0 %shard_map.114 = (bf16[14,16,1024]{2,1,0:T(8,128)(2,1)}, bf16[13,16,1024]{2,1,0:T(8,128)(2,1)}, bf16[96,1024]{1,0:T(8,128)(2,1)}, bf16[96,1024]{1,0:T(8,128)(2,1)}) custom-call(s32[2]{0:T(128)} %add_convert_fusion.where_ref, f32[4,6]{1,0:T(4,128)} %negate_exponential_fusion.decay_ref, f32[6]{0:T(128)} %gain_ref.5, f32[4,6,16,1024]{3,2,1,0:T(8,128)} %lam_ref.3, ...), custom_call_target="tpu_custom_call" | custom-call | bytes 4194304 | tf_op jit(solution)/shard_map/pallas_call | solution.py:446
  17.5 2.2 %collective-permute-start = (bf16[14,16,1024]{2,1,0:T(8,128)(2,1)}, bf16[14,16,1024]{2,1,0:T(8,128)(2,1)S(1)}, u32[]{:S(2)}, u32[]{:S(2)}) collective-permute-start(bf16[14,16,1024]{2,1,0:T(8,128)(2,1)} %get-tuple-element.17), channel_id=1, source_target_pairs={{0,64},{64,128},{128,192},{192,256},{256,320},{320,384},{384,448},... | collective-permute-start | bytes 1376264 | tf_op jit(solution)/shard_map/ppermute | solution.py:459
  19.7 1.3 %collective-permute-start.1 = (bf16[13,16,1024]{2,1,0:T(8,128)(2,1)}, bf16[13,16,1024]{2,1,0:T(8,128)(2,1)}, u32[]{:S(2)}, u32[]{:S(2)}) collective-permute-start(bf16[13,16,1024]{2,1,0:T(8,128)(2,1)} %get-tuple-element.18), channel_id=1, source_target_pairs={{64,0},{128,64},{192,128},{256,192},{320,256},{384,320},{448,384},... | collective-permute-start | bytes 1277960 | tf_op jit(solution)/shard_map/ppermute | solution.py:460
  21.0 9.5 %all-to-all-done.got_ref = bf16[32,144,128]{2,1,0:T(8,128)(2,1)S(1)} async-done(((bf16[32,144,128]{2,1,0:T(8,128)(2,1)}), bf16[32,144,128]{2,1,0:T(8,128)(2,1)S(1)}, u32[]{:S(2)}, u32[]{:S(2)}) %all-to-all-start) | async-done | bytes 1179680 | tf_op jit(solution)/shard_map/all_to_all | solution.py:444
  30.5 0.7 shard_map.117
  31.3 13.7 %collective-permute-start.5 = (f32[128,128]{1,0:T(8,128)S(1)}, f32[128,128]{1,0:T(8,128)S(1)}, u32[]{:S(2)}, u32[]{:S(2)}) collective-permute-start(f32[128,128]{1,0:T(8,128)S(1)} %get-tuple-element.32), channel_id=1, source_target_pairs={{0,32},{4,36},{8,40},{12,44},{16,48},{20,52},{24,56},{28,60},{32,0... | collective-permute-start | bytes 196616 | tf_op jit(solution)/shard_map/ppermute | solution.py:509
  45.7 0.9 copy-done.10
  46.6 0.9 copy-done.11
  47.5 1.2 %shard_map.115 = (bf16[144,1024]{1,0:T(8,128)(2,1)S(1)}, bf16[144,1024]{1,0:T(8,128)(2,1)S(1)}) custom-call(bf16[96,1024]{1,0:T(8,128)(2,1)S(1)} %copy-done.10, bf16[96,1024]{1,0:T(8,128)(2,1)S(1)} %copy-done.11, bf16[14,16,1024]{2,1,0:T(8,128)(2,1)S(1)} %collective-permute-done.low_ref, bf16[13,16,1024]{2,1,0:T(8,128)(2,1)} %collective-permute-done.1.high_ref), custom_call_target="tpu_custom_call" | custom-call | bytes 2097152 | tf_op jit(solution)/shard_map/pallas_call | solution.py:461
  48.7 2.7 %collective-permute-start.2 = (bf16[144,1024]{1,0:T(8,128)(2,1)S(1)}, bf16[144,1024]{1,0:T(8,128)(2,1)S(1)}, u32[]{:S(2)}, u32[]{:S(2)}) collective-permute-start(bf16[144,1024]{1,0:T(8,128)(2,1)S(1)} %get-tuple-element.21), channel_id=1, source_target_pairs={{1,0},{2,1},{3,2},{4,3},{5,4},{6,5},{7,6},{8,7},{9,8},{10,9},{11,1... | collective-permute-start | bytes 884744 | tf_op jit(solution)/shard_map/ppermute | solution.py:468
  51.4 5.2 %collective-permute-start.3 = (bf16[144,1024]{1,0:T(8,128)(2,1)S(1)}, bf16[144,1024]{1,0:T(8,128)(2,1)S(1)}, u32[]{:S(2)}, u32[]{:S(2)}) collective-permute-start(bf16[144,1024]{1,0:T(8,128)(2,1)S(1)} %get-tuple-element.22), channel_id=1, source_target_pairs={{0,1},{1,2},{2,3},{3,4},{4,5},{5,6},{6,7},{7,8},{8,9},{9,10},{10,1... | collective-permute-start | bytes 884744 | tf_op jit(solution)/shard_map/ppermute | solution.py:469
  56.7 1.9 %collective-permute-start.6 = (f32[16,128]{1,0:T(8,128)S(1)}, f32[16,128]{1,0:T(8,128)S(1)}, u32[]{:S(2)}, u32[]{:S(2)}) collective-permute-start(f32[16,128]{1,0:T(8,128)S(1)} %get-tuple-element.34), channel_id=1, source_target_pairs={{1,0},{2,1},{3,2},{4,3},{5,4},{6,5},{7,6},{8,7},{9,8},{10,9},{11,1... | collective-permute-start | bytes 24584 | tf_op jit(solution)/shard_map/ppermute | solution.py:513
  58.7 6.0 %collective-permute-start.7 = (f32[16,128]{1,0:T(8,128)S(1)}, f32[16,128]{1,0:T(8,128)S(1)}, u32[]{:S(2)}, u32[]{:S(2)}) collective-permute-start(f32[16,128]{1,0:T(8,128)S(1)} %get-tuple-element.35), channel_id=1, source_target_pairs={{0,1},{1,2},{2,3},{3,4},{4,5},{5,6},{6,7},{7,8},{8,9},{9,10},{10,1... | collective-permute-start | bytes 24584 | tf_op jit(solution)/shard_map/ppermute | solution.py:514
  64.8 3.9 %shard_map.116 = (f32[9,24,1024]{2,1,0:T(8,128)S(1)}, f32[8,24,1024]{2,1,0:T(8,128)S(1)}, f32[8,24,1024]{2,1,0:T(8,128)S(1)}, f32[4,8,24,1024]{3,2,1,0:T(8,128)S...) custom-call(s32[2]{0:T(128)S(1)} %copy-done.15, f32[4,6]{1,0:T(4,128)S(1)} %copy-done.12, ...), custom_call_target="tpu_custom_call" | custom-call | bytes 12582912 | tf_op jit(solution)/shard_map/pallas_call | solution.py:470
  68.8 13.2 %all-gather = f32[1280,128]{1,0:T(8,128)S(1)} all-gather(f32[160,128]{1,0:T(8,128)S(1)} %pad_maximum_fusion), channel_id=2, replica_groups=mesh['x'=4,'core'=2,'z'=16,'y'=4] {'x','core'}, dimensions={0}, use_global_device_ids=true | all-gather | bytes 737280 | tf_op jit(solution)/shard_map/all_gather | solution.py:515
  82.0 4.5 %shard_map.118 = (f32[4,8,24,1024]{3,2,1,0:T(8,128)S(1)}, f32[8,64,128]{2,1,0:T(8,128)}) custom-call(f32[6]{0:T(128)S(1)} %copy-done.14, f32[4,6]{1,0:T(4,128)S(1)} %copy-done.13, f32[8,24,1024]{2,1,0:T(8,128)S(1)} %get-tuple-element.24.cxs, f32[8,24,1024]{2,1,0:T(8,128)S(1)} %get-tuple-element.25.cys, f32[4,8,24,1024]{3,2,1,0:T(8,128)S(1)} %get-tuple-element.26.mixed_ref, ...), custom_call_target="tpu_custom_call" | custom-call | bytes 8388608 | tf_op jit(solution)/shard_map/pallas_call | solution.py:517
  86.5 3.4 %all-to-all-start.1 = ((f32[8,64,128]{2,1,0:T(8,128)}), f32[8,64,128]{2,1,0:T(8,128)S(1)}, u32[]{:S(2)}, u32[]{:S(2)}) async-start(f32[8,64,128]{2,1,0:T(8,128)} %get-tuple-element.31), calls=%async_computation.1 | async-start | bytes 524288 | tf_op jit(solution)/shard_map/all_to_all | solution.py:527
  90.0 1.1 %copy-done.2 = f32[8,24,1024]{2,1,0:T(8,128)S(1)} copy-done((f32[8,24,1024]{2,1,0:T(8,128)S(1)}, f32[8,24,1024]{2,1,0:T(8,128)}, u32[]{:S(2)}) %copy-start.2) | copy-done | bytes 786456
  91.1 1.1 %copy-done.4 = f32[8,24,1024]{2,1,0:T(8,128)S(1)} copy-done((f32[8,24,1024]{2,1,0:T(8,128)S(1)}, f32[8,24,1024]{2,1,0:T(8,128)}, u32[]{:S(2)}) %copy-start.4) | copy-done | bytes 786456
  92.2 1.2 %copy-done.9 = f32[9,24,1024]{2,1,0:T(8,128)S(1)} copy-done((f32[9,24,1024]{2,1,0:T(8,128)S(1)}, f32[9,24,1024]{2,1,0:T(8,128)}, u32[]{:S(2)}) %copy-start.9) | copy-done | bytes 884760
  93.4 3.0 %shard_map.119 = f32[4,6,16,1024]{3,2,1,0:T(8,128)} custom-call(f32[9,24,1024]{2,1,0:T(8,128)S(1)} %copy-done.9, f32[8,24,1024]{2,1,0:T(8,128)S(1)} %copy-done.2, f32[8,24,1024]{2,1,0:T(8,128)S(1)} %copy-done.4, f32[4,8,24,1024]{3,2,1,0:T(8,128)S(1)} %get-tuple-element.30.later_ref), custom_call_target="tpu_custom_call" | custom-call | bytes 6291456 | tf_op jit(solution)/shard_map/pallas_call | solution.py:528
  96.4 1.0 %all-to-all-done.1 = f32[8,64,128]{2,1,0:T(8,128)S(1)} async-done(((f32[8,64,128]{2,1,0:T(8,128)}), f32[8,64,128]{2,1,0:T(8,128)S(1)}, u32[]{:S(2)}, u32[]{:S(2)}) %all-to-all-start.1) | async-done | bytes 262176 | tf_op jit(solution)/shard_map/all_to_all | solution.py:527
  (45 shorter events, 2.6 us)
Async XLA Ops:
  3.9 9.9 %copy-start.16 = (f32[4,6]{1,0:T(4,128)S(1)}, f32[4,6]{1,0:T(4,128)}, u32[]{:S(2)}) copy-start(f32[4,6]{1,0:T(4,128)} %param.14) | copy-start | bytes 292
  3.9 26.6 %all-to-all-start = ((bf16[32,144,128]{2,1,0:T(8,128)(2,1)}), bf16[32,144,128]{2,1,0:T(8,128)(2,1)S(1)}, u32[]{:S(2)}, u32[]{:S(2)}) async-start(bf16[32,144,128]{2,1,0:T(8,128)(2,1)} %shard_map.113.after_ref), calls=%async_computation | async-start | bytes 2359296 | tf_op jit(solution)/shard_map/all_to_all | solution.py:444
  14.4 50.3 %copy-start.12 = (f32[4,6]{1,0:T(4,128)S(1)}, f32[4,6]{1,0:T(4,128)}, u32[]{:S(2)}) copy-start(f32[4,6]{1,0:T(4,128)} %negate_exponential_fusion.decay_ref) | copy-start | bytes 292
  14.4 50.3 %copy-start.13 = (f32[4,6]{1,0:T(4,128)S(1)}, f32[4,6]{1,0:T(4,128)}, u32[]{:S(2)}) copy-start(f32[4,6]{1,0:T(4,128)} %profile_ref.3) | copy-start | bytes 292
  14.4 50.3 %copy-start.14 = (f32[6]{0:T(128)S(1)}, f32[6]{0:T(128)}, u32[]{:S(2)}) copy-start(f32[6]{0:T(128)} %gain_ref.5) | copy-start | bytes 76
  14.4 50.3 %copy-start.15 = (s32[2]{0:T(128)S(1)}, s32[2]{0:T(128)}, u32[]{:S(2)}) copy-start(s32[2]{0:T(128)} %add_convert_fusion.where_ref) | copy-start | bytes 28
  17.5 47.3 %copy-start = (f32[4,6,16,1024]{3,2,1,0:T(8,128)S(1)}, f32[4,6,16,1024]{3,2,1,0:T(8,128)}, u32[]{:S(2)}) copy-start(f32[4,6,16,1024]{3,2,1,0:T(8,128)} %lam_ref.3) | copy-start | bytes 4718596
  17.5 28.2 %collective-permute-start = (bf16[14,16,1024]{2,1,0:T(8,128)(2,1)}, bf16[14,16,1024]{2,1,0:T(8,128)(2,1)S(1)}, u32[]{:S(2)}, u32[]{:S(2)}) collective-permute-start(bf16[14,16,1024]{2,1,0:T(8,128)(2,1)} %get-tuple-element.17), channel_id=1, source_target_pairs={{0,64},{64,128},{128,192},{192,256},{256,320},{320,384},{384,448},... | collective-permute-start | bytes 1376264 | tf_op jit(solution)/shard_map/ppermute | solution.py:459
  19.7 26.0 %collective-permute-start.1 = (bf16[13,16,1024]{2,1,0:T(8,128)(2,1)}, bf16[13,16,1024]{2,1,0:T(8,128)(2,1)}, u32[]{:S(2)}, u32[]{:S(2)}) collective-permute-start(bf16[13,16,1024]{2,1,0:T(8,128)(2,1)} %get-tuple-element.18), channel_id=1, source_target_pairs={{64,0},{128,64},{192,128},{256,192},{320,256},{384,320},{448,384},... | collective-permute-start | bytes 1277960 | tf_op jit(solution)/shard_map/ppermute | solution.py:460
  30.5 34.2 %copy-start.5 = (f32[6,16,1024]{2,1,0:T(8,128)S(1)}, f32[6,16,1024]{2,1,0:T(8,128)}, u32[]{:S(2)}) copy-start(f32[6,16,1024]{2,1,0:T(8,128)} %kz_ref.3) | copy-start | bytes 1179652
  30.5 34.2 %copy-start.6 = (f32[6,16,1024]{2,1,0:T(8,128)S(1)}, f32[6,16,1024]{2,1,0:T(8,128)}, u32[]{:S(2)}) copy-start(f32[6,16,1024]{2,1,0:T(8,128)} %cx_ref.3) | copy-start | bytes 1179652
  30.5 34.2 %copy-start.7 = (f32[6,16,1024]{2,1,0:T(8,128)S(1)}, f32[6,16,1024]{2,1,0:T(8,128)}, u32[]{:S(2)}) copy-start(f32[6,16,1024]{2,1,0:T(8,128)} %cy_ref.3) | copy-start | bytes 1179652
  31.3 25.4 %collective-permute-start.5 = (f32[128,128]{1,0:T(8,128)S(1)}, f32[128,128]{1,0:T(8,128)S(1)}, u32[]{:S(2)}, u32[]{:S(2)}) collective-permute-start(f32[128,128]{1,0:T(8,128)S(1)} %get-tuple-element.32), channel_id=1, source_target_pairs={{0,32},{4,36},{8,40},{12,44},{16,48},{20,52},{24,56},{28,60},{32,0... | collective-permute-start | bytes 196616 | tf_op jit(solution)/shard_map/ppermute | solution.py:509
  45.0 11.7 %collective-permute-start.4 = (f32[128,128]{1,0:T(8,128)S(1)}, f32[128,128]{1,0:T(8,128)S(1)}, u32[]{:S(2)}, u32[]{:S(2)}) collective-permute-start(f32[128,128]{1,0:T(8,128)S(1)} %get-tuple-element.33), channel_id=1, source_target_pairs={{0,0},{4,4},{8,8},{12,12},{16,16},{20,20},{24,24},{28,28},{32,32},... | collective-permute-start | bytes 196616 | tf_op jit(solution)/shard_map/ppermute | solution.py:509
  48.7 16.0 %collective-permute-start.2 = (bf16[144,1024]{1,0:T(8,128)(2,1)S(1)}, bf16[144,1024]{1,0:T(8,128)(2,1)S(1)}, u32[]{:S(2)}, u32[]{:S(2)}) collective-permute-start(bf16[144,1024]{1,0:T(8,128)(2,1)S(1)} %get-tuple-element.21), channel_id=1, source_target_pairs={{1,0},{2,1},{3,2},{4,3},{5,4},{6,5},{7,6},{8,7},{9,8},{10,9},{11,1... | collective-permute-start | bytes 884744 | tf_op jit(solution)/shard_map/ppermute | solution.py:468
  51.4 13.3 %collective-permute-start.3 = (bf16[144,1024]{1,0:T(8,128)(2,1)S(1)}, bf16[144,1024]{1,0:T(8,128)(2,1)S(1)}, u32[]{:S(2)}, u32[]{:S(2)}) collective-permute-start(bf16[144,1024]{1,0:T(8,128)(2,1)S(1)} %get-tuple-element.22), channel_id=1, source_target_pairs={{0,1},{1,2},{2,3},{3,4},{4,5},{5,6},{6,7},{7,8},{8,9},{9,10},{10,1... | collective-permute-start | bytes 884744 | tf_op jit(solution)/shard_map/ppermute | solution.py:469
  56.7 12.0 %collective-permute-start.6 = (f32[16,128]{1,0:T(8,128)S(1)}, f32[16,128]{1,0:T(8,128)S(1)}, u32[]{:S(2)}, u32[]{:S(2)}) collective-permute-start(f32[16,128]{1,0:T(8,128)S(1)} %get-tuple-element.34), channel_id=1, source_target_pairs={{1,0},{2,1},{3,2},{4,3},{5,4},{6,5},{7,6},{8,7},{9,8},{10,9},{11,1... | collective-permute-start | bytes 24584 | tf_op jit(solution)/shard_map/ppermute | solution.py:513
  58.7 10.1 %collective-permute-start.7 = (f32[16,128]{1,0:T(8,128)S(1)}, f32[16,128]{1,0:T(8,128)S(1)}, u32[]{:S(2)}, u32[]{:S(2)}) collective-permute-start(f32[16,128]{1,0:T(8,128)S(1)} %get-tuple-element.35), channel_id=1, source_target_pairs={{0,1},{1,2},{2,3},{3,4},{4,5},{5,6},{6,7},{7,8},{8,9},{9,10},{10,1... | collective-permute-start | bytes 24584 | tf_op jit(solution)/shard_map/ppermute | solution.py:514
  68.7 17.8 %copy-start.1 = (f32[8,24,1024]{2,1,0:T(8,128)}, f32[8,24,1024]{2,1,0:T(8,128)S(1)}, u32[]{:S(2)}) copy-start(f32[8,24,1024]{2,1,0:T(8,128)S(1)} %get-tuple-element.24.cxs) | copy-start | bytes 2359300
  68.7 17.8 %copy-start.3 = (f32[8,24,1024]{2,1,0:T(8,128)}, f32[8,24,1024]{2,1,0:T(8,128)S(1)}, u32[]{:S(2)}) copy-start(f32[8,24,1024]{2,1,0:T(8,128)S(1)} %get-tuple-element.25.cys) | copy-start | bytes 2359300
  68.7 17.8 %copy-start.8 = (f32[9,24,1024]{2,1,0:T(8,128)}, f32[9,24,1024]{2,1,0:T(8,128)S(1)}, u32[]{:S(2)}) copy-start(f32[9,24,1024]{2,1,0:T(8,128)S(1)} %get-tuple-element.23.kzs) | copy-start | bytes 2654212
  86.5 10.9 %all-to-all-start.1 = ((f32[8,64,128]{2,1,0:T(8,128)}), f32[8,64,128]{2,1,0:T(8,128)S(1)}, u32[]{:S(2)}, u32[]{:S(2)}) async-start(f32[8,64,128]{2,1,0:T(8,128)} %get-tuple-element.31), calls=%async_computation.1 | async-start | bytes 524288 | tf_op jit(solution)/shard_map/all_to_all | solution.py:527
  90.0 1.1 %copy-start.2 = (f32[8,24,1024]{2,1,0:T(8,128)S(1)}, f32[8,24,1024]{2,1,0:T(8,128)}, u32[]{:S(2)}) copy-start(f32[8,24,1024]{2,1,0:T(8,128)} %copy-done.1) | copy-start | bytes 2359300
  92.2 1.2 %copy-start.9 = (f32[9,24,1024]{2,1,0:T(8,128)S(1)}, f32[9,24,1024]{2,1,0:T(8,128)}, u32[]{:S(2)}) copy-start(f32[9,24,1024]{2,1,0:T(8,128)} %copy-done.8) | copy-start | bytes 2654212
  (3 other events, 3.0 us)
